TPU v7x, 32 devices: a whole 2x2x4 slice. The times are simulated.
32 devices in a mesh: section: 4 (over y, x), dp: 8 (over z, core).
Axes of the slice: x: 2, y: 2, z: 4, core: 2. Of those that a mesh axis runs over, the one named last changes fastest.
Arguments:
- tokens: bfloat16 [2, 4096, 1024], P(None, 'dp'), may hold values from -6 to 6
- lengths: int32 [2, 8, 16], P(None, 'dp'), may hold values from 1 to 256, 512 in all within a row
- gain_attn: bfloat16 [4, 1024], P('section'), may hold values from 0.099609375 to 1.8984375
- w_query: bfloat16 [4, 1024, 1024], P('section'), may hold values from -0.1875 to 0.1875
- w_key: bfloat16 [4, 1024, 128], P('section'), may hold values from -0.1875 to 0.1875
- w_value: bfloat16 [4, 1024, 128], P('section'), may hold values from -0.1875 to 0.1875
- w_out: bfloat16 [4, 1024, 1024], P('section'), may hold values from -0.5 to 0.5
- gain_ffn: bfloat16 [4, 1024], P('section'), may hold values from 0.099609375 to 1.8984375
- w_up: bfloat16 [4, 1024, 4096], P('section'), may hold values from -0.1875 to 0.1875
- w_down: bfloat16 [4, 4096, 1024], P('section'), may hold values from -0.09375 to 0.09375
- cotangent: bfloat16 [2, 4096, 1024], P(None, 'dp'), may hold values from -6 to 6
Outputs:
- layer_outputs: bfloat16 [4, 2, 4096, 1024], P('section', None, 'dp')
- input_grads: bfloat16 [4, 2, 4096, 1024], P('section', None, 'dp')
- grad_gain_attn: float32 [4, 1024], P('section', 'dp')
- grad_query: float32 [4, 1024, 1024], P('section', 'dp')
- grad_key: float32 [4, 1024, 128], P('section', 'dp')
- grad_value: float32 [4, 1024, 128], P('section', 'dp')
- grad_out: float32 [4, 1024, 1024], P('section', 'dp')
- grad_gain_ffn: float32 [4, 1024], P('section', 'dp')
- grad_up: float32 [4, 1024, 4096], P('section', 'dp')
- grad_down: float32 [4, 4096, 1024], P('section', 'dp')
Inputs may be any that keep to these rules, and one draw needn't show every extreme that they name: The 16 lengths of a row sum to 512; the last counts the padding positions at the row's end.
All inputs are finite; a program needn't handle non-finite values.
Results may differ from a plain program's by a relative error of at most 0.029.
Values may be sent and summed in bfloat16 or wider, within the bound.
No kernel may reach another device: no remote copies, remote signals or barrier semaphores. Data moves between devices by JAX's collectives and lax.ppermute only.
A program may use at most 384 MiB of HBM per device.

v0:
```python
import jax
import jax.numpy as jnp
from jax import lax
from jax.sharding import PartitionSpec as P

NORM_EPS = 1e-06
NEG_BIG = -1e30


def from_behind(block, axis, distance):
    devices = range(lax.axis_size(axis))
    route = [(i - distance, i) for i in devices if i - distance in devices]
    return lax.ppermute(block, axis, route)


def for_sending(shard):

    def short(part):
        return part.astype(jnp.bfloat16) if part.dtype == jnp.float32 else part

    return jax.tree.map(short, shard)


def rms_norm(tensor, gain):
    return tensor * lax.rsqrt(jnp.mean(tensor * tensor, axis=-1, keepdims=True) + NORM_EPS) * gain


def gelu_exact(tensor):
    return jax.nn.gelu(tensor, approximate=False)


def contract_rows(left, right):
    return lax.dot_general(
        left, right, (((0,), (0,)), ((), ())), preferred_element_type=jnp.float32
    )


def contract_cols(left, right):
    return lax.dot_general(
        left, right, (((1,), (1,)), ((), ())), preferred_element_type=jnp.float32
    )


def row_mask(lengths_row, row_count):
    seq_ends = jnp.cumsum(lengths_row, dtype=jnp.int32)
    position = lax.iota(jnp.int32, row_count)
    segment = jnp.sum((position[:, None] >= seq_ends[None, :]).astype(jnp.int32), axis=1)
    pad_seq = lengths_row.shape[0] - 1
    same_seq = segment[:, None] == segment[None, :]
    causal = position[None, :] <= position[:, None]
    own_pos = position[None, :] == position[:, None]
    return same_seq & causal & ((segment[:, None] < pad_seq) | own_pos)


def forward_parts(source, allowed, weights):
    gain_attn, w_query, w_key, w_value, w_out, gain_ffn, w_up, w_down = weights
    row_count = source.shape[0]
    head_size = w_key.shape[1]
    head_count = w_query.shape[1] // head_size
    normed_attn = rms_norm(source, gain_attn.astype(jnp.float32)).astype(jnp.bfloat16)
    queries = jnp.dot(normed_attn, w_query, preferred_element_type=jnp.float32).astype(jnp.bfloat16)
    key_rows = jnp.dot(normed_attn, w_key, preferred_element_type=jnp.float32).astype(jnp.bfloat16)
    value_rows = jnp.dot(normed_attn, w_value, preferred_element_type=jnp.float32).astype(
        jnp.bfloat16
    )
    query_heads = queries.reshape(row_count, head_count, head_size)
    scores = jnp.einsum(
        "qhe,ke->hqk", query_heads, key_rows, preferred_element_type=jnp.float32
    ) * head_size ** (-0.5)
    attn_probs = jax.nn.softmax(jnp.where(allowed[None], scores, NEG_BIG), axis=-1)
    probs_low = attn_probs.astype(jnp.bfloat16)
    mixed_heads = jnp.einsum(
        "hqk,ke->qhe", probs_low, value_rows, preferred_element_type=jnp.float32
    )
    mixed_heads = mixed_heads.reshape(row_count, head_count * head_size).astype(jnp.bfloat16)
    middle = source + jnp.dot(mixed_heads, w_out, preferred_element_type=jnp.float32)
    normed_ffn = rms_norm(middle, gain_ffn.astype(jnp.float32)).astype(jnp.bfloat16)
    pre_act = jnp.dot(normed_ffn, w_up, preferred_element_type=jnp.float32)
    activated = gelu_exact(pre_act).astype(jnp.bfloat16)
    result = middle + jnp.dot(activated, w_down, preferred_element_type=jnp.float32)
    return (
        normed_attn,
        query_heads,
        key_rows,
        value_rows,
        attn_probs,
        probs_low,
        mixed_heads,
        middle,
        normed_ffn,
        pre_act,
        activated,
        result,
    )


def ffn_backward(source, allowed, weights, grad_result):
    gain_attn, w_query, w_key, w_value, w_out, gain_ffn, w_up, w_down = weights
    parts = forward_parts(source, allowed, weights)
    middle, normed_ffn, pre_act, activated = (parts[7], parts[8], parts[9], parts[10])
    grad_branch = grad_result.astype(jnp.bfloat16)
    grad_down = contract_rows(activated, grad_branch)
    grad_act = contract_cols(grad_branch, w_down)
    unused_act, gelu_back = jax.vjp(gelu_exact, pre_act)
    grad_pre = gelu_back(grad_act)[0].astype(jnp.bfloat16)
    grad_up = contract_rows(normed_ffn, grad_pre)
    grad_normed_ffn = contract_cols(grad_pre, w_up)
    unused_ffn, norm_back_ffn = jax.vjp(rms_norm, middle, gain_ffn.astype(jnp.float32))
    grad_mid_norm, grad_gain_ffn = norm_back_ffn(grad_normed_ffn)
    grad_middle = grad_result + grad_mid_norm
    return (parts, grad_middle, (grad_gain_ffn, grad_up, grad_down))


def attn_backward(source, weights, parts, grad_middle):
    gain_attn, w_query, w_key, w_value, w_out, gain_ffn, w_up, w_down = weights
    normed_attn, query_heads, key_rows, value_rows, attn_probs, probs_low, mixed_heads = parts[:7]
    row_count, head_count, head_size = query_heads.shape
    grad_attn = grad_middle.astype(jnp.bfloat16)
    grad_out = contract_rows(mixed_heads, grad_attn)
    grad_mixed = (
        contract_cols(grad_attn, w_out)
        .astype(jnp.bfloat16)
        .reshape(row_count, head_count, head_size)
    )
    grad_probs = jnp.einsum(
        "qhe,ke->hqk", grad_mixed, value_rows, preferred_element_type=jnp.float32
    )
    grad_values = jnp.einsum(
        "hqk,qhe->ke", probs_low, grad_mixed, preferred_element_type=jnp.float32
    ).astype(jnp.bfloat16)
    grad_scores = attn_probs * (
        grad_probs - jnp.sum(attn_probs * grad_probs, axis=-1, keepdims=True)
    )
    grad_scores = grad_scores.astype(jnp.bfloat16)
    score_scale = head_size ** (-0.5)
    grad_queries = (
        jnp.einsum("hqk,ke->qhe", grad_scores, key_rows, preferred_element_type=jnp.float32)
        * score_scale
    )
    grad_queries = grad_queries.reshape(row_count, head_count * head_size).astype(jnp.bfloat16)
    grad_keys = (
        jnp.einsum("hqk,qhe->ke", grad_scores, query_heads, preferred_element_type=jnp.float32)
        * score_scale
    ).astype(jnp.bfloat16)
    grad_query = contract_rows(normed_attn, grad_queries)
    grad_key = contract_rows(normed_attn, grad_keys)
    grad_value = contract_rows(normed_attn, grad_values)
    grad_normed_attn = (
        contract_cols(grad_queries, w_query)
        + contract_cols(grad_keys, w_key)
        + contract_cols(grad_values, w_value)
    )
    unused_attn, norm_back_attn = jax.vjp(rms_norm, source, gain_attn.astype(jnp.float32))
    grad_src_norm, grad_gain_attn = norm_back_attn(grad_normed_attn)
    grad_source = grad_middle + grad_src_norm
    return (grad_source, (grad_gain_attn, grad_query, grad_key, grad_value, grad_out))


def layer_backward(source, allowed, weights, grad_result):
    parts, grad_middle, ffn_grads = ffn_backward(source, allowed, weights, grad_result)
    grad_source, attn_grads = attn_backward(source, weights, parts, grad_middle)
    return (grad_source, attn_grads + ffn_grads)


def body(
    tokens, lengths, gain_attn, w_query, w_key, w_value, w_out, gain_ffn, w_up, w_down, cotangent
):
    weights = (
        gain_attn[0],
        w_query[0],
        w_key[0],
        w_value[0],
        w_out[0],
        gain_ffn[0],
        w_up[0],
        w_down[0],
    )
    micro_count, row_count, model_width = tokens.shape
    sections = lax.axis_size("section")
    section_pos = lax.axis_index("section")
    tick_count = micro_count + sections - 1
    kept_shape = (micro_count, 1, 1)

    def slot_of(micro_pos):
        active = (micro_pos >= 0) & (micro_pos < micro_count)
        return (active, jnp.clip(micro_pos, 0, micro_count - 1))

    def take_slot(buffer, mb_slot):
        return lax.dynamic_index_in_dim(buffer, mb_slot, 0, keepdims=False)

    def write_slot(buffer, mb_slot, active, update):
        return lax.dynamic_update_index_in_dim(
            buffer, jnp.where(active, update, take_slot(buffer, mb_slot)), mb_slot, 0
        )

    def forward_tick(tick_num, loop_state):
        incoming, stored, layer_outs, kept = loop_state
        active, mb_slot = slot_of(tick_num - section_pos)
        source = jnp.where(section_pos == 0, take_slot(tokens, mb_slot), incoming)
        allowed = row_mask(take_slot(lengths, mb_slot)[0], row_count)

        def forward_compute():
            parts = forward_parts(source.astype(jnp.float32), allowed, weights)
            pre_keep = jnp.zeros(kept_shape[1:], jnp.float32)
            return (parts[11].astype(jnp.bfloat16), pre_keep)

        def forward_bypass():
            return (
                jnp.zeros((row_count, model_width), jnp.bfloat16),
                jnp.zeros(kept_shape[1:], jnp.float32),
            )

        result, pre_keep = lax.cond(active, forward_compute, forward_bypass)
        stored = write_slot(stored, mb_slot, active, source)
        layer_outs = write_slot(layer_outs, mb_slot, active, result)
        outgoing = from_behind(result, "section", 1)
        return (outgoing, stored, layer_outs, kept)

    forward_init = (
        jnp.zeros((row_count, model_width), jnp.bfloat16),
        jnp.zeros_like(tokens),
        jnp.zeros_like(tokens),
        jnp.zeros(kept_shape, jnp.float32),
    )
    unused_in, stored, layer_outs, kept = lax.fori_loop(0, tick_count, forward_tick, forward_init)
    grad_init = tuple((jnp.zeros(weight.shape, jnp.float32) for weight in weights))

    def backward_inputs(tick_num, incoming):
        active, mb_slot = slot_of(tick_num - (sections - 1 - section_pos))
        grad_result = jnp.where(
            section_pos == sections - 1, take_slot(cotangent, mb_slot), incoming
        )
        source = take_slot(stored, mb_slot).astype(jnp.float32)
        allowed = row_mask(take_slot(lengths, mb_slot)[0], row_count)
        kept_row = None
        return (active, mb_slot, grad_result, source, allowed, kept_row)

    def backward_tick(tick_num, loop_state):
        incoming, grad_totals, input_grads = loop_state
        active, mb_slot, grad_result, source, allowed, kept_row = backward_inputs(
            tick_num, incoming
        )

        def backward_compute():
            grad_source, tick_grads = layer_backward(
                source, allowed, weights, grad_result.astype(jnp.float32)
            )
            return (grad_source.astype(jnp.bfloat16), tick_grads)

        def backward_bypass():
            return (
                jnp.zeros((row_count, model_width), jnp.bfloat16),
                tuple((jnp.zeros(weight.shape, jnp.float32) for weight in weights)),
            )

        grad_source, tick_grads = lax.cond(active, backward_compute, backward_bypass)
        grad_totals = tuple(
            (running + portion for running, portion in zip(grad_totals, tick_grads))
        )
        input_grads = write_slot(input_grads, mb_slot, active, grad_source)
        outgoing = from_behind(grad_source, "section", -1)
        return (outgoing, grad_totals, input_grads)

    backward_init = (
        jnp.zeros((row_count, model_width), jnp.bfloat16),
        grad_init,
        jnp.zeros_like(tokens),
    )
    incoming, grad_totals, input_grads = lax.fori_loop(
        0, tick_count - 1, backward_tick, backward_init
    )
    active, mb_slot, grad_result, source, allowed, kept_row = backward_inputs(
        tick_count - 1, incoming
    )
    parts, grad_middle, ffn_grads = ffn_backward(
        source, allowed, weights, grad_result.astype(jnp.float32)
    )
    ffn_totals = tuple(
        (
            running + jnp.where(active, portion, 0.0)
            for running, portion in zip(grad_totals[5:], ffn_grads)
        )
    )
    grad_source, attn_grads = attn_backward(source, weights, parts, grad_middle)
    attn_totals = tuple(
        (
            running + jnp.where(active, portion, 0.0)
            for running, portion in zip(grad_totals[:5], attn_grads)
        )
    )
    grad_shares = jax.tree.map(
        lambda part: part.astype(jnp.float32),
        lax.psum_scatter(
            for_sending(attn_totals + ffn_totals), "dp", scatter_dimension=0, tiled=True
        ),
    )
    input_grads = write_slot(input_grads, mb_slot, active, grad_source.astype(jnp.bfloat16))
    return (layer_outs[None], input_grads[None]) + tuple((portion[None] for portion in grad_shares))


def solution(mesh):
    return jax.shard_map(
        body,
        mesh=mesh,
        in_specs=(
            P(None, "dp", None),
            P(None, "dp", None),
            P("section", None),
            P("section", None, None),
            P("section", None, None),
            P("section", None, None),
            P("section", None, None),
            P("section", None),
            P("section", None, None),
            P("section", None, None),
            P(None, "dp", None),
        ),
        out_specs=(
            P("section", None, "dp", None),
            P("section", None, "dp", None),
            P("section", "dp"),
            P("section", "dp", None),
            P("section", "dp", None),
            P("section", "dp", None),
            P("section", "dp", None),
            P("section", "dp"),
            P("section", "dp", None),
            P("section", "dp", None),
        ),
        check_vma=False,
    )
```

profile of v0, /device:TPU:0, one launch (start us, length us, event | category | flops | bytes accessed | tf_op | source)
XLA Modules:
  0.0 1628.8 jit_solution(2040057287352599943)
XLA Ops:
  12.3 435.9 %while.52 = (s32[]{:T(128)}, bf16[512,1024]{1,0:T(8,128)(2,1)}, bf16[2,512,1024]{2,1,0:T(8,128)(2,1)S(1)}, bf16[2,512,1024]{2,1,0:T(8,128)(2,1)}, s32[]{:T(128)}...) while((s32[]{:T(128)}, bf16[512,1024]{1,0:T(8,128)(2,1)}, ...), condition=%wide.region_9.10_spmd, body=%wide.region_0.9_spmd.sunk | while | flops 12249624576 | bytes 95576104 | solution.py:225
  18.9 67.3 %conditional.5 = (bf16[512,1024]{1,0:T(8,128)(2,1)S(1)}) conditional(s32[]{:T(128)} %convert_element_type.686, () %tuple.131, (bf16[512,1024]{1,0:T(8,128)(2,1)S(1)}, bf16[1024]{0:T(1024)(128)(2,1)S(1)}, bf16[1024,128]{1,0:T(8,128)(2,1)}, s32[512,16]{0,1:T(8,128)S(1)}, s32[512,512]{0,1:T(8,128)}, /*index=5*/s32[512,512]{0,1:T(8,128)}, ...), branch_computations={%region_2.2_spmd, %region_3.8_spmd} | conditional | flops 12248035328 | bytes 75619368 | solution.py:213
  55.3 30.8 %add_convert_fusion = bf16[512,1024]{1,0:T(8,128)(2,1)S(1)} fusion(f32[512,1024]{1,0:T(8,128)} %get-tuple-element.1368, bf16[4096,1024]{1,0:T(8,128)(2,1)} %get-tuple-element.1083, bf16[1024,4096]{1,0:T(8,128)(2,1)} %get-tuple-element.1082, f32[1024]{0:T(1024)S(1)} %convert_element_type.317, f32[512]{0:T(512)S(1)} %add_rsqrt_fusion), kind=kOutput, calls=%fused_computation.35 | convolution fusion | flops 8728870912 | bytes 19929088 | tf_op jit(solution)/shard_map/while/body/eval_jaxpr/cond/branch_1_fun/dot_general | solution.py:80
  91.1 19.6 %collective-permute-done = bf16[512,1024]{1,0:T(8,128)(2,1)} collective-permute-done((bf16[512,1024]{1,0:T(8,128)(2,1)S(1)}, bf16[512,1024]{1,0:T(8,128)(2,1)}, u32[]{:S(2)}, u32[]{:S(2)}) %collective-permute-start) | collective-permute-done | bytes 1048608 | tf_op jit(solution)/shard_map/while/body/eval_jaxpr/ppermute | solution.py:13
  117.4 67.2 %conditional.5 = (bf16[512,1024]{1,0:T(8,128)(2,1)S(1)}) conditional(s32[]{:T(128)} %convert_element_type.686, () %tuple.131, (bf16[512,1024]{1,0:T(8,128)(2,1)S(1)}, bf16[1024]{0:T(1024)(128)(2,1)S(1)}, bf16[1024,128]{1,0:T(8,128)(2,1)}, s32[512,16]{0,1:T(8,128)S(1)}, s32[512,512]{0,1:T(8,128)}, /*index=5*/s32[512,512]{0,1:T(8,128)}, ...), branch_computations={%region_2.2_spmd, %region_3.8_spmd} | conditional | flops 12248035328 | bytes 75619368 | solution.py:213
  153.8 30.8 %add_convert_fusion = bf16[512,1024]{1,0:T(8,128)(2,1)S(1)} fusion(f32[512,1024]{1,0:T(8,128)} %get-tuple-element.1368, bf16[4096,1024]{1,0:T(8,128)(2,1)} %get-tuple-element.1083, bf16[1024,4096]{1,0:T(8,128)(2,1)} %get-tuple-element.1082, f32[1024]{0:T(1024)S(1)} %convert_element_type.317, f32[512]{0:T(512)S(1)} %add_rsqrt_fusion), kind=kOutput, calls=%fused_computation.35 | convolution fusion | flops 8728870912 | bytes 19929088 | tf_op jit(solution)/shard_map/while/body/eval_jaxpr/cond/branch_1_fun/dot_general | solution.py:80
  193.1 18.7 %collective-permute-done = bf16[512,1024]{1,0:T(8,128)(2,1)} collective-permute-done((bf16[512,1024]{1,0:T(8,128)(2,1)S(1)}, bf16[512,1024]{1,0:T(8,128)(2,1)}, u32[]{:S(2)}, u32[]{:S(2)}) %collective-permute-start) | collective-permute-done | bytes 1048608 | tf_op jit(solution)/shard_map/while/body/eval_jaxpr/ppermute | solution.py:13
  218.7 72.9 %collective-permute-start = (bf16[512,1024]{1,0:T(8,128)(2,1)S(1)}, bf16[512,1024]{1,0:T(8,128)(2,1)}, u32[]{:S(2)}, u32[]{:S(2)}) collective-permute-start(bf16[512,1024]{1,0:T(8,128)(2,1)S(1)} %get-tuple-element.1825), channel_id=1, source_target_pairs={{0,8},{8,16},{16,24},{1,9},{9,17},{17,25},{2,10},{10,18},{18,26},{... | collective-permute-start | bytes 3145736 | tf_op jit(solution)/shard_map/while/body/eval_jaxpr/ppermute | solution.py:13
  294.2 17.9 %collective-permute-done = bf16[512,1024]{1,0:T(8,128)(2,1)} collective-permute-done((bf16[512,1024]{1,0:T(8,128)(2,1)S(1)}, bf16[512,1024]{1,0:T(8,128)(2,1)}, u32[]{:S(2)}, u32[]{:S(2)}) %collective-permute-start) | collective-permute-done | bytes 1048608 | tf_op jit(solution)/shard_map/while/body/eval_jaxpr/ppermute | solution.py:13
  327.3 16.9 %collective-permute-done = bf16[512,1024]{1,0:T(8,128)(2,1)} collective-permute-done((bf16[512,1024]{1,0:T(8,128)(2,1)S(1)}, bf16[512,1024]{1,0:T(8,128)(2,1)}, u32[]{:S(2)}, u32[]{:S(2)}) %collective-permute-start) | collective-permute-done | bytes 1048608 | tf_op jit(solution)/shard_map/while/body/eval_jaxpr/ppermute | solution.py:13
  351.1 73.0 %collective-permute-start = (bf16[512,1024]{1,0:T(8,128)(2,1)S(1)}, bf16[512,1024]{1,0:T(8,128)(2,1)}, u32[]{:S(2)}, u32[]{:S(2)}) collective-permute-start(bf16[512,1024]{1,0:T(8,128)(2,1)S(1)} %get-tuple-element.1825), channel_id=1, source_target_pairs={{0,8},{8,16},{16,24},{1,9},{9,17},{17,25},{2,10},{10,18},{18,26},{... | collective-permute-start | bytes 3145736 | tf_op jit(solution)/shard_map/while/body/eval_jaxpr/ppermute | solution.py:13
  426.8 16.3 %collective-permute-done = bf16[512,1024]{1,0:T(8,128)(2,1)} collective-permute-done((bf16[512,1024]{1,0:T(8,128)(2,1)S(1)}, bf16[512,1024]{1,0:T(8,128)(2,1)}, u32[]{:S(2)}, u32[]{:S(2)}) %collective-permute-start) | collective-permute-done | bytes 1048608 | tf_op jit(solution)/shard_map/while/body/eval_jaxpr/ppermute | solution.py:13
  474.0 731.6 %while.53 = (s32[]{:T(128)}, bf16[512,1024]{1,0:T(8,128)(2,1)}, f32[1024]{0:T(1024)}, f32[1024,1024]{1,0:T(8,128)}, f32[1024,128]{1,0:T(8,128)}, /*index=5*/f32[...) while((s32[]{:T(128)}, bf16[512,1024]{1,0:T(8,128)(2,1)}, ...), condition=%wide.region_24.25_spmd.clone, body=%wide.region_10.24_spmd.clone.sunk | while | flops 32200028160 | bytes 612317312 | solution.py:269
  475.7 29.2 %conditional.6 = (bf16[512,1024]{1,0:T(8,128)(2,1)}, f32[1024]{0:T(1024)}, f32[1024,1024]{1,0:T(8,128)}, f32[1024,128]{1,0:T(8,128)}, f32[1024,128]{1,0:T(8,128)...) conditional(s32[]{:T(128)} %convert_element_type.688, ...), branch_computations={%region_12.12_spmd, %region_13.23_spmd} | conditional | flops 32177987584 | bytes 429739744 | solution.py:256
  549.3 24.7 %conditional.6 = (bf16[512,1024]{1,0:T(8,128)(2,1)}, f32[1024]{0:T(1024)}, f32[1024,1024]{1,0:T(8,128)}, f32[1024,128]{1,0:T(8,128)}, f32[1024,128]{1,0:T(8,128)...) conditional(s32[]{:T(128)} %convert_element_type.688, ...), branch_computations={%region_12.12_spmd, %region_13.23_spmd} | conditional | flops 32177987584 | bytes 429739744 | solution.py:256
  578.0 17.7 %select_add_fusion.16 = f32[1024,4096]{1,0:T(8,128)} fusion(f32[1024,4096]{1,0:T(8,128)} %get-tuple-element.1667, f32[1024,4096]{1,0:T(8,128)} %get-tuple-element.1779, pred[]{:T(512)S(6)} %compare.3), kind=kLoop, calls=%fused_computation.210.clone.1 | loop fusion | flops 8388608 | bytes 50331648 | tf_op jit(solution)/shard_map/while/body/eval_jaxpr/add | solution.py:258
  595.7 18.5 %select_add_fusion.17 = f32[4096,1024]{1,0:T(8,128)} fusion(f32[4096,1024]{1,0:T(8,128)} %get-tuple-element.1668, f32[4096,1024]{1,0:T(8,128)} %get-tuple-element.1780, pred[]{:T(512)S(6)} %compare.3), kind=kLoop, calls=%fused_computation.209.clone.1 | loop fusion | flops 8388608 | bytes 50331648 | tf_op jit(solution)/shard_map/while/body/eval_jaxpr/add | solution.py:258
  626.3 19.1 %collective-permute-done.1 = bf16[512,1024]{1,0:T(8,128)(2,1)} collective-permute-done((bf16[512,1024]{1,0:T(8,128)(2,1)}, bf16[512,1024]{1,0:T(8,128)(2,1)}, u32[]{:S(2)}, u32[]{:S(2)}) %collective-permute-start.1) | collective-permute-done | bytes 1048608 | tf_op jit(solution)/shard_map/while/body/eval_jaxpr/ppermute | solution.py:13
  646.8 24.7 %conditional.6 = (bf16[512,1024]{1,0:T(8,128)(2,1)}, f32[1024]{0:T(1024)}, f32[1024,1024]{1,0:T(8,128)}, f32[1024,128]{1,0:T(8,128)}, f32[1024,128]{1,0:T(8,128)...) conditional(s32[]{:T(128)} %convert_element_type.688, ...), branch_computations={%region_12.12_spmd, %region_13.23_spmd} | conditional | flops 32177987584 | bytes 429739744 | solution.py:256
  675.5 17.7 %select_add_fusion.16 = f32[1024,4096]{1,0:T(8,128)} fusion(f32[1024,4096]{1,0:T(8,128)} %get-tuple-element.1667, f32[1024,4096]{1,0:T(8,128)} %get-tuple-element.1779, pred[]{:T(512)S(6)} %compare.3), kind=kLoop, calls=%fused_computation.210.clone.1 | loop fusion | flops 8388608 | bytes 50331648 | tf_op jit(solution)/shard_map/while/body/eval_jaxpr/add | solution.py:258
  693.3 18.5 %select_add_fusion.17 = f32[4096,1024]{1,0:T(8,128)} fusion(f32[4096,1024]{1,0:T(8,128)} %get-tuple-element.1668, f32[4096,1024]{1,0:T(8,128)} %get-tuple-element.1780, pred[]{:T(512)S(6)} %compare.3), kind=kLoop, calls=%fused_computation.209.clone.1 | loop fusion | flops 8388608 | bytes 50331648 | tf_op jit(solution)/shard_map/while/body/eval_jaxpr/add | solution.py:258
  723.8 277.1 %collective-permute-done.1 = bf16[512,1024]{1,0:T(8,128)(2,1)} collective-permute-done((bf16[512,1024]{1,0:T(8,128)(2,1)}, bf16[512,1024]{1,0:T(8,128)(2,1)}, u32[]{:S(2)}, u32[]{:S(2)}) %collective-permute-start.1) | collective-permute-done | bytes 1048608 | tf_op jit(solution)/shard_map/while/body/eval_jaxpr/ppermute | solution.py:13
  1002.5 127.0 %conditional.6 = (bf16[512,1024]{1,0:T(8,128)(2,1)}, f32[1024]{0:T(1024)}, f32[1024,1024]{1,0:T(8,128)}, f32[1024,128]{1,0:T(8,128)}, f32[1024,128]{1,0:T(8,128)...) conditional(s32[]{:T(128)} %convert_element_type.688, ...), branch_computations={%region_12.12_spmd, %region_13.23_spmd} | conditional | flops 32177987584 | bytes 429739744 | solution.py:256
  1040.2 25.0 %add_convert_fusion.1 = (bf16[512,4096]{1,0:T(8,128)(2,1)}, f32[512,4096]{1,0:T(8,128)}) fusion(f32[512,4096]{1,0:T(8,128)S(1)} %fusion.147, bf16[512,1024]{1,0:T(8,128)(2,1)S(1)} %bitcast_select_fusion.8, bf16[4096,1024]{1,0:T(8,128)(2,1)S(1)} %bitcast.425), kind=kOutput, calls=%fused_computation.97 | convolution fusion | flops 4445962240 | bytes 30408704 | tf_op jit(solution)/shard_map/while/body/eval_jaxpr/cond/branch_1_fun/dot_general | solution.py:39
  1134.7 17.7 %select_add_fusion.16 = f32[1024,4096]{1,0:T(8,128)} fusion(f32[1024,4096]{1,0:T(8,128)} %get-tuple-element.1667, f32[1024,4096]{1,0:T(8,128)} %get-tuple-element.1779, pred[]{:T(512)S(6)} %compare.3), kind=kLoop, calls=%fused_computation.210.clone.1 | loop fusion | flops 8388608 | bytes 50331648 | tf_op jit(solution)/shard_map/while/body/eval_jaxpr/add | solution.py:258
  1152.5 18.5 %select_add_fusion.17 = f32[4096,1024]{1,0:T(8,128)} fusion(f32[4096,1024]{1,0:T(8,128)} %get-tuple-element.1668, f32[4096,1024]{1,0:T(8,128)} %get-tuple-element.1780, pred[]{:T(512)S(6)} %compare.3), kind=kLoop, calls=%fused_computation.209.clone.1 | loop fusion | flops 8388608 | bytes 50331648 | tf_op jit(solution)/shard_map/while/body/eval_jaxpr/add | solution.py:258
  1219.7 26.0 %add_convert_fusion.4 = bf16[512,4096]{1,0:T(8,128)(2,1)} fusion(f32[512,4096]{1,0:T(8,128)} %fusion.245, bf16[512,1024]{1,0:T(8,128)(2,1)S(1)} %bitcast_select_fusion.17, bf16[1,4096,1024]{2,1,0:T(8,128)(2,1)S(1)} %bitcast.428), kind=kOutput, calls=%fused_computation.236 | convolution fusion | flops 4445962240 | bytes 22020096 | tf_op jit(solution)/shard_map/dot_general | solution.py:39
  1309.9 26.6 %add_convert_fusion.2 = bf16[4096,1024]{1,0:T(8,128)(2,1)} fusion(f32[4096,1024]{1,0:T(8,128)} %get-tuple-element.1877, pred[]{:T(512)S(6)} %and.81, bf16[512,1024]{1,0:T(8,128)(2,1)S(1)} %copy-done.30, f32[512,4096]{1,0:T(8,128)} %fusion.245), kind=kOutput, calls=%fused_computation.225 | convolution fusion | flops 4443865088 | bytes 34603008 | tf_op jit(solution)/shard_map/dot_general | solution.py:33
  1368.7 32.9 %reduce-scatter.7.cloned.1.call-done = bf16[128,1024]{1,0:T(8,128)(2,1)} async-done(((bf16[1024,1024]{1,0:T(8,128)(2,1)}), bf16[128,1024]{1,0:T(8,128)(2,1)}) %reduce-scatter.7.cloned.1.call-update) | async-done | bytes 262160 | tf_op jit(solution)/shard_map/reduce_scatter | solution.py:293
  1403.4 34.7 %reduce-scatter.13.cloned.1.call-done = bf16[128,1024]{1,0:T(8,128)(2,1)} async-done(((bf16[1024,1024]{1,0:T(8,128)(2,1)}), bf16[128,1024]{1,0:T(8,128)(2,1)}) %reduce-scatter.13.cloned.1.call-update) | async-done | bytes 262160 | tf_op jit(solution)/shard_map/reduce_scatter | solution.py:293
  1439.9 88.7 %reduce-scatter.15.cloned.1.call-done = bf16[128,4096]{1,0:T(8,128)(2,1)} async-done(((bf16[1024,4096]{1,0:T(8,128)(2,1)}), bf16[128,4096]{1,0:T(8,128)(2,1)}) %reduce-scatter.15.cloned.1.call-update) | async-done | bytes 1048592 | tf_op jit(solution)/shard_map/reduce_scatter | solution.py:293
  1531.3 87.4 %reduce-scatter.17.cloned.1.call-done = bf16[512,1024]{1,0:T(8,128)(2,1)} async-done(((bf16[4096,1024]{1,0:T(8,128)(2,1)}), bf16[512,1024]{1,0:T(8,128)(2,1)}) %reduce-scatter.17.cloned.1.call-update) | async-done | bytes 1048592 | tf_op jit(solution)/shard_map/reduce_scatter | solution.py:293
  (519 shorter events, 570.3 us)
Async XLA Ops:
  7.2 1358.8 %reduce-scatter.9.cloned.1.call-start = ((), (), s32[]{:S(2)}) async-start(), calls=%async_computation.7 | async-start | bytes 294912 | tf_op jit(solution)/shard_map/reduce_scatter | solution.py:293
  12.3 436.8 %copy-start.47 = (f32[1024]{0:T(1024)S(1)}, f32[1024]{0:T(1024)}, u32[]{:S(2)}) copy-start(f32[1024]{0:T(1024)} %mul.565) | copy-start | bytes 12292
  86.2 24.6 %collective-permute-start = (bf16[512,1024]{1,0:T(8,128)(2,1)S(1)}, bf16[512,1024]{1,0:T(8,128)(2,1)}, u32[]{:S(2)}, u32[]{:S(2)}) collective-permute-start(bf16[512,1024]{1,0:T(8,128)(2,1)S(1)} %get-tuple-element.1825), channel_id=1, source_target_pairs={{0,8},{8,16},{16,24},{1,9},{9,17},{17,25},{2,10},{10,18},{18,26},{... | collective-permute-start | bytes 3145736 | tf_op jit(solution)/shard_map/while/body/eval_jaxpr/ppermute | solution.py:13
  184.6 27.2 %collective-permute-start = (bf16[512,1024]{1,0:T(8,128)(2,1)S(1)}, bf16[512,1024]{1,0:T(8,128)(2,1)}, u32[]{:S(2)}, u32[]{:S(2)}) collective-permute-start(bf16[512,1024]{1,0:T(8,128)(2,1)S(1)} %get-tuple-element.1825), channel_id=1, source_target_pairs={{0,8},{8,16},{16,24},{1,9},{9,17},{17,25},{2,10},{10,18},{18,26},{... | collective-permute-start | bytes 3145736 | tf_op jit(solution)/shard_map/while/body/eval_jaxpr/ppermute | solution.py:13
  218.7 93.4 %collective-permute-start = (bf16[512,1024]{1,0:T(8,128)(2,1)S(1)}, bf16[512,1024]{1,0:T(8,128)(2,1)}, u32[]{:S(2)}, u32[]{:S(2)}) collective-permute-start(bf16[512,1024]{1,0:T(8,128)(2,1)S(1)} %get-tuple-element.1825), channel_id=1, source_target_pairs={{0,8},{8,16},{16,24},{1,9},{9,17},{17,25},{2,10},{10,18},{18,26},{... | collective-permute-start | bytes 3145736 | tf_op jit(solution)/shard_map/while/body/eval_jaxpr/ppermute | solution.py:13
  318.9 25.4 %collective-permute-start = (bf16[512,1024]{1,0:T(8,128)(2,1)S(1)}, bf16[512,1024]{1,0:T(8,128)(2,1)}, u32[]{:S(2)}, u32[]{:S(2)}) collective-permute-start(bf16[512,1024]{1,0:T(8,128)(2,1)S(1)} %get-tuple-element.1825), channel_id=1, source_target_pairs={{0,8},{8,16},{16,24},{1,9},{9,17},{17,25},{2,10},{10,18},{18,26},{... | collective-permute-start | bytes 3145736 | tf_op jit(solution)/shard_map/while/body/eval_jaxpr/ppermute | solution.py:13
  351.1 92.1 %collective-permute-start = (bf16[512,1024]{1,0:T(8,128)(2,1)S(1)}, bf16[512,1024]{1,0:T(8,128)(2,1)}, u32[]{:S(2)}, u32[]{:S(2)}) collective-permute-start(bf16[512,1024]{1,0:T(8,128)(2,1)S(1)} %get-tuple-element.1825), channel_id=1, source_target_pairs={{0,8},{8,16},{16,24},{1,9},{9,17},{17,25},{2,10},{10,18},{18,26},{... | collective-permute-start | bytes 3145736 | tf_op jit(solution)/shard_map/while/body/eval_jaxpr/ppermute | solution.py:13
  474.0 733.5 %copy-start.53 = (f32[512]{0:T(512)S(1)}, f32[512]{0:T(512)}, u32[]{:S(2)}) copy-start(f32[512]{0:T(512)} %get-tuple-element.1385) | copy-start | bytes 6148
  474.0 733.5 %copy-start.56 = (f32[1024]{0:T(1024)S(1)}, f32[1024]{0:T(1024)}, u32[]{:S(2)}) copy-start(f32[1024]{0:T(1024)} %mul.573) | copy-start | bytes 12292
  504.9 40.9 %collective-permute-start.1 = (bf16[512,1024]{1,0:T(8,128)(2,1)}, bf16[512,1024]{1,0:T(8,128)(2,1)}, u32[]{:S(2)}, u32[]{:S(2)}) collective-permute-start(bf16[512,1024]{1,0:T(8,128)(2,1)} %get-tuple-element.1654), channel_id=1, source_target_pairs={{8,0},{16,8},{24,16},{9,1},{17,9},{25,17},{10,2},{18,10},{26,18},{... | collective-permute-start | bytes 3145736 | tf_op jit(solution)/shard_map/while/body/eval_jaxpr/ppermute | solution.py:13
  574.0 71.4 %collective-permute-start.1 = (bf16[512,1024]{1,0:T(8,128)(2,1)}, bf16[512,1024]{1,0:T(8,128)(2,1)}, u32[]{:S(2)}, u32[]{:S(2)}) collective-permute-start(bf16[512,1024]{1,0:T(8,128)(2,1)} %get-tuple-element.1654), channel_id=1, source_target_pairs={{8,0},{16,8},{24,16},{9,1},{17,9},{25,17},{10,2},{18,10},{26,18},{... | collective-permute-start | bytes 3145736 | tf_op jit(solution)/shard_map/while/body/eval_jaxpr/ppermute | solution.py:13
  595.7 20.1 %copy-start.44 = (f32[1024]{0:T(1024)S(1)}, f32[1024]{0:T(1024)}, u32[]{:S(2)}) copy-start(f32[1024]{0:T(1024)} %get-tuple-element.1778) | copy-start | bytes 12292 | tf_op jit(solution)/shard_map/while
  595.7 21.1 %copy-start.4 = (f32[1024,1024]{1,0:T(8,128)S(1)}, f32[1024,1024]{1,0:T(8,128)}, u32[]{:S(2)}) copy-start(f32[1024,1024]{1,0:T(8,128)} %get-tuple-element.1777) | copy-start | bytes 12582916 | tf_op jit(solution)/shard_map/while
  616.8 28.6 %copy-start.60 = (s32[2,1,16]{2,1,0:T(1,128)S(1)}, s32[2,1,16]{2,1,0:T(1,128)}, u32[]{:S(2)}) copy-start(s32[2,1,16]{2,1,0:T(1,128)} %get-tuple-element.1895) | copy-start | bytes 388 | tf_op jit(solution)/shard_map/while
  671.5 329.5 %collective-permute-start.1 = (bf16[512,1024]{1,0:T(8,128)(2,1)}, bf16[512,1024]{1,0:T(8,128)(2,1)}, u32[]{:S(2)}, u32[]{:S(2)}) collective-permute-start(bf16[512,1024]{1,0:T(8,128)(2,1)} %get-tuple-element.1654), channel_id=1, source_target_pairs={{8,0},{16,8},{24,16},{9,1},{17,9},{25,17},{10,2},{18,10},{26,18},{... | collective-permute-start | bytes 3145736 | tf_op jit(solution)/shard_map/while/body/eval_jaxpr/ppermute | solution.py:13
  693.2 20.1 %copy-start.44 = (f32[1024]{0:T(1024)S(1)}, f32[1024]{0:T(1024)}, u32[]{:S(2)}) copy-start(f32[1024]{0:T(1024)} %get-tuple-element.1778) | copy-start | bytes 12292 | tf_op jit(solution)/shard_map/while
  693.3 21.1 %copy-start.4 = (f32[1024,1024]{1,0:T(8,128)S(1)}, f32[1024,1024]{1,0:T(8,128)}, u32[]{:S(2)}) copy-start(f32[1024,1024]{1,0:T(8,128)} %get-tuple-element.1777) | copy-start | bytes 12582916 | tf_op jit(solution)/shard_map/while
  714.3 286.7 %copy-start.60 = (s32[2,1,16]{2,1,0:T(1,128)S(1)}, s32[2,1,16]{2,1,0:T(1,128)}, u32[]{:S(2)}) copy-start(s32[2,1,16]{2,1,0:T(1,128)} %get-tuple-element.1895) | copy-start | bytes 388 | tf_op jit(solution)/shard_map/while
  723.8 277.2 %copy-start.5 = (f32[1024,1024]{1,0:T(8,128)}, f32[1024,1024]{1,0:T(8,128)S(1)}, u32[]{:S(2)}) copy-start(f32[1024,1024]{1,0:T(8,128)S(1)} %get-tuple-element.1804) | copy-start | bytes 12582916 | tf_op jit(solution)/shard_map/while
  1129.5 67.4 %collective-permute-start.1 = (bf16[512,1024]{1,0:T(8,128)(2,1)}, bf16[512,1024]{1,0:T(8,128)(2,1)}, u32[]{:S(2)}, u32[]{:S(2)}) collective-permute-start(bf16[512,1024]{1,0:T(8,128)(2,1)} %get-tuple-element.1654), channel_id=1, source_target_pairs={{8,0},{16,8},{24,16},{9,1},{17,9},{25,17},{10,2},{18,10},{26,18},{... | collective-permute-start | bytes 3145736 | tf_op jit(solution)/shard_map/while/body/eval_jaxpr/ppermute | solution.py:13
  1152.5 21.1 %copy-start.4 = (f32[1024,1024]{1,0:T(8,128)S(1)}, f32[1024,1024]{1,0:T(8,128)}, u32[]{:S(2)}) copy-start(f32[1024,1024]{1,0:T(8,128)} %get-tuple-element.1777) | copy-start | bytes 12582916 | tf_op jit(solution)/shard_map/while
  1173.5 23.4 %copy-start.60 = (s32[2,1,16]{2,1,0:T(1,128)S(1)}, s32[2,1,16]{2,1,0:T(1,128)}, u32[]{:S(2)}) copy-start(s32[2,1,16]{2,1,0:T(1,128)} %get-tuple-element.1895) | copy-start | bytes 388 | tf_op jit(solution)/shard_map/while
  1207.4 47.5 %copy-start.29 = (bf16[512,1024]{1,0:T(8,128)(2,1)}, bf16[512,1024]{1,0:T(8,128)(2,1)S(1)}, u32[]{:S(2)}) copy-start(bf16[512,1024]{1,0:T(8,128)(2,1)S(1)} %bitcast_select_fusion.17) | copy-start | bytes 3145732
  1207.5 50.7 %slice-start.2 = ((s8[8388608]{0:T(1024)(128)(4,1)}), s8[4194304]{0:T(1024)(128)(4,1)S(1)}, s32[]{:S(2)}) async-start(s8[8388608]{0:T(1024)(128)(4,1)} %bitcast.417), calls=%async_computation.14 | async-start | bytes 8388608
  1219.7 26.0 %copy-start.26 = (f32[512,1024]{1,0:T(8,128)S(1)}, f32[512,1024]{1,0:T(8,128)}, u32[]{:S(2)}) copy-start(f32[512,1024]{1,0:T(8,128)} %get-tuple-element.1386) | copy-start | bytes 6291460
  1219.7 38.5 %slice-start.3 = ((s8[8388608]{0:T(1024)(128)(4,1)}), s8[4194304]{0:T(1024)(128)(4,1)S(1)}, s32[]{:S(2)}) async-start(s8[8388608]{0:T(1024)(128)(4,1)} %bitcast.417), calls=%async_computation.15 | async-start | bytes 8388608
  1272.1 95.2 %reduce-scatter.11.cloned.1.call-start = ((), (), s32[]{:S(2)}) async-start(), calls=%async_computation.8 | async-start | bytes 294912 | tf_op jit(solution)/shard_map/reduce_scatter | solution.py:293
  1278.5 123.1 %reduce-scatter.7.cloned.1.call-start = ((), (), s32[]{:S(2)}) async-start(), calls=%async_computation.6 | async-start | bytes 2359296 | tf_op jit(solution)/shard_map/reduce_scatter | solution.py:293
  1287.6 150.4 %reduce-scatter.13.cloned.1.call-start = ((), (), s32[]{:S(2)}) async-start(), calls=%async_computation.9 | async-start | bytes 2359296 | tf_op jit(solution)/shard_map/reduce_scatter | solution.py:293
  1293.1 235.4 %reduce-scatter.15.cloned.1.call-start = ((), (), s32[]{:S(2)}) async-start(), calls=%async_computation.10 | async-start | bytes 9437184 | tf_op jit(solution)/shard_map/reduce_scatter | solution.py:293
  1308.7 310.0 %reduce-scatter.17.cloned.1.call-start = ((), (), s32[]{:S(2)}) async-start(), calls=%async_computation.11 | async-start | bytes 9437184 | tf_op jit(solution)/shard_map/reduce_scatter | solution.py:293
  1341.5 20.3 %copy-start.52 = (f32[512]{0:T(512)S(1)}, f32[512]{0:T(512)}, u32[]{:S(2)}) copy-start(f32[512]{0:T(512)} %copy-done.51) | copy-start | bytes 6148
  (95 other events, 739.9 us)
Sparse Core Ops, SparseCore 0:
  1272.2 61.7 reduce-scatter.8
  1336.9 28.4 reduce-scatter.10
  1367.7 33.8 reduce-scatter.6
  1403.7 34.3 reduce-scatter.12
  1440.2 88.2 reduce-scatter.14
  1530.7 87.9 reduce-scatter.16
where the time goes:
time: 1650 us; the launch traced here: 1630 us
  waiting for transfers between devices  643 us (39%)
  matrix products  342 us (21%)
  other arithmetic  293 us (18%)
  starting transfers between devices  165 us (10%)
  local copies, waits for them, and re-layouts  136 us (8%)
  loops' own time  19.7 us (1%)
    ppermute x9, waiting for transfers between devices, from_behind(): return lax.ppermute(block, axis, route)  400 us
    reduce_scatter x6, waiting for transfers between devices, body(): lax.psum_scatter(for_sending(attn_totals + ffn_totals), 'dp', scatter_dim...  244 us
    add x20, other arithmetic, backward_tick(): running + portion  181 us
    ppermute x9, starting transfers between devices, from_behind(): return lax.ppermute(block, axis, route)  165 us
    dot_general x12, matrix products, contract_rows(): lax.dot_general(left, right, (((0,), (0,)), ((), ())), preferred_element_...  85.2 us
    another operation x55, local copies, waits for them, and re-layouts  84.2 us
    dot_general x12, matrix products, contract_cols(): lax.dot_general(left, right, (((1,), (1,)), ((), ())), preferred_element_...  81.1 us
    dot_general x2, matrix products, forward_parts(): jnp.dot(activated, w_down, preferred_element_type=jnp.float32)  61.7 us
  transfers between devices with their start and end apart: 15, of which 12 were waited for; matrix products, arithmetic and copies ran while one was open for 18% of the time, Pallas kernels for 0%

commit v1 on v0

v1 whole, which is shorter than its diff:
```python
import functools

import jax
import jax.numpy as jnp
from jax import lax
from jax.experimental import pallas as pl
from jax.experimental.pallas import tpu as pltpu
from jax.sharding import PartitionSpec as P

NORM_EPS = 1e-06
MASKED = -1e30
LOG2E = 1.4426950408889634
FWD_ROWS = 128
BWD_ROWS = 256
FFN_TILE = 1024
SKEW = 2
MIB = 1 << 20

BF16 = jnp.bfloat16
F32 = jnp.float32


def in_hbm(array):
    return pltpu.with_memory_space_constraint(array, pltpu.HBM)


def in_vmem(array):
    return pltpu.with_memory_space_constraint(array, pltpu.VMEM)


def dot(left, right):
    return jnp.dot(left, right, preferred_element_type=F32)


def dot_t(left, right):
    return lax.dot_general(left, right, (((1,), (1,)), ((), ())), preferred_element_type=F32)


def inverse_rms(rows):
    return lax.rsqrt(jnp.mean(rows * rows, axis=-1, keepdims=True) + NORM_EPS)


def gelu_parts(u):
    t = pl.reciprocal(1.0 + jnp.abs(u) * 0.23164190, approx=True)
    bell = jnp.exp2(u * u * (-0.5 * LOG2E))
    poly = t * (0.127414796 + t * (-0.142248368 + t * (0.7107068705 + t * (-0.7265760135 + t * 0.5307027145))))
    tail = poly * bell
    cdf = jnp.where(u >= 0, 1.0 - tail, tail)
    return u * cdf, cdf + u * bell * 0.3989422804014327


def position_bias(start_col, first_row, rows, length):
    own = first_row + lax.broadcasted_iota(jnp.int32, (rows, length), 0)
    other = lax.broadcasted_iota(jnp.int32, (rows, length), 1)
    return jnp.where((other >= start_col) & (other <= own), 0.0, MASKED)


def forward_kernel(
    geometry, meta, starts, tokens, incoming, gain_attn, w_query, w_kv, w_out, gain_ffn, w_up, w_down,
    *refs,
):
    rows, row_len, heads, size = geometry
    saved = refs[len(FWD_SAVED):2 * len(FWD_SAVED) + 1]
    out, hs, n1s, qs, ks, vs, kts, vts, os_, mids, n2s, acts, slopes, lses, outs = saved
    (h_v, n1_v, q_v, k_v, v_v, kt_v, vt_v, o_v, mid_v, n2_v, act_v, slope_v, lse_v, out_v, bias_v, sems) = (
        refs[2 * len(FWD_SAVED) + 1:]
    )
    parts = row_len // rows
    active, chunk, first = meta[0], meta[1], meta[2]
    width = heads * size
    scale = size**-0.5 * LOG2E

    @pl.when(active == 1)
    def _():
        row = chunk // parts
        place = chunk % parts
        at = pl.ds(pl.multiple_of(chunk * rows, rows), rows)
        within = pl.ds(pl.multiple_of(place * rows, rows), rows)
        whole = pl.ds(pl.multiple_of(row * row_len, row_len), row_len)

        @pl.when(first == 1)
        def _():
            pltpu.make_async_copy(tokens.at[at], h_v, sems.at[0]).start()

        @pl.when(first == 0)
        def _():
            pltpu.make_async_copy(incoming, h_v, sems.at[0]).start()

        load_v = pltpu.make_async_copy(vs.at[whole], v_v, sems.at[1])
        load_kt = pltpu.make_async_copy(kts.at[row], kt_v, sems.at[2])
        load_v.start()
        load_kt.start()
        pending = []

        def keep(source, target, slot):
            copy = pltpu.make_async_copy(source, target, sems.at[slot])
            copy.start()
            pending.append(copy)

        start_col = starts[at, :]
        for step in range(parts):
            @pl.when(place == step)
            def _():
                bias_v[:, : (step + 1) * rows] = position_bias(start_col, step * rows, rows, (step + 1) * rows)

        pltpu.make_async_copy(incoming, h_v, sems.at[0]).wait()
        h = h_v[...].astype(F32)
        n1 = (h * inverse_rms(h) * gain_attn[...].astype(F32)).astype(BF16)
        n1_v[...] = n1
        keep(h_v, hs.at[at], 3)
        keep(n1_v, n1s.at[at], 4)
        kv = dot(n1, w_kv[...]).astype(BF16)
        q_v[...] = dot(n1, w_query[...]).astype(BF16)
        k_v[...] = kv[:, :size]
        keep(k_v, ks.at[at], 5)
        keep(q_v, qs.at[at], 6)
        load_v.wait()
        load_kt.wait()
        v_v[within, :] = kv[:, size:]
        kt_v[:, within] = kv[:, :size].T
        vt_v[...] = kv[:, size:].T
        keep(v_v.at[within], vs.at[at], 7)
        keep(kt_v.at[:, within], kts.at[row, :, within], 8)
        keep(vt_v, vts.at[row, :, within], 9)

        def attend(length):
            lane = lax.broadcasted_iota(jnp.int32, (rows, size), 1)
            stats = jnp.zeros((rows, size), F32)
            for head in range(heads):
                cols = slice(head * size, (head + 1) * size)
                scores = dot(q_v[:, cols], kt_v[:, :length]) * scale + bias_v[:, :length]
                top = jnp.max(scores, axis=1, keepdims=True)
                weights = jnp.exp2(scores - top)
                total = jnp.sum(weights, axis=1, keepdims=True)
                mixed = dot(weights.astype(BF16), v_v[:length, :]) * (1.0 / total)
                o_v[:, cols] = mixed.astype(BF16)
                stats = jnp.where(lane == head, top + jnp.log2(total), stats)
            lse_v[...] = stats

        for step in range(parts):
            pl.when(place == step)(functools.partial(attend, (step + 1) * rows))

        keep(lse_v, lses.at[at], 10)
        keep(o_v, os_.at[at], 11)
        mid = h + dot(o_v[...], w_out[...])
        mid_v[...] = mid
        keep(mid_v, mids.at[at], 12)
        n2 = (mid * inverse_rms(mid) * gain_ffn[...].astype(F32)).astype(BF16)
        n2_v[...] = n2
        keep(n2_v, n2s.at[at], 13)
        ffn = w_up.shape[1]
        tile = min(FFN_TILE, ffn)
        total = mid
        for f in range(ffn // tile):
            cols = slice(f * tile, (f + 1) * tile)
            act, slope = gelu_parts(dot(n2, w_up[:, cols]))
            act = act.astype(BF16)
            act_v[:, cols] = act
            slope_v[:, cols] = slope.astype(BF16)
            total = total + dot(act, w_down[cols, :])
        keep(act_v, acts.at[at], 14)
        keep(slope_v, slopes.at[at], 15)
        result = total.astype(BF16)
        out[...] = result
        out_v[...] = result
        keep(out_v, outs.at[at], 16)
        for copy in pending:
            copy.wait()


FWD_SAVED = ("hs", "n1s", "qs", "ks", "vs", "kts", "vts", "os", "mids", "n2s", "acts", "slopes", "lses", "outs")


def forward_chunk(geometry, meta, starts, tokens, incoming, weights, saved):
    rows, row_len, heads, size = geometry
    width = tokens.shape[1]
    ffn = weights[5].shape[1]
    vmem = pl.BlockSpec(memory_space=pltpu.VMEM)
    anywhere = pl.BlockSpec(memory_space=pltpu.HBM)
    lead = 5 + len(weights)
    flops = 2 * rows * (2 * width * heads * size + 2 * width * size + 2 * width * ffn + row_len * heads * size)
    return pl.pallas_call(
        functools.partial(forward_kernel, geometry),
        out_shape=[jax.ShapeDtypeStruct((rows, width), BF16)]
        + [pltpu.HBM(array.shape, array.dtype) for array in saved],
        in_specs=[pl.BlockSpec(memory_space=pltpu.SMEM), vmem, anywhere, anywhere]
        + [vmem] * len(weights) + [anywhere] * len(saved),
        out_specs=[vmem] + [anywhere] * len(saved),
        input_output_aliases={4 + len(weights) + i: 1 + i for i in range(len(saved))},
        scratch_shapes=[
            pltpu.VMEM((rows, width), BF16),
            pltpu.VMEM((rows, width), BF16),
            pltpu.VMEM((rows, heads * size), BF16),
            pltpu.VMEM((rows, size), BF16),
            pltpu.VMEM((row_len, size), BF16),
            pltpu.VMEM((size, row_len), BF16),
            pltpu.VMEM((size, rows), BF16),
            pltpu.VMEM((rows, heads * size), BF16),
            pltpu.VMEM((rows, width), F32),
            pltpu.VMEM((rows, width), BF16),
            pltpu.VMEM((rows, ffn), BF16),
            pltpu.VMEM((rows, ffn), BF16),
            pltpu.VMEM((rows, size), F32),
            pltpu.VMEM((rows, width), BF16),
            pltpu.VMEM((rows, row_len), F32),
            pltpu.SemaphoreType.DMA((17,)),
        ],
        compiler_params=pltpu.CompilerParams(vmem_limit_bytes=16 * MIB),
        cost_estimate=pl.CostEstimate(flops=flops, bytes_accessed=8 * MIB, transcendentals=0),
        name="forward_chunk",
    )(meta, starts, in_hbm(tokens), incoming, *map(in_vmem, weights), *saved)


BWD_SAVED = ("gbs", "dus", "gms", "dqs", "dkvs", "igs", "gains", "carry")


def norm_backward(rows, gain, upstream):
    inverse = inverse_rms(rows)
    unit = rows * inverse
    steered = upstream * gain
    grad = inverse * (steered - unit * jnp.mean(steered * unit, axis=-1, keepdims=True))
    return grad, jnp.sum(upstream * unit, axis=0, keepdims=True)


def backward_kernel(
    geometry, meta, starts, cotangent, incoming, hs, qs, ks, kts, vts, mids, slopes, lses,
    gain_attn, w_query, w_kv, w_out, gain_ffn, w_up, w_down, *refs,
):
    rows, row_len, heads, size = geometry
    count = len(BWD_SAVED)
    out, gbs, dus, gms, dqs, dkvs, igs, gains, carry = refs[count:2 * count + 1]
    (g_v, h_v, q_v, k_v, kt_v, vt_v, mid_v, slope_v, lse_v, du_v, gm_v, do_v, dq_v, dkv_v, ig_v, gain_v, carry_v,
     bias_v, p_v, ds_v, qt_v, dot_v, sems) = refs[2 * count + 1:]
    parts = row_len // rows
    active, chunk, first = meta[0], meta[1], meta[2]
    scale = size**-0.5

    @pl.when(active == 1)
    def _():
        row = chunk // parts
        place = chunk % parts
        at = pl.ds(pl.multiple_of(chunk * rows, rows), rows)
        within = pl.ds(pl.multiple_of(place * rows, rows), rows)
        whole = pl.ds(pl.multiple_of(row * row_len, row_len), row_len)

        @pl.when(first == 1)
        def _():
            pltpu.make_async_copy(cotangent.at[at], g_v, sems.at[0]).start()

        @pl.when(first == 0)
        def _():
            pltpu.make_async_copy(incoming, g_v, sems.at[0]).start()

        loads = [
            pltpu.make_async_copy(source, target, sems.at[1 + i])
            for i, (source, target) in enumerate((
                (slopes.at[at], slope_v),
                (mids.at[at], mid_v),
                (qs.at[at], q_v),
                (lses.at[at], lse_v),
                (kts.at[row], kt_v),
                (vts.at[row], vt_v),
                (ks.at[whole], k_v),
                (carry, carry_v),
                (hs.at[at], h_v),
            ))
        ]
        for load in loads:
            load.start()
        pending = []

        def keep(source, target, slot):
            copy = pltpu.make_async_copy(source, target, sems.at[slot])
            copy.start()
            pending.append(copy)

        start_col = starts[at, :]
        for step in range(parts):
            @pl.when(place == step)
            def _():
                bias_v[:, : (step + 1) * rows] = position_bias(start_col, step * rows, rows, (step + 1) * rows)

        pltpu.make_async_copy(incoming, g_v, sems.at[0]).wait()
        g = g_v[...]
        keep(g_v, gbs.at[at], 10)
        loads[0].wait()
        ffn = w_up.shape[1]
        tile = min(FFN_TILE, ffn)
        dn2 = None
        for f in range(ffn // tile):
            cols = slice(f * tile, (f + 1) * tile)
            du = (slope_v[:, cols].astype(F32) * dot_t(g, w_down[cols, :])).astype(BF16)
            du_v[:, cols] = du
            part = dot_t(du, w_up[:, cols])
            dn2 = part if dn2 is None else dn2 + part
        keep(du_v, dus.at[at], 11)
        loads[1].wait()
        dv, dgain_ffn = norm_backward(mid_v[...], gain_ffn[...].astype(F32), dn2)
        dmid = g.astype(F32) + dv
        mid_v[...] = dmid
        gm = dmid.astype(BF16)
        gm_v[...] = gm
        keep(gm_v, gms.at[at], 12)
        do_v[...] = dot_t(gm, w_out[...]).astype(BF16)
        for load in loads[2:8]:
            load.wait()

        def attend(length, last):
            for head in range(heads):
                cols = slice(head * size, (head + 1) * size)
                span = slice(head * rows, (head + 1) * rows)
                q_h = q_v[:, cols]
                do_h = do_v[:, cols]
                qt_v[:, span] = q_h.T
                dot_v[:, span] = do_h.T
                scores = dot(q_h, kt_v[:, :length]) * (scale * LOG2E) + bias_v[:, :length]
                probs = jnp.exp2(scores - lse_v[:, head:head + 1])
                p_v[span, :length] = probs.astype(BF16)
                dprobs = dot(do_h, vt_v[:, :length])
                mean = jnp.sum(probs * dprobs, axis=1, keepdims=True)
                dscores = (probs * (dprobs - mean)).astype(BF16)
                ds_v[span, :length] = dscores
                dq_v[:, cols] = (dot(dscores, k_v[:length, :]) * scale).astype(BF16)
            dkt = dot(qt_v[...], ds_v[:, :length])
            dvt = dot(dot_v[...], p_v[:, :length])
            if not last:
                dkt = dkt + carry_v[:size, :length]
                dvt = dvt + carry_v[size:, :length]
            if length > rows:
                carry_v[:size, :length - rows] = dkt[:, :length - rows]
                carry_v[size:, :length - rows] = dvt[:, :length - rows]
            dkv_v[:, :size] = (dkt[:, length - rows:].T * scale).astype(BF16)
            dkv_v[:, size:] = dvt[:, length - rows:].T.astype(BF16)

        for step in range(parts):
            pl.when(place == step)(functools.partial(attend, (step + 1) * rows, step == parts - 1))

        keep(carry_v, carry, 13)
        keep(dq_v, dqs.at[at], 14)
        keep(dkv_v, dkvs.at[at], 15)
        dn1 = dot_t(dq_v[...], w_query[...]) + dot_t(dkv_v[...], w_kv[...])
        loads[8].wait()
        dv, dgain_attn = norm_backward(h_v[...].astype(F32), gain_attn[...].astype(F32), dn1)
        result = (mid_v[...] + dv).astype(BF16)
        out[...] = result
        ig_v[...] = result
        keep(ig_v, igs.at[at], 16)
        gain_v[...] = jnp.concatenate([dgain_attn, dgain_ffn, jnp.zeros((6, dgain_attn.shape[1]), F32)], axis=0)
        keep(gain_v, gains.at[chunk], 17)
        for copy in pending:
            copy.wait()


def backward_chunk(geometry, meta, starts, cotangent, incoming, kept, weights, saved):
    rows, row_len, heads, size = geometry
    width = cotangent.shape[1]
    ffn = weights[5].shape[1]
    vmem = pl.BlockSpec(memory_space=pltpu.VMEM)
    anywhere = pl.BlockSpec(memory_space=pltpu.HBM)
    lead = 4 + len(kept) + len(weights)
    flops = 2 * rows * (2 * width * heads * size + 2 * width * size + 2 * width * ffn + 3 * row_len * heads * size)
    return pl.pallas_call(
        functools.partial(backward_kernel, geometry),
        out_shape=[jax.ShapeDtypeStruct((rows, width), BF16)]
        + [pltpu.HBM(array.shape, array.dtype) for array in saved],
        in_specs=[pl.BlockSpec(memory_space=pltpu.SMEM), vmem, anywhere, anywhere]
        + [anywhere] * len(kept) + [vmem] * len(weights) + [anywhere] * len(saved),
        out_specs=[vmem] + [anywhere] * len(saved),
        input_output_aliases={lead + i: 1 + i for i in range(len(saved))},
        scratch_shapes=[
            pltpu.VMEM((rows, width), BF16),
            pltpu.VMEM((rows, width), BF16),
            pltpu.VMEM((rows, heads * size), BF16),
            pltpu.VMEM((row_len, size), BF16),
            pltpu.VMEM((size, row_len), BF16),
            pltpu.VMEM((size, row_len), BF16),
            pltpu.VMEM((rows, width), F32),
            pltpu.VMEM((rows, ffn), BF16),
            pltpu.VMEM((rows, size), F32),
            pltpu.VMEM((rows, ffn), BF16),
            pltpu.VMEM((rows, width), BF16),
            pltpu.VMEM((rows, heads * size), BF16),
            pltpu.VMEM((rows, heads * size), BF16),
            pltpu.VMEM((rows, 2 * size), BF16),
            pltpu.VMEM((rows, width), BF16),
            pltpu.VMEM((8, width), F32),
            pltpu.VMEM((2 * size, row_len), F32),
            pltpu.VMEM((rows, row_len), F32),
            pltpu.VMEM((heads * rows, row_len), BF16),
            pltpu.VMEM((heads * rows, row_len), BF16),
            pltpu.VMEM((size, heads * rows), BF16),
            pltpu.VMEM((size, heads * rows), BF16),
            pltpu.SemaphoreType.DMA((18,)),
        ],
        compiler_params=pltpu.CompilerParams(vmem_limit_bytes=30 * MIB),
        cost_estimate=pl.CostEstimate(flops=flops, bytes_accessed=8 * MIB, transcendentals=0),
        name="backward_chunk",
    )(meta, starts, in_hbm(cotangent), incoming, *map(in_hbm, kept), *map(in_vmem, weights), *saved)


def unwritten(shapes):
    return pl.pallas_call(
        lambda *refs: None,
        out_shape=shapes,
        out_specs=[pl.BlockSpec(memory_space=pltpu.HBM)] * len(shapes),
        name="unwritten",
    )()


def segment_starts(lengths, row_len):
    count = lengths.shape[1]
    upto = jnp.arange(count)[:, None] <= jnp.arange(count)[None, :]
    ends = jnp.sum(jnp.where(upto[None], lengths[:, :, None], 0), axis=1)
    position = jnp.arange(row_len, dtype=jnp.int32)
    over = ends[:, None, :] <= position[None, :, None]
    start = jnp.sum(jnp.where(over, lengths[:, None, :], 0), axis=2)
    segment = jnp.sum(over.astype(jnp.int32), axis=2)
    return jnp.where(segment < count - 1, start, position[None]).astype(jnp.int32)


def contract_rows(left, right):
    return lax.dot_general(left, right, (((0,), (0,)), ((), ())), preferred_element_type=F32)


def body(
    tokens, lengths, gain_attn, w_query, w_key, w_value, w_out, gain_ffn, w_up, w_down, cotangent
):
    micro, row_len, width = tokens.shape
    size = w_key.shape[2]
    heads = w_query.shape[2] // size
    ffn = w_up.shape[2]
    count = micro * row_len
    sections = lax.axis_size("section")
    place = lax.axis_index("section")
    weights = (
        gain_attn, w_query[0], jnp.concatenate([w_key[0], w_value[0]], axis=1), w_out[0],
        gain_ffn, w_up[0], w_down[0],
    )
    token_rows = tokens.reshape(count, width)
    cotangent_rows = cotangent.reshape(count, width)
    starts = segment_starts(lengths[:, 0], row_len).reshape(count, 1)

    def empty(*shape, dtype=BF16):
        return pltpu.HBM(shape, dtype)

    def meta_of(tick, chunks, rank, order):
        step = tick - SKEW * rank
        active = (step >= 0) & (step < chunks)
        chunk = order(jnp.clip(step, 0, chunks - 1))
        return jnp.stack([active.astype(jnp.int32), chunk.astype(jnp.int32), (rank == 0).astype(jnp.int32)])

    def hop(block, tick, chunks, rank_of, shift):
        route = [
            (s, s + shift)
            for s in range(sections)
            if 0 <= s + shift < sections and 0 <= tick - SKEW * rank_of(s) < chunks
        ]
        return lax.ppermute(block, "section", route) if route else None

    fwd_geometry = (FWD_ROWS, row_len, heads, size)
    fwd_chunks = count // FWD_ROWS
    saved = [
        empty(count, width), empty(count, width), empty(count, heads * size), empty(count, size), empty(count, size),
        empty(micro, size, row_len), empty(micro, size, row_len), empty(count, heads * size),
        empty(count, width, dtype=F32), empty(count, width), empty(count, ffn), empty(count, ffn),
        empty(count, size, dtype=F32), empty(count, width),
    ]
    saved = unwritten(saved)
    received = {}
    nothing = jnp.zeros((FWD_ROWS, width), BF16)
    for tick in range(fwd_chunks + SKEW * (sections - 1)):
        meta = meta_of(tick, fwd_chunks, place, lambda step: step)
        incoming = received.pop(tick - SKEW, None)
        out, *saved = forward_chunk(
            fwd_geometry, meta, starts, token_rows, nothing if incoming is None else incoming, weights, saved
        )
        received[tick] = hop(out, tick, fwd_chunks, lambda s: s, 1)

    kept = dict(zip(FWD_SAVED, saved))
    layer_outs = kept["outs"]
    needed = [kept[name] for name in ("hs", "qs", "ks", "kts", "vts", "mids", "slopes", "lses")]
    bwd_geometry = (BWD_ROWS, row_len, heads, size)
    bwd_chunks = count // BWD_ROWS
    parts = row_len // BWD_ROWS
    saved = [
        empty(count, width), empty(count, ffn), empty(count, width), empty(count, heads * size),
        empty(count, 2 * size), empty(count, width), empty(bwd_chunks, 8, width, dtype=F32),
        empty(2 * size, row_len, dtype=F32),
    ]
    saved = unwritten(saved)
    received = {}
    nothing = jnp.zeros((BWD_ROWS, width), BF16)
    for tick in range(bwd_chunks + SKEW * (sections - 1)):
        meta = meta_of(
            tick, bwd_chunks, sections - 1 - place, lambda step: step // parts * parts + parts - 1 - step % parts
        )
        incoming = received.pop(tick - SKEW, None)
        out, *saved = backward_chunk(
            bwd_geometry, meta, starts, cotangent_rows, nothing if incoming is None else incoming, needed, weights,
            saved,
        )
        received[tick] = hop(out, tick, bwd_chunks, lambda s: sections - 1 - s, -1)
    done = dict(zip(BWD_SAVED, saved))

    gains = jnp.sum(done["gains"], axis=0)
    dkv = done["dkvs"]
    grads = (
        gains[0],
        contract_rows(kept["n1s"], done["dqs"]),
        contract_rows(kept["n1s"], dkv[:, :size]),
        contract_rows(kept["n1s"], dkv[:, size:]),
        contract_rows(kept["os"], done["gms"]),
        gains[1],
        contract_rows(kept["n2s"], done["dus"]),
        contract_rows(kept["acts"], done["gbs"]),
    )
    shares = tuple(
        lax.psum_scatter(grad.astype(BF16), "dp", scatter_dimension=0, tiled=True).astype(F32) for grad in grads
    )
    shape = (1, micro, row_len, width)
    return (layer_outs.reshape(shape), done["igs"].reshape(shape)) + tuple(share[None] for share in shares)


def solution(mesh):
    return jax.shard_map(
        body,
        mesh=mesh,
        in_specs=(
            P(None, "dp", None),
            P(None, "dp", None),
            P("section", None),
            P("section", None, None),
            P("section", None, None),
            P("section", None, None),
            P("section", None, None),
            P("section", None),
            P("section", None, None),
            P("section", None, None),
            P(None, "dp", None),
        ),
        out_specs=(
            P("section", None, "dp", None),
            P("section", None, "dp", None),
            P("section", "dp"),
            P("section", "dp", None),
            P("section", "dp", None),
            P("section", "dp", None),
            P("section", "dp", None),
            P("section", "dp"),
            P("section", "dp", None),
            P("section", "dp", None),
        ),
        check_vma=False,
    )
```

time: 1650 us -> 667 us (0.40)
  waiting for transfers between devices: 643 us -> 296 us
  matrix products: 342 us -> 44.5 us
  other arithmetic: 293 us -> 17.4 us
  Pallas kernels: 0 us -> 223 us
  starting transfers between devices: 165 us -> 22.3 us
  local copies, waits for them, and re-layouts: 136 us -> 24.1 us
  loops' own time: 19.7 us -> 0 us
    ppermute x9 -> x20, waiting for transfers between devices: 400 us -> 53.9 us  [hop(): return lax.ppermute(block, 'section', route) if route else None]
    dot_general x44 -> x0, matrix products: 257 us -> none  [the longest x12 81.1 us: contract_cols(): lax.dot_general(left, right, (((1,), (1,)), ((), ())), preferred_element_...]
    pallas_call x0 -> x26, Pallas kernels: none -> 223 us  [the longest x14 117 us: forward_chunk(): pl.pallas_call(functools.partial(forward_kernel, geometry), out_shape=[ja...]
    add x22 -> x0, other arithmetic: 182 us -> none  [the longest x20 181 us: backward_tick(): running + portion]
    ppermute x9 -> x20, starting transfers between devices: 165 us -> 21.8 us  [hop(): return lax.ppermute(block, 'section', route) if route else None]
    another operation x55 -> x0, local copies, waits for them, and re-layouts: 84.2 us -> none
    dot_general x12 -> x6, matrix products: 85.2 us -> 44.5 us  [contract_rows(): lax.dot_general(left, right, (((0,), (0,)), ((), ())), preferred_element_...]
    sub x4 -> x0, other arithmetic: 38.2 us -> none  [forward_parts(): jax.nn.softmax(jnp.where(allowed[None], scores, NEG_BIG), axis=-1)]
  transfers between devices with their start and end apart: 15 -> 26, of which waited for: 12 -> 7; matrix products, arithmetic and copies ran while one was open for 18% -> 8% of each run, Pallas kernels for 0% -> 27%
where the time goes in v1:
time: 667 us; the launch traced here: 657 us
  waiting for transfers between devices  296 us (44%)
  Pallas kernels  223 us (33%)
  matrix products  44.5 us (7%)
  local copies, waits for them, and re-layouts  24.1 us (4%)
  starting transfers between devices  22.3 us (3%)
  other arithmetic  17.4 us (3%)
  between operations  16.1 us (2%)
  blocking collectives  13.6 us (2%)
    reduce_scatter x6, waiting for transfers between devices, body(): lax.psum_scatter(grad.astype(BF16), 'dp', scatter_dimension=0, tiled=True)  242 us
    pallas_call x14, Pallas kernels, forward_chunk(): pl.pallas_call(functools.partial(forward_kernel, geometry), out_shape=[ja...  117 us
    pallas_call x10, Pallas kernels, backward_chunk(): pl.pallas_call(functools.partial(backward_kernel, geometry), out_shape=[j...  106 us
    ppermute x20, waiting for transfers between devices, hop(): return lax.ppermute(block, 'section', route) if route else None  53.9 us
    dot_general x6, matrix products, contract_rows(): lax.dot_general(left, right, (((0,), (0,)), ((), ())), preferred_element_...  44.5 us
    unnamed x57, local copies, waits for them, and re-layouts  24 us
    ppermute x20, starting transfers between devices, hop(): return lax.ppermute(block, 'section', route) if route else None  21.8 us
    unnamed x1, blocking collectives  13.6 us
  transfers between devices with their start and end apart: 26, of which 7 were waited for; matrix products, arithmetic and copies ran while one was open for 8% of the time, Pallas kernels for 27%

profile of v1, /device:TPU:0, one launch (start us, length us, event | category | flops | bytes accessed | tf_op | source)
XLA Modules:
  0.0 657.0 jit_solution(13939142920563430257)
XLA Ops:
  21.6 9.4 %forward_chunk.14 = (bf16[128,1024]{1,0:T(8,128)(2,1)}, bf16[1024,1024]{1,0:T(8,128)(2,1)}, bf16[1024,1024]{1,0:T(8,128)(2,1)}, bf16[1024,1024]{1,0:T(8,128)(2,1...) custom-call(s32[3]{0:T(128)S(1)} %get-tuple-element.649.meta, ...), custom_call_target="tpu_custom_call", output_to_operand_aliasing={{1}: (11, {}), {2}: (12, {}), {3}: (13, {}), {4}: (14, {}),... | custom-call | flops 2885681152 | bytes 8388608 | tf_op jit(solution)/shard_map/forward_chunk/pallas_call | solution.py:182
  33.1 12.7 %forward_chunk.15 = (bf16[128,1024]{1,0:T(8,128)(2,1)}, bf16[1024,1024]{1,0:T(8,128)(2,1)}, bf16[1024,1024]{1,0:T(8,128)(2,1)}, bf16[1024,1024]{1,0:T(8,128)(2,1...) custom-call(s32[3]{0:T(128)S(1)} %get-tuple-element.648.meta, ...), custom_call_target="tpu_custom_call", output_to_operand_aliasing={{1}: (11, {}), {2}: (12, {}), {3}: (13, {}), {4}: (14, {}),... | custom-call | flops 2885681152 | bytes 8388608 | tf_op jit(solution)/shard_map/forward_chunk/pallas_call | solution.py:182
  57.3 10.0 %forward_chunk.16 = (bf16[128,1024]{1,0:T(8,128)(2,1)S(1)}, bf16[1024,1024]{1,0:T(8,128)(2,1)}, bf16[1024,1024]{1,0:T(8,128)(2,1)}, bf16[1024,1024]{1,0:T(8,128)...) custom-call(s32[3]{0:T(128)S(1)} %add_add_fusion.8.meta, ...), custom_call_target="tpu_custom_call", output_to_operand_aliasing={{1}: (11, {}), {2}: (12, {}), {3}: (13, {}), {4}: (14, {}),... | custom-call | flops 2885681152 | bytes 8388608 | tf_op jit(solution)/shard_map/forward_chunk/pallas_call | solution.py:182
  68.7 10.6 %forward_chunk.17 = (bf16[128,1024]{1,0:T(8,128)(2,1)S(1)}, bf16[1024,1024]{1,0:T(8,128)(2,1)}, bf16[1024,1024]{1,0:T(8,128)(2,1)}, bf16[1024,1024]{1,0:T(8,128)...) custom-call(s32[3]{0:T(128)S(1)} %add_add_fusion.5.meta, ...), custom_call_target="tpu_custom_call", output_to_operand_aliasing={{1}: (11, {}), {2}: (12, {}), {3}: (13, {}), {4}: (14, {}),... | custom-call | flops 2885681152 | bytes 8388608 | tf_op jit(solution)/shard_map/forward_chunk/pallas_call | solution.py:182
  80.7 8.4 %forward_chunk.18 = (bf16[128,1024]{1,0:T(8,128)(2,1)S(1)}, bf16[1024,1024]{1,0:T(8,128)(2,1)}, bf16[1024,1024]{1,0:T(8,128)(2,1)}, bf16[1024,1024]{1,0:T(8,128)...) custom-call(s32[3]{0:T(128)S(1)} %add_add_fusion.9.meta, ...), custom_call_target="tpu_custom_call", output_to_operand_aliasing={{1}: (11, {}), {2}: (12, {}), {3}: (13, {}), {4}: (14, {}),... | custom-call | flops 2885681152 | bytes 8388608 | tf_op jit(solution)/shard_map/forward_chunk/pallas_call | solution.py:182
  90.4 11.6 %forward_chunk.19 = (bf16[128,1024]{1,0:T(8,128)(2,1)S(1)}, bf16[1024,1024]{1,0:T(8,128)(2,1)}, bf16[1024,1024]{1,0:T(8,128)(2,1)}, bf16[1024,1024]{1,0:T(8,128)...) custom-call(s32[3]{0:T(128)S(1)} %add_add_fusion.4.meta, ...), custom_call_target="tpu_custom_call", output_to_operand_aliasing={{1}: (11, {}), {2}: (12, {}), {3}: (13, {}), {4}: (14, {}),... | custom-call | flops 2885681152 | bytes 8388608 | tf_op jit(solution)/shard_map/forward_chunk/pallas_call | solution.py:182
  103.3 10.1 %forward_chunk.20 = (bf16[128,1024]{1,0:T(8,128)(2,1)S(1)}, bf16[1024,1024]{1,0:T(8,128)(2,1)}, bf16[1024,1024]{1,0:T(8,128)(2,1)}, bf16[1024,1024]{1,0:T(8,128)...) custom-call(s32[3]{0:T(128)S(1)} %add_add_fusion.10.meta, ...), custom_call_target="tpu_custom_call", output_to_operand_aliasing={{1}: (11, {}), {2}: (12, {}), {3}: (13, {}), {4}: (14, {}),... | custom-call | flops 2885681152 | bytes 8388608 | tf_op jit(solution)/shard_map/forward_chunk/pallas_call | solution.py:182
  114.8 10.6 %forward_chunk.21 = (bf16[128,1024]{1,0:T(8,128)(2,1)S(1)}, bf16[1024,1024]{1,0:T(8,128)(2,1)}, bf16[1024,1024]{1,0:T(8,128)(2,1)}, bf16[1024,1024]{1,0:T(8,128)...) custom-call(s32[3]{0:T(128)S(1)} %add_add_fusion.3.meta, ...), custom_call_target="tpu_custom_call", output_to_operand_aliasing={{1}: (11, {}), {2}: (12, {}), {3}: (13, {}), {4}: (14, {}),... | custom-call | flops 2885681152 | bytes 8388608 | tf_op jit(solution)/shard_map/forward_chunk/pallas_call | solution.py:182
  128.2 4.9 collective-permute-done.6.incoming
  133.1 9.1 %forward_chunk.23 = (bf16[128,1024]{1,0:T(8,128)(2,1)S(1)}, bf16[1024,1024]{1,0:T(8,128)(2,1)}, bf16[1024,1024]{1,0:T(8,128)(2,1)}, bf16[1024,1024]{1,0:T(8,128)...) custom-call(s32[3]{0:T(128)S(1)} %add_add_fusion.2.meta, ...), custom_call_target="tpu_custom_call", output_to_operand_aliasing={{1}: (11, {}), {2}: (12, {}), {3}: (13, {}), {4}: (14, {}),... | custom-call | flops 2885681152 | bytes 8388608 | tf_op jit(solution)/shard_map/forward_chunk/pallas_call | solution.py:182
  144.4 10.0 %forward_chunk.25 = (bf16[128,1024]{1,0:T(8,128)(2,1)S(1)}, bf16[1024,1024]{1,0:T(8,128)(2,1)}, bf16[1024,1024]{1,0:T(8,128)(2,1)}, bf16[1024,1024]{1,0:T(8,128)...) custom-call(s32[3]{0:T(128)S(1)} %add_add_fusion.1.meta, ...), custom_call_target="tpu_custom_call", output_to_operand_aliasing={{1}: (11, {}), {2}: (12, {}), {3}: (13, {}), {4}: (14, {}),... | custom-call | flops 2885681152 | bytes 8388608 | tf_op jit(solution)/shard_map/forward_chunk/pallas_call | solution.py:182
  156.7 11.4 %forward_chunk.27 = (bf16[128,1024]{1,0:T(8,128)(2,1)}, bf16[1024,1024]{1,0:T(8,128)(2,1)}, bf16[1024,1024]{1,0:T(8,128)(2,1)}, bf16[1024,1024]{1,0:T(8,128)(2,1...) custom-call(s32[3]{0:T(128)S(1)} %add_add_fusion.meta, ...), custom_call_target="tpu_custom_call", output_to_operand_aliasing={{1}: (11, {}), {2}: (12, {}), {3}: (13, {}), {4}: (14, {}),... | custom-call | flops 2885681152 | bytes 8388608 | tf_op jit(solution)/shard_map/forward_chunk/pallas_call | solution.py:182
  168.2 7.7 %backward_chunk.10 = (bf16[256,1024]{1,0:T(8,128)(2,1)S(1)}, bf16[1024,1024]{1,0:T(8,128)(2,1)}, bf16[1024,4096]{1,0:T(8,128)(2,1)}, bf16[1024,1024]{1,0:T(8,128...) custom-call(s32[3]{0:T(128)S(1)} %get-tuple-element.651.meta, ...), custom_call_target="tpu_custom_call", output_to_operand_aliasing={{1}: (19, {}), {2}: (20, {}), {3}: (21, {}), {4}: (22, {}),... | custom-call | flops 6308233216 | bytes 8388608 | tf_op jit(solution)/shard_map/backward_chunk/pallas_call | solution.py:362
  176.6 8.1 %backward_chunk.11 = (bf16[256,1024]{1,0:T(8,128)(2,1)S(1)}, bf16[1024,1024]{1,0:T(8,128)(2,1)}, bf16[1024,4096]{1,0:T(8,128)(2,1)}, bf16[1024,1024]{1,0:T(8,128...) custom-call(s32[3]{0:T(128)S(1)} %get-tuple-element.650.meta, ...), custom_call_target="tpu_custom_call", output_to_operand_aliasing={{1}: (19, {}), {2}: (20, {}), {3}: (21, {}), {4}: (22, {}),... | custom-call | flops 6308233216 | bytes 8388608 | tf_op jit(solution)/shard_map/backward_chunk/pallas_call | solution.py:362
  185.4 7.8 %backward_chunk.12 = (bf16[256,1024]{1,0:T(8,128)(2,1)S(1)}, bf16[1024,1024]{1,0:T(8,128)(2,1)}, bf16[1024,4096]{1,0:T(8,128)(2,1)}, bf16[1024,1024]{1,0:T(8,128...) custom-call(s32[3]{0:T(128)S(1)} %add_add_fusion.20.meta, ...), custom_call_target="tpu_custom_call", output_to_operand_aliasing={{1}: (19, {}), {2}: (20, {}), {3}: (21, {}), {4}: (22, {}),... | custom-call | flops 6308233216 | bytes 8388608 | tf_op jit(solution)/shard_map/backward_chunk/pallas_call | solution.py:362
  193.9 8.0 %backward_chunk.13 = (bf16[256,1024]{1,0:T(8,128)(2,1)S(1)}, bf16[1024,1024]{1,0:T(8,128)(2,1)}, bf16[1024,4096]{1,0:T(8,128)(2,1)}, bf16[1024,1024]{1,0:T(8,128...) custom-call(s32[3]{0:T(128)S(1)} %add_add_fusion.17.meta, ...), custom_call_target="tpu_custom_call", output_to_operand_aliasing={{1}: (19, {}), {2}: (20, {}), {3}: (21, {}), {4}: (22, {}),... | custom-call | flops 6308233216 | bytes 8388608 | tf_op jit(solution)/shard_map/backward_chunk/pallas_call | solution.py:362
  202.7 7.8 %backward_chunk.14 = (bf16[256,1024]{1,0:T(8,128)(2,1)S(1)}, bf16[1024,1024]{1,0:T(8,128)(2,1)}, bf16[1024,4096]{1,0:T(8,128)(2,1)}, bf16[1024,1024]{1,0:T(8,128...) custom-call(s32[3]{0:T(128)S(1)} %add_add_fusion.21.meta, ...), custom_call_target="tpu_custom_call", output_to_operand_aliasing={{1}: (19, {}), {2}: (20, {}), {3}: (21, {}), {4}: (22, {}),... | custom-call | flops 6308233216 | bytes 8388608 | tf_op jit(solution)/shard_map/backward_chunk/pallas_call | solution.py:362
  211.8 7.4 %backward_chunk.15 = (bf16[256,1024]{1,0:T(8,128)(2,1)S(1)}, bf16[1024,1024]{1,0:T(8,128)(2,1)}, bf16[1024,4096]{1,0:T(8,128)(2,1)}, bf16[1024,1024]{1,0:T(8,128...) custom-call(s32[3]{0:T(128)S(1)} %add_add_fusion.16.meta, ...), custom_call_target="tpu_custom_call", output_to_operand_aliasing={{1}: (19, {}), {2}: (20, {}), {3}: (21, {}), {4}: (22, {}),... | custom-call | flops 6308233216 | bytes 8388608 | tf_op jit(solution)/shard_map/backward_chunk/pallas_call | solution.py:362
  220.6 48.0 %collective-permute-done.17.incoming = bf16[256,1024]{1,0:T(8,128)(2,1)S(1)} collective-permute-done((bf16[256,1024]{1,0:T(8,128)(2,1)S(1)}, bf16[256,1024]{1,0:T(8,128)(2,1)S(1)}, u32[]{:S(2)}, u32[]{:S(2)}) %collective-permute-start.17) | collective-permute-done | bytes 524320 | tf_op jit(solution)/shard_map/ppermute | solution.py:458
  268.6 14.7 %backward_chunk.16 = (bf16[256,1024]{1,0:T(8,128)(2,1)S(1)}, bf16[1024,1024]{1,0:T(8,128)(2,1)}, bf16[1024,4096]{1,0:T(8,128)(2,1)}, bf16[1024,1024]{1,0:T(8,128...) custom-call(s32[3]{0:T(128)S(1)} %add_add_fusion.22.meta, ...), custom_call_target="tpu_custom_call", output_to_operand_aliasing={{1}: (19, {}), {2}: (20, {}), {3}: (21, {}), {4}: (22, {}),... | custom-call | flops 6308233216 | bytes 8388608 | tf_op jit(solution)/shard_map/backward_chunk/pallas_call | solution.py:362
  284.7 13.8 %backward_chunk.17 = (bf16[256,1024]{1,0:T(8,128)(2,1)S(1)}, bf16[1024,1024]{1,0:T(8,128)(2,1)}, bf16[1024,4096]{1,0:T(8,128)(2,1)}, bf16[1024,1024]{1,0:T(8,128...) custom-call(s32[3]{0:T(128)S(1)} %add_add_fusion.15.meta, ...), custom_call_target="tpu_custom_call", output_to_operand_aliasing={{1}: (19, {}), {2}: (20, {}), {3}: (21, {}), {4}: (22, {}),... | custom-call | flops 6308233216 | bytes 8388608 | tf_op jit(solution)/shard_map/backward_chunk/pallas_call | solution.py:362
  300.7 15.8 %backward_chunk.18 = (bf16[256,1024]{1,0:T(8,128)(2,1)}, bf16[1024,1024]{1,0:T(8,128)(2,1)}, bf16[1024,4096]{1,0:T(8,128)(2,1)}, bf16[1024,1024]{1,0:T(8,128)(2,...) custom-call(s32[3]{0:T(128)S(1)} %add_add_fusion.23.meta, ...), custom_call_target="tpu_custom_call", output_to_operand_aliasing={{1}: (19, {}), {2}: (20, {}), {3}: (21, {}), {4}: (22, {}),... | custom-call | flops 6308233216 | bytes 8388608 | tf_op jit(solution)/shard_map/backward_chunk/pallas_call | solution.py:362
  316.5 14.6 %backward_chunk.19 = (bf16[256,1024]{1,0:T(8,128)(2,1)}, bf16[1024,1024]{1,0:T(8,128)(2,1)}, bf16[1024,4096]{1,0:T(8,128)(2,1)}, bf16[1024,1024]{1,0:T(8,128)(2,...) custom-call(s32[3]{0:T(128)S(1)} %add_add_fusion.14.meta, ...), custom_call_target="tpu_custom_call", output_to_operand_aliasing={{1}: (19, {}), {2}: (20, {}), {3}: (21, {}), {4}: (22, {}),... | custom-call | flops 6308233216 | bytes 8388608 | tf_op jit(solution)/shard_map/backward_chunk/pallas_call | solution.py:362
  335.3 6.0 convolution_convert_fusion.2
  341.4 5.3 convolution_convert_fusion.3
  348.3 14.7 %convolution_convert_fusion = bf16[4096,1024]{1,0:T(8,128)(2,1)} fusion(bf16[1024,4096]{1,0:T(8,128)(2,1)} %get-tuple-element.640, bf16[1024,1024]{1,0:T(8,128)(2,1)S(1)} %copy-done.19), kind=kOutput, calls=%fused_computation | convolution fusion | flops 8594128896 | bytes 18874368 | tf_op jit(solution)/shard_map/dot_general | solution.py:422
  364.5 14.5 %convolution_convert_fusion.1 = bf16[1024,4096]{1,0:T(8,128)(2,1)} fusion(bf16[1024,1024]{1,0:T(8,128)(2,1)S(1)} %copy-done.18, bf16[1024,4096]{1,0:T(8,128)(2,1)} %get-tuple-element.639), kind=kOutput, calls=%fused_computation.1 | convolution fusion | flops 8594128896 | bytes 18874368 | tf_op jit(solution)/shard_map/dot_general | solution.py:422
  381.0 13.6 %all-reduce.2 = (bf16[1024]{0:T(1024)(128)(2,1)S(1)}, bf16[1024]{0:T(1024)(128)(2,1)S(1)}) all-reduce(bf16[1024]{0:T(1024)(128)(2,1)S(1)} %get-tuple-element.643, bf16[1024]{0:T(1024)(128)(2,1)S(1)} %get-tuple-element.642), channel_id=2, replica_groups=mesh['section'=4,'dp'=8] {'dp'}, use_global_device_ids=true, to_apply=%region_4.5.clone | all-reduce | flops 2048 | bytes 8192
  398.6 30.8 %reduce-scatter.13.cloned.1.call-done = bf16[128,1024]{1,0:T(8,128)(2,1)} async-done(((bf16[1024,1024]{1,0:T(8,128)(2,1)}), bf16[128,1024]{1,0:T(8,128)(2,1)}) %reduce-scatter.13.cloned.1.call-update) | async-done | bytes 262160 | tf_op jit(solution)/shard_map/reduce_scatter | solution.py:518
  431.2 35.4 %reduce-scatter.7.cloned.1.call-done = bf16[128,1024]{1,0:T(8,128)(2,1)} async-done(((bf16[1024,1024]{1,0:T(8,128)(2,1)}), bf16[128,1024]{1,0:T(8,128)(2,1)}) %reduce-scatter.7.cloned.1.call-update) | async-done | bytes 262160 | tf_op jit(solution)/shard_map/reduce_scatter | solution.py:518
  468.4 88.6 %reduce-scatter.17.cloned.1.call-done = bf16[512,1024]{1,0:T(8,128)(2,1)} async-done(((bf16[4096,1024]{1,0:T(8,128)(2,1)}), bf16[512,1024]{1,0:T(8,128)(2,1)}) %reduce-scatter.17.cloned.1.call-update) | async-done | bytes 1048592 | tf_op jit(solution)/shard_map/reduce_scatter | solution.py:518
  559.9 87.3 %reduce-scatter.15.cloned.1.call-done = bf16[128,4096]{1,0:T(8,128)(2,1)} async-done(((bf16[1024,4096]{1,0:T(8,128)(2,1)}), bf16[128,4096]{1,0:T(8,128)(2,1)}) %reduce-scatter.15.cloned.1.call-update) | async-done | bytes 1048592 | tf_op jit(solution)/shard_map/reduce_scatter | solution.py:518
  (157 shorter events, 71.8 us)
Async XLA Ops:
  7.2 388.6 %reduce-scatter.11.cloned.1.call-start = ((), (), s32[]{:S(2)}) async-start(), calls=%async_computation.8 | async-start | bytes 294912 | tf_op jit(solution)/shard_map/reduce_scatter | solution.py:518
  31.0 17.9 %collective-permute-start.1 = (bf16[128,1024]{1,0:T(8,128)(2,1)}, bf16[128,1024]{1,0:T(8,128)(2,1)}, u32[]{:S(2)}, u32[]{:S(2)}) collective-permute-start(bf16[128,1024]{1,0:T(8,128)(2,1)} %get-tuple-element.355), channel_id=1, source_target_pairs={{0,8},{1,9},{2,10},{3,11},{4,12},{5,13},{6,14},{7,15}} | collective-permute-start | bytes 786440 | tf_op jit(solution)/shard_map/ppermute | solution.py:458
  33.1 15.9 %copy-start.13 = (bf16[1,1024]{1,0:T(2,128)(2,1)S(1)}, bf16[1,1024]{1,0:T(2,128)(2,1)}, u32[]{:S(2)}) copy-start(bf16[1,1024]{1,0:T(2,128)(2,1)} %gain_attn.47) | copy-start | bytes 6148
  33.1 15.9 %copy-start.15 = (bf16[1,1024]{1,0:T(2,128)(2,1)S(1)}, bf16[1,1024]{1,0:T(2,128)(2,1)}, u32[]{:S(2)}) copy-start(bf16[1,1024]{1,0:T(2,128)(2,1)} %gain_ffn.47) | copy-start | bytes 6148
  45.8 22.9 %collective-permute-start = (bf16[128,1024]{1,0:T(8,128)(2,1)}, bf16[128,1024]{1,0:T(8,128)(2,1)S(1)}, u32[]{:S(2)}, u32[]{:S(2)}) collective-permute-start(bf16[128,1024]{1,0:T(8,128)(2,1)} %get-tuple-element.354), channel_id=1, source_target_pairs={{0,8},{1,9},{2,10},{3,11},{4,12},{5,13},{6,14},{7,15}} | collective-permute-start | bytes 786440 | tf_op jit(solution)/shard_map/ppermute | solution.py:458
  67.4 13.3 %collective-permute-start.3 = (bf16[128,1024]{1,0:T(8,128)(2,1)S(1)}, bf16[128,1024]{1,0:T(8,128)(2,1)S(1)}, u32[]{:S(2)}, u32[]{:S(2)}) collective-permute-start(bf16[128,1024]{1,0:T(8,128)(2,1)S(1)} %get-tuple-element.385), channel_id=1, source_target_pairs={{0,8},{8,16},{1,9},{9,17},{2,10},{10,18},{3,11},{11,19},{4,12},{12... | collective-permute-start | bytes 786440 | tf_op jit(solution)/shard_map/ppermute | solution.py:458
  79.3 11.1 %collective-permute-start.2 = (bf16[128,1024]{1,0:T(8,128)(2,1)S(1)}, bf16[128,1024]{1,0:T(8,128)(2,1)S(1)}, u32[]{:S(2)}, u32[]{:S(2)}) collective-permute-start(bf16[128,1024]{1,0:T(8,128)(2,1)S(1)} %get-tuple-element.384), channel_id=1, source_target_pairs={{0,8},{8,16},{1,9},{9,17},{2,10},{10,18},{3,11},{11,19},{4,12},{12... | collective-permute-start | bytes 786440 | tf_op jit(solution)/shard_map/ppermute | solution.py:458
  89.1 14.2 %collective-permute-start.5 = (bf16[128,1024]{1,0:T(8,128)(2,1)S(1)}, bf16[128,1024]{1,0:T(8,128)(2,1)S(1)}, u32[]{:S(2)}, u32[]{:S(2)}) collective-permute-start(bf16[128,1024]{1,0:T(8,128)(2,1)S(1)} %get-tuple-element.415), channel_id=1, source_target_pairs={{0,8},{8,16},{16,24},{1,9},{9,17},{17,25},{2,10},{10,18},{18,26},{... | collective-permute-start | bytes 786440 | tf_op jit(solution)/shard_map/ppermute | solution.py:458
  102.0 12.7 %collective-permute-start.4 = (bf16[128,1024]{1,0:T(8,128)(2,1)S(1)}, bf16[128,1024]{1,0:T(8,128)(2,1)S(1)}, u32[]{:S(2)}, u32[]{:S(2)}) collective-permute-start(bf16[128,1024]{1,0:T(8,128)(2,1)S(1)} %get-tuple-element.414), channel_id=1, source_target_pairs={{0,8},{8,16},{16,24},{1,9},{9,17},{17,25},{2,10},{10,18},{18,26},{... | collective-permute-start | bytes 786440 | tf_op jit(solution)/shard_map/ppermute | solution.py:458
  113.5 13.3 %collective-permute-start.7 = (bf16[128,1024]{1,0:T(8,128)(2,1)S(1)}, bf16[128,1024]{1,0:T(8,128)(2,1)S(1)}, u32[]{:S(2)}, u32[]{:S(2)}) collective-permute-start(bf16[128,1024]{1,0:T(8,128)(2,1)S(1)} %get-tuple-element.445), channel_id=1, source_target_pairs={{0,8},{8,16},{16,24},{1,9},{9,17},{17,25},{2,10},{10,18},{18,26},{... | collective-permute-start | bytes 786440 | tf_op jit(solution)/shard_map/ppermute | solution.py:458
  125.4 7.7 %collective-permute-start.6 = (bf16[128,1024]{1,0:T(8,128)(2,1)S(1)}, bf16[128,1024]{1,0:T(8,128)(2,1)S(1)}, u32[]{:S(2)}, u32[]{:S(2)}) collective-permute-start(bf16[128,1024]{1,0:T(8,128)(2,1)S(1)} %get-tuple-element.444), channel_id=1, source_target_pairs={{0,8},{8,16},{16,24},{1,9},{9,17},{17,25},{2,10},{10,18},{18,26},{... | collective-permute-start | bytes 786440 | tf_op jit(solution)/shard_map/ppermute | solution.py:458
  127.5 15.4 %collective-permute-start.9 = (bf16[128,1024]{1,0:T(8,128)(2,1)S(1)}, bf16[128,1024]{1,0:T(8,128)(2,1)S(1)}, u32[]{:S(2)}, u32[]{:S(2)}) collective-permute-start(bf16[128,1024]{1,0:T(8,128)(2,1)S(1)} %get-tuple-element.475), channel_id=1, source_target_pairs={{8,16},{16,24},{9,17},{17,25},{10,18},{18,26},{11,19},{19,27},{12,... | collective-permute-start | bytes 786440 | tf_op jit(solution)/shard_map/ppermute | solution.py:458
  142.2 2.1 collective-permute-start.8
  143.7 11.4 %collective-permute-start.11 = (bf16[128,1024]{1,0:T(8,128)(2,1)S(1)}, bf16[128,1024]{1,0:T(8,128)(2,1)S(1)}, u32[]{:S(2)}, u32[]{:S(2)}) collective-permute-start(bf16[128,1024]{1,0:T(8,128)(2,1)S(1)} %get-tuple-element.505), channel_id=1, source_target_pairs={{16,24},{17,25},{18,26},{19,27},{20,28},{21,29},{22,30},{23,31}} | collective-permute-start | bytes 786440 | tf_op jit(solution)/shard_map/ppermute | solution.py:458
  154.4 2.2 collective-permute-start.10
  156.6 11.6 %slice-start = ((s8[8388608]{0:T(1024)(128)(4,1)}), s8[4194304]{0:T(1024)(128)(4,1)S(1)}, s32[]{:S(2)}) async-start(s8[8388608]{0:T(1024)(128)(4,1)} %bitcast.115), calls=%async_computation.12 | async-start | bytes 8388608
  156.6 11.6 %slice-start.2 = ((s8[8388608]{0:T(1024)(128)(4,1)}), s8[4194304]{0:T(1024)(128)(4,1)S(1)}, s32[]{:S(2)}) async-start(s8[8388608]{0:T(1024)(128)(4,1)} %bitcast.141), calls=%async_computation.14 | async-start | bytes 8388608
  156.6 11.5 %slice-start.1 = ((s8[8388608]{0:T(1024)(128)(4,1)}), s8[4194304]{0:T(1024)(128)(4,1)S(1)}, s32[]{:S(2)}) async-start(s8[8388608]{0:T(1024)(128)(4,1)} %bitcast.115), calls=%async_computation.13 | async-start | bytes 8388608
  175.9 9.5 %collective-permute-start.13 = (bf16[256,1024]{1,0:T(8,128)(2,1)S(1)}, bf16[256,1024]{1,0:T(8,128)(2,1)S(1)}, u32[]{:S(2)}, u32[]{:S(2)}) collective-permute-start(bf16[256,1024]{1,0:T(8,128)(2,1)S(1)} %get-tuple-element.560), channel_id=1, source_target_pairs={{24,16},{25,17},{26,18},{27,19},{28,20},{29,21},{30,22},{31,23}} | collective-permute-start | bytes 1572872 | tf_op jit(solution)/shard_map/ppermute | solution.py:458
  184.7 9.2 %collective-permute-start.12 = (bf16[256,1024]{1,0:T(8,128)(2,1)S(1)}, bf16[256,1024]{1,0:T(8,128)(2,1)S(1)}, u32[]{:S(2)}, u32[]{:S(2)}) collective-permute-start(bf16[256,1024]{1,0:T(8,128)(2,1)S(1)} %get-tuple-element.559), channel_id=1, source_target_pairs={{24,16},{25,17},{26,18},{27,19},{28,20},{29,21},{30,22},{31,23}} | collective-permute-start | bytes 1572872 | tf_op jit(solution)/shard_map/ppermute | solution.py:458
  193.2 9.5 %collective-permute-start.15 = (bf16[256,1024]{1,0:T(8,128)(2,1)S(1)}, bf16[256,1024]{1,0:T(8,128)(2,1)S(1)}, u32[]{:S(2)}, u32[]{:S(2)}) collective-permute-start(bf16[256,1024]{1,0:T(8,128)(2,1)S(1)} %get-tuple-element.578), channel_id=1, source_target_pairs={{16,8},{24,16},{17,9},{25,17},{18,10},{26,18},{19,11},{27,19},{20,... | collective-permute-start | bytes 1572872 | tf_op jit(solution)/shard_map/ppermute | solution.py:458
  202.0 9.8 %collective-permute-start.14 = (bf16[256,1024]{1,0:T(8,128)(2,1)S(1)}, bf16[256,1024]{1,0:T(8,128)(2,1)S(1)}, u32[]{:S(2)}, u32[]{:S(2)}) collective-permute-start(bf16[256,1024]{1,0:T(8,128)(2,1)S(1)} %get-tuple-element.577), channel_id=1, source_target_pairs={{16,8},{24,16},{17,9},{25,17},{18,10},{26,18},{19,11},{27,19},{20,... | collective-permute-start | bytes 1572872 | tf_op jit(solution)/shard_map/ppermute | solution.py:458
  210.5 58.1 %collective-permute-start.17 = (bf16[256,1024]{1,0:T(8,128)(2,1)S(1)}, bf16[256,1024]{1,0:T(8,128)(2,1)S(1)}, u32[]{:S(2)}, u32[]{:S(2)}) collective-permute-start(bf16[256,1024]{1,0:T(8,128)(2,1)S(1)} %get-tuple-element.596), channel_id=1, source_target_pairs={{8,0},{16,8},{9,1},{17,9},{10,2},{18,10},{11,3},{19,11},{12,4},{20... | collective-permute-start | bytes 1572872 | tf_op jit(solution)/shard_map/ppermute | solution.py:458
  219.3 65.4 %collective-permute-start.16 = (bf16[256,1024]{1,0:T(8,128)(2,1)S(1)}, bf16[256,1024]{1,0:T(8,128)(2,1)S(1)}, u32[]{:S(2)}, u32[]{:S(2)}) collective-permute-start(bf16[256,1024]{1,0:T(8,128)(2,1)S(1)} %get-tuple-element.595), channel_id=1, source_target_pairs={{8,0},{16,8},{9,1},{17,9},{10,2},{18,10},{11,3},{19,11},{12,4},{20... | collective-permute-start | bytes 1572872 | tf_op jit(solution)/shard_map/ppermute | solution.py:458
  283.3 17.3 %collective-permute-start.19 = (bf16[256,1024]{1,0:T(8,128)(2,1)S(1)}, bf16[256,1024]{1,0:T(8,128)(2,1)S(1)}, u32[]{:S(2)}, u32[]{:S(2)}) collective-permute-start(bf16[256,1024]{1,0:T(8,128)(2,1)S(1)} %get-tuple-element.614), channel_id=1, source_target_pairs={{8,0},{9,1},{10,2},{11,3},{12,4},{13,5},{14,6},{15,7}} | collective-permute-start | bytes 1572872 | tf_op jit(solution)/shard_map/ppermute | solution.py:458
  298.5 18.0 %collective-permute-start.18 = (bf16[256,1024]{1,0:T(8,128)(2,1)S(1)}, bf16[256,1024]{1,0:T(8,128)(2,1)S(1)}, u32[]{:S(2)}, u32[]{:S(2)}) collective-permute-start(bf16[256,1024]{1,0:T(8,128)(2,1)S(1)} %get-tuple-element.613), channel_id=1, source_target_pairs={{8,0},{9,1},{10,2},{11,3},{12,4},{13,5},{14,6},{15,7}} | collective-permute-start | bytes 1572872 | tf_op jit(solution)/shard_map/ppermute | solution.py:458
  316.5 14.6 %copy-start.16 = (bf16[1024,1024]{1,0:T(8,128)(2,1)S(1)}, bf16[1024,1024]{1,0:T(8,128)(2,1)}, u32[]{:S(2)}) copy-start(bf16[1024,1024]{1,0:T(8,128)(2,1)} %get-tuple-element.633) | copy-start | bytes 6291460
  333.7 63.5 %reduce-scatter.9.cloned.1.call-start = ((), (), s32[]{:S(2)}) async-start(), calls=%async_computation.7 | async-start | bytes 294912 | tf_op jit(solution)/shard_map/reduce_scatter | solution.py:518
  335.3 94.1 %reduce-scatter.13.cloned.1.call-start = ((), (), s32[]{:S(2)}) async-start(), calls=%async_computation.9 | async-start | bytes 2359296 | tf_op jit(solution)/shard_map/reduce_scatter | solution.py:518
  341.3 125.3 %reduce-scatter.7.cloned.1.call-start = ((), (), s32[]{:S(2)}) async-start(), calls=%async_computation.6 | async-start | bytes 2359296 | tf_op jit(solution)/shard_map/reduce_scatter | solution.py:518
  346.7 210.4 %reduce-scatter.17.cloned.1.call-start = ((), (), s32[]{:S(2)}) async-start(), calls=%async_computation.11 | async-start | bytes 9437184 | tf_op jit(solution)/shard_map/reduce_scatter | solution.py:518
  363.0 284.2 %reduce-scatter.15.cloned.1.call-start = ((), (), s32[]{:S(2)}) async-start(), calls=%async_computation.10 | async-start | bytes 9437184 | tf_op jit(solution)/shard_map/reduce_scatter | solution.py:518
  (21 other events, 99.5 us)
Sparse Core Ops, SparseCore 0:
  333.8 27.2 reduce-scatter.10
  364.0 28.4 reduce-scatter.8
  395.4 33.9 reduce-scatter.12
  432.1 34.4 reduce-scatter.6
  468.8 88.2 reduce-scatter.16
  559.2 87.9 reduce-scatter.14

commit v2 on v1

--- a/solution.py
+++ b/solution.py
@@ -14,6 +14,9 @@
 BWD_ROWS = 256
 FFN_TILE = 1024
 SKEW = 2
+FWD_HEADS = 4
+BWD_HEADS = 2
+SIDE_TILE = 512
 MIB = 1 << 20
 
 BF16 = jnp.bfloat16
@@ -62,7 +65,7 @@
     rows, row_len, heads, size = geometry
     saved = refs[len(FWD_SAVED):2 * len(FWD_SAVED) + 1]
     out, hs, n1s, qs, ks, vs, kts, vts, os_, mids, n2s, acts, slopes, lses, outs = saved
-    (h_v, n1_v, q_v, k_v, v_v, kt_v, vt_v, o_v, mid_v, n2_v, act_v, slope_v, lse_v, out_v, bias_v, sems) = (
+    (h_v, n1_v, q_v, k_v, v_v, kt_v, vt_v, o_v, mid_v, n2_v, act_v, slope_v, lse_v, out_v, bias_v, total_v, sems) = (
         refs[2 * len(FWD_SAVED) + 1:]
     )
     parts = row_len // rows
@@ -82,10 +85,6 @@
         def _():
             pltpu.make_async_copy(tokens.at[at], h_v, sems.at[0]).start()
 
-        @pl.when(first == 0)
-        def _():
-            pltpu.make_async_copy(incoming, h_v, sems.at[0]).start()
-
         load_v = pltpu.make_async_copy(vs.at[whole], v_v, sems.at[1])
         load_kt = pltpu.make_async_copy(kts.at[row], kt_v, sems.at[2])
         load_v.start()
@@ -98,12 +97,16 @@
             pending.append(copy)
 
         start_col = starts[at, :]
-        for step in range(parts):
-            @pl.when(place == step)
-            def _():
-                bias_v[:, : (step + 1) * rows] = position_bias(start_col, step * rows, rows, (step + 1) * rows)
-
-        pltpu.make_async_copy(incoming, h_v, sems.at[0]).wait()
+        bias_v[...] = position_bias(start_col, place * rows, rows, row_len)
+
+        @pl.when(first == 1)
+        def _():
+            pltpu.make_async_copy(tokens.at[at], h_v, sems.at[0]).wait()
+
+        @pl.when(first == 0)
+        def _():
+            h_v[...] = incoming[...]
+
         h = h_v[...].astype(F32)
         n1 = (h * inverse_rms(h) * gain_attn[...].astype(F32)).astype(BF16)
         n1_v[...] = n1
@@ -116,6 +119,9 @@
         keep(q_v, qs.at[at], 6)
         load_v.wait()
         load_kt.wait()
+        known = place * rows
+        v_v[...] = jnp.where(lax.broadcasted_iota(jnp.int32, v_v.shape, 0) < known, v_v[...], 0.0).astype(BF16)
+        kt_v[...] = jnp.where(lax.broadcasted_iota(jnp.int32, kt_v.shape, 1) < known, kt_v[...], 0.0).astype(BF16)
         v_v[within, :] = kv[:, size:]
         kt_v[:, within] = kv[:, :size].T
         vt_v[...] = kv[:, size:].T
@@ -123,22 +129,30 @@
         keep(kt_v.at[:, within], kts.at[row, :, within], 8)
         keep(vt_v, vts.at[row, :, within], 9)
 
+        lse_v[...] = jnp.zeros((rows, size), F32)
+
         def attend(length):
             lane = lax.broadcasted_iota(jnp.int32, (rows, size), 1)
-            stats = jnp.zeros((rows, size), F32)
-            for head in range(heads):
-                cols = slice(head * size, (head + 1) * size)
-                scores = dot(q_v[:, cols], kt_v[:, :length]) * scale + bias_v[:, :length]
-                top = jnp.max(scores, axis=1, keepdims=True)
-                weights = jnp.exp2(scores - top)
-                total = jnp.sum(weights, axis=1, keepdims=True)
-                mixed = dot(weights.astype(BF16), v_v[:length, :]) * (1.0 / total)
-                o_v[:, cols] = mixed.astype(BF16)
-                stats = jnp.where(lane == head, top + jnp.log2(total), stats)
-            lse_v[...] = stats
-
-        for step in range(parts):
-            pl.when(place == step)(functools.partial(attend, (step + 1) * rows))
+
+            def some_heads(step, carry):
+                for head in [step * FWD_HEADS + i for i in range(FWD_HEADS)]:
+                    cols = pl.ds(pl.multiple_of(head * size, size), size)
+                    scores = dot(q_v[:, cols], kt_v[:, :length]) * scale + bias_v[:, :length]
+                    top = jnp.max(scores, axis=1, keepdims=True)
+                    weights = jnp.exp2(scores - top)
+                    total = jnp.sum(weights, axis=1, keepdims=True)
+                    mixed = dot(weights.astype(BF16), v_v[:length, :]) * (1.0 / total)
+                    o_v[:, cols] = mixed.astype(BF16)
+                    lse_v[...] = jnp.where(lane == head, top + jnp.log2(total), lse_v[...])
+                return carry
+
+            lax.fori_loop(0, heads // FWD_HEADS, some_heads, 0)
+
+        cases = [row_len // 2, row_len] if parts > 2 else [rows * (i + 1) for i in range(parts)]
+        low = 0
+        for length in cases:
+            pl.when((place >= low) & (place < length // rows))(functools.partial(attend, length))
+            low = length // rows
 
         keep(lse_v, lses.at[at], 10)
         keep(o_v, os_.at[at], 11)
@@ -150,16 +164,38 @@
         keep(n2_v, n2s.at[at], 13)
         ffn = w_up.shape[1]
         tile = min(FFN_TILE, ffn)
-        total = mid
-        for f in range(ffn // tile):
-            cols = slice(f * tile, (f + 1) * tile)
-            act, slope = gelu_parts(dot(n2, w_up[:, cols]))
-            act = act.astype(BF16)
-            act_v[:, cols] = act
-            slope_v[:, cols] = slope.astype(BF16)
-            total = total + dot(act, w_down[cols, :])
-        keep(act_v, acts.at[at], 14)
-        keep(slope_v, slopes.at[at], 15)
+        total_v[...] = mid
+
+
+        def columns(f):
+            return pl.ds(pl.multiple_of(f * tile, tile), tile)
+
+        def rise(f):
+            return dot(n2_v[...], w_up[:, columns(f)])
+
+        def bend(f, u):
+            act, slope = gelu_parts(u)
+            act_v[:, columns(f)] = act.astype(BF16)
+            slope_v[:, columns(f)] = slope.astype(BF16)
+            pltpu.make_async_copy(act_v.at[:, columns(f)], acts.at[at, columns(f)], sems.at[14]).start()
+            pltpu.make_async_copy(slope_v.at[:, columns(f)], slopes.at[at, columns(f)], sems.at[15]).start()
+
+        def fall(f):
+            return dot(act_v[:, columns(f)], w_down[columns(f), :])
+
+        def both(f, carry):
+            u = rise(f)
+            part = fall(f - 1)
+            bend(f, u)
+            total_v[...] += part
+            return carry
+
+        bend(0, rise(0))
+        lax.fori_loop(1, ffn // tile, both, 0)
+        total_v[...] += fall(ffn // tile - 1)
+        total = total_v[...]
+        pending.append(pltpu.make_async_copy(act_v, acts.at[at], sems.at[14]))
+        pending.append(pltpu.make_async_copy(slope_v, slopes.at[at], sems.at[15]))
         result = total.astype(BF16)
         out[...] = result
         out_v[...] = result
@@ -183,7 +219,7 @@
         functools.partial(forward_kernel, geometry),
         out_shape=[jax.ShapeDtypeStruct((rows, width), BF16)]
         + [pltpu.HBM(array.shape, array.dtype) for array in saved],
-        in_specs=[pl.BlockSpec(memory_space=pltpu.SMEM), vmem, anywhere, anywhere]
+        in_specs=[pl.BlockSpec(memory_space=pltpu.SMEM), vmem, anywhere, vmem]
         + [vmem] * len(weights) + [anywhere] * len(saved),
         out_specs=[vmem] + [anywhere] * len(saved),
         input_output_aliases={4 + len(weights) + i: 1 + i for i in range(len(saved))},
@@ -203,15 +239,16 @@
             pltpu.VMEM((rows, size), F32),
             pltpu.VMEM((rows, width), BF16),
             pltpu.VMEM((rows, row_len), F32),
+            pltpu.VMEM((rows, width), F32),
             pltpu.SemaphoreType.DMA((17,)),
         ],
-        compiler_params=pltpu.CompilerParams(vmem_limit_bytes=16 * MIB),
+        compiler_params=pltpu.CompilerParams(vmem_limit_bytes=12 * MIB),
         cost_estimate=pl.CostEstimate(flops=flops, bytes_accessed=8 * MIB, transcendentals=0),
         name="forward_chunk",
-    )(meta, starts, in_hbm(tokens), incoming, *map(in_vmem, weights), *saved)
-
-
-BWD_SAVED = ("gbs", "dus", "gms", "dqs", "dkvs", "igs", "gains", "carry")
+    )(meta, starts, in_hbm(tokens), in_vmem(incoming), *map(in_vmem, weights), *saved)
+
+
+BWD_SAVED = ("gbs", "dus", "gms", "dqkvs", "igs", "gains", "carry")
 
 
 def norm_backward(rows, gain, upstream):
@@ -223,17 +260,19 @@
 
 
 def backward_kernel(
-    geometry, meta, starts, cotangent, incoming, hs, qs, ks, kts, vts, mids, slopes, lses,
+    geometry, last_call, gates, meta, starts, cotangent, incoming, hs, qs, ks, kts, vts, mids, slopes, lses,
     gain_attn, w_query, w_kv, w_out, gain_ffn, w_up, w_down, *refs,
 ):
     rows, row_len, heads, size = geometry
-    count = len(BWD_SAVED)
-    out, gbs, dus, gms, dqs, dkvs, igs, gains, carry = refs[count:2 * count + 1]
-    (g_v, h_v, q_v, k_v, kt_v, vt_v, mid_v, slope_v, lse_v, du_v, gm_v, do_v, dq_v, dkv_v, ig_v, gain_v, carry_v,
-     bias_v, p_v, ds_v, qt_v, dot_v, sems) = refs[2 * count + 1:]
+    refs = refs[gates:]
+    count = len(BWD_SAVED) - last_call
+    out, *gbs, dus, gms, dqkvs, igs, gains, carry = refs[count:2 * count + 1]
+    (g_v, h_v, q_v, k_v, kt_v, vt_v, mid_v, slope_v, lse_v, du_v, gm_v, do_v, dqkv_v, ig_v, gain_v, carry_v,
+     bias_v, total_v, sems) = refs[2 * count + 1:]
     parts = row_len // rows
     active, chunk, first = meta[0], meta[1], meta[2]
     scale = size**-0.5
+    width = heads * size
 
     @pl.when(active == 1)
     def _():
@@ -275,24 +314,33 @@
             pending.append(copy)
 
         start_col = starts[at, :]
-        for step in range(parts):
-            @pl.when(place == step)
-            def _():
-                bias_v[:, : (step + 1) * rows] = position_bias(start_col, step * rows, rows, (step + 1) * rows)
-
+        bias_v[...] = position_bias(start_col, place * rows, rows, row_len)
         pltpu.make_async_copy(incoming, g_v, sems.at[0]).wait()
         g = g_v[...]
-        keep(g_v, gbs.at[at], 10)
+        if not last_call:
+            keep(g_v, gbs[0].at[at], 10)
         loads[0].wait()
         ffn = w_up.shape[1]
         tile = min(FFN_TILE, ffn)
-        dn2 = None
-        for f in range(ffn // tile):
-            cols = slice(f * tile, (f + 1) * tile)
-            du = (slope_v[:, cols].astype(F32) * dot_t(g, w_down[cols, :])).astype(BF16)
-            du_v[:, cols] = du
-            part = dot_t(du, w_up[:, cols])
-            dn2 = part if dn2 is None else dn2 + part
+
+        def rise(f):
+            cols = pl.ds(pl.multiple_of(f * tile, tile), tile)
+            du = slope_v[:, cols].astype(F32) * dot_t(g_v[...], w_down[cols, :])
+            du_v[:, cols] = du.astype(BF16)
+
+        def fall(f):
+            cols = pl.ds(pl.multiple_of(f * tile, tile), tile)
+            return dot_t(du_v[:, cols], w_up[:, cols])
+
+        def both(f, carry):
+            part = fall(f - 1)
+            total_v[...] = jnp.where(f == 1, part, total_v[...] + part)
+            rise(f)
+            return carry
+
+        rise(0)
+        lax.fori_loop(1, ffn // tile, both, 0)
+        dn2 = total_v[...] + fall(ffn // tile - 1)
         keep(du_v, dus.at[at], 11)
         loads[1].wait()
         dv, dgain_ffn = norm_backward(mid_v[...], gain_ffn[...].astype(F32), dn2)
@@ -305,40 +353,39 @@
         for load in loads[2:8]:
             load.wait()
 
-        def attend(length, last):
-            for head in range(heads):
-                cols = slice(head * size, (head + 1) * size)
-                span = slice(head * rows, (head + 1) * rows)
-                q_h = q_v[:, cols]
-                do_h = do_v[:, cols]
-                qt_v[:, span] = q_h.T
-                dot_v[:, span] = do_h.T
-                scores = dot(q_h, kt_v[:, :length]) * (scale * LOG2E) + bias_v[:, :length]
-                probs = jnp.exp2(scores - lse_v[:, head:head + 1])
-                p_v[span, :length] = probs.astype(BF16)
-                dprobs = dot(do_h, vt_v[:, :length])
-                mean = jnp.sum(probs * dprobs, axis=1, keepdims=True)
-                dscores = (probs * (dprobs - mean)).astype(BF16)
-                ds_v[span, :length] = dscores
-                dq_v[:, cols] = (dot(dscores, k_v[:length, :]) * scale).astype(BF16)
-            dkt = dot(qt_v[...], ds_v[:, :length])
-            dvt = dot(dot_v[...], p_v[:, :length])
-            if not last:
-                dkt = dkt + carry_v[:size, :length]
-                dvt = dvt + carry_v[size:, :length]
-            if length > rows:
-                carry_v[:size, :length - rows] = dkt[:, :length - rows]
-                carry_v[size:, :length - rows] = dvt[:, :length - rows]
-            dkv_v[:, :size] = (dkt[:, length - rows:].T * scale).astype(BF16)
-            dkv_v[:, size:] = dvt[:, length - rows:].T.astype(BF16)
+        @pl.when(place == parts - 1)
+        def _():
+            carry_v[...] = jnp.zeros(carry_v.shape, F32)
+
+        def attend(length):
+            def some_heads(step, unused):
+                for head in [step * BWD_HEADS + i for i in range(BWD_HEADS)]:
+                    cols = pl.ds(pl.multiple_of(head * size, size), size)
+                    q_h = q_v[:, cols]
+                    do_h = do_v[:, cols]
+                    lane = lax.broadcasted_iota(jnp.int32, (rows, size), 1)
+                    lse = jnp.sum(jnp.where(lane == head, lse_v[...], 0.0), axis=1, keepdims=True)
+                    scores = dot(q_h, kt_v[:, :length]) * (scale * LOG2E) + bias_v[:, :length]
+                    probs = jnp.exp2(scores - lse)
+                    dprobs = dot(do_h, vt_v[:, :length])
+                    mean = jnp.sum(probs * dprobs, axis=1, keepdims=True)
+                    dscores = (probs * (dprobs - mean)).astype(BF16)
+                    dqkv_v[:, cols] = (dot(dscores, k_v[:length, :]) * scale).astype(BF16)
+                    carry_v[:size, :length] += dot(q_h.T, dscores)
+                    carry_v[size:, :length] += dot(do_h.T, probs.astype(BF16))
+                return unused
+
+            lax.fori_loop(0, heads // BWD_HEADS, some_heads, 0)
+            own = slice(length - rows, length)
+            dqkv_v[:, width:width + size] = (carry_v[:size, own].T * scale).astype(BF16)
+            dqkv_v[:, width + size:] = carry_v[size:, own].T.astype(BF16)
 
         for step in range(parts):
-            pl.when(place == step)(functools.partial(attend, (step + 1) * rows, step == parts - 1))
+            pl.when(place == step)(functools.partial(attend, (step + 1) * rows))
 
         keep(carry_v, carry, 13)
-        keep(dq_v, dqs.at[at], 14)
-        keep(dkv_v, dkvs.at[at], 15)
-        dn1 = dot_t(dq_v[...], w_query[...]) + dot_t(dkv_v[...], w_kv[...])
+        keep(dqkv_v, dqkvs.at[at], 14)
+        dn1 = dot_t(dqkv_v[:, :width], w_query[...]) + dot_t(dqkv_v[:, width:], w_kv[...])
         loads[8].wait()
         dv, dgain_attn = norm_backward(h_v[...].astype(F32), gain_attn[...].astype(F32), dn1)
         result = (mid_v[...] + dv).astype(BF16)
@@ -351,20 +398,21 @@
             copy.wait()
 
 
-def backward_chunk(geometry, meta, starts, cotangent, incoming, kept, weights, saved):
+def backward_chunk(geometry, last_call, meta, starts, cotangent, incoming, kept, weights, saved, gates=()):
     rows, row_len, heads, size = geometry
     width = cotangent.shape[1]
     ffn = weights[5].shape[1]
     vmem = pl.BlockSpec(memory_space=pltpu.VMEM)
     anywhere = pl.BlockSpec(memory_space=pltpu.HBM)
-    lead = 4 + len(kept) + len(weights)
+    lead = 4 + len(kept) + len(weights) + len(gates)
     flops = 2 * rows * (2 * width * heads * size + 2 * width * size + 2 * width * ffn + 3 * row_len * heads * size)
     return pl.pallas_call(
-        functools.partial(backward_kernel, geometry),
+        functools.partial(backward_kernel, geometry, last_call, len(gates)),
         out_shape=[jax.ShapeDtypeStruct((rows, width), BF16)]
         + [pltpu.HBM(array.shape, array.dtype) for array in saved],
         in_specs=[pl.BlockSpec(memory_space=pltpu.SMEM), vmem, anywhere, anywhere]
-        + [anywhere] * len(kept) + [vmem] * len(weights) + [anywhere] * len(saved),
+        + [anywhere] * len(kept) + [vmem] * len(weights) + [pl.BlockSpec(memory_space=pl.ANY)] * len(gates)
+        + [anywhere] * len(saved),
         out_specs=[vmem] + [anywhere] * len(saved),
         input_output_aliases={lead + i: 1 + i for i in range(len(saved))},
         scratch_shapes=[
@@ -380,22 +428,20 @@
             pltpu.VMEM((rows, ffn), BF16),
             pltpu.VMEM((rows, width), BF16),
             pltpu.VMEM((rows, heads * size), BF16),
-            pltpu.VMEM((rows, heads * size), BF16),
-            pltpu.VMEM((rows, 2 * size), BF16),
+            pltpu.VMEM((rows, (heads + 2) * size), BF16),
             pltpu.VMEM((rows, width), BF16),
             pltpu.VMEM((8, width), F32),
             pltpu.VMEM((2 * size, row_len), F32),
             pltpu.VMEM((rows, row_len), F32),
-            pltpu.VMEM((heads * rows, row_len), BF16),
-            pltpu.VMEM((heads * rows, row_len), BF16),
-            pltpu.VMEM((size, heads * rows), BF16),
-            pltpu.VMEM((size, heads * rows), BF16),
+            pltpu.VMEM((rows, width), F32),
             pltpu.SemaphoreType.DMA((18,)),
         ],
-        compiler_params=pltpu.CompilerParams(vmem_limit_bytes=30 * MIB),
-        cost_estimate=pl.CostEstimate(flops=flops, bytes_accessed=8 * MIB, transcendentals=0),
+        compiler_params=pltpu.CompilerParams(vmem_limit_bytes=20 * MIB),
+        cost_estimate=pl.CostEstimate(
+            flops=1024 if last_call else flops, bytes_accessed=1024 if last_call else 8 * MIB, transcendentals=0
+        ),
         name="backward_chunk",
-    )(meta, starts, in_hbm(cotangent), incoming, *map(in_hbm, kept), *map(in_vmem, weights), *saved)
+    )(meta, starts, in_hbm(cotangent), incoming, *map(in_hbm, kept), *map(in_vmem, weights), *gates, *saved)
 
 
 def unwritten(shapes):
@@ -403,8 +449,52 @@
         lambda *refs: None,
         out_shape=shapes,
         out_specs=[pl.BlockSpec(memory_space=pltpu.HBM)] * len(shapes),
+        compiler_params=pltpu.CompilerParams(vmem_limit_bytes=2 * MIB),
         name="unwritten",
     )()
+
+
+def load_kernel(*refs):
+    count = (len(refs) - 1) // 2
+    sources, targets, sems = refs[:count + 1], refs[count + 1:-1], refs[-1]
+    gain_attn, w_query, w_key, w_value, w_out, gain_ffn, w_up, w_down = sources
+    gain_attn_v, w_query_v, w_kv_v, w_out_v, gain_ffn_v, w_up_v, w_down_v = targets
+    size = w_key.shape[1]
+    gain_attn_v[...] = gain_attn[...]
+    gain_ffn_v[...] = gain_ffn[...]
+    copies = [
+        pltpu.make_async_copy(source, target, sems.at[i])
+        for i, (source, target) in enumerate((
+            (w_query, w_query_v),
+            (w_key, w_kv_v.at[:, :size]),
+            (w_value, w_kv_v.at[:, size:]),
+            (w_out, w_out_v),
+            (w_up, w_up_v),
+            (w_down, w_down_v),
+        ))
+    ]
+    for copy in copies:
+        copy.start()
+    for copy in copies:
+        copy.wait()
+
+
+def load_weights(gain_attn, w_query, w_key, w_value, w_out, gain_ffn, w_up, w_down):
+    vmem = pl.BlockSpec(memory_space=pltpu.VMEM)
+    hbm = pl.BlockSpec(memory_space=pltpu.HBM)
+    shapes = [
+        gain_attn.shape, w_query.shape, (w_key.shape[0], w_key.shape[1] + w_value.shape[1]), w_out.shape,
+        gain_ffn.shape, w_up.shape, w_down.shape,
+    ]
+    return pl.pallas_call(
+        load_kernel,
+        out_shape=[pltpu.VMEM(shape, BF16) for shape in shapes],
+        in_specs=[vmem, hbm, hbm, hbm, hbm, vmem, hbm, hbm],
+        out_specs=[vmem] * len(shapes),
+        scratch_shapes=[pltpu.SemaphoreType.DMA((6,))],
+        compiler_params=pltpu.CompilerParams(vmem_limit_bytes=2 * MIB),
+        name="load_weights",
+    )(gain_attn, *map(in_hbm, (w_query, w_key, w_value, w_out)), gain_ffn, *map(in_hbm, (w_up, w_down)))
 
 
 def segment_starts(lengths, row_len):
@@ -418,8 +508,172 @@
     return jnp.where(segment < count - 1, start, position[None]).astype(jnp.int32)
 
 
-def contract_rows(left, right):
-    return lax.dot_general(left, right, (((0,), (0,)), ((), ())), preferred_element_type=F32)
+def dest_chip(step):
+    chips = lax.axis_size("dp") // 2
+    return lax.rem(lax.axis_index("dp") // 2 + 2 * chips - 1 - step, chips)
+
+
+def swap_cores(block):
+    return lax.ppermute(block, "dp", [(i, i ^ 1) for i in range(lax.axis_size("dp"))])
+
+
+def next_chip(block):
+    devices = lax.axis_size("dp")
+    return lax.ppermute(block, "dp", [(i, (i + 2) % devices) for i in range(devices)])
+
+
+def largest_tile(width, most):
+    return max(tile for tile in range(128, most + 1, 128) if width % tile == 0)
+
+
+def product_kernel(pairs, offsets, gates, share, meta, *refs):
+    refs = refs[gates:]
+    lefts, rights, refs = refs[:pairs], refs[pairs:2 * pairs], refs[2 * pairs:]
+    extras = refs[:1] if pairs > 1 else ()
+    refs = refs[len(extras):]
+    added, refs = refs[:len(offsets)], refs[len(offsets):]
+    outs, refs = refs[:len(refs) - 2 * pairs - 2], refs[len(refs) - 2 * pairs - 2:]
+    lefts_v, rights_v, left_sems, right_sems = refs[:pairs], refs[pairs:2 * pairs], refs[-2], refs[-1]
+    blocks = lefts_v[0].shape[0]
+    left_copies, right_copies = [], []
+    for i in range(pairs):
+        for b in range(blocks):
+            source = lefts[i]
+            if source.shape[1] != share:
+                source = source.at[:, pl.ds(pl.multiple_of(meta[b], 128), share)]
+            left_copies.append(pltpu.make_async_copy(source, lefts_v[i].at[b], left_sems.at[i * blocks + b]))
+            left_copies[-1].start()
+        wide = largest_tile(rights[i].shape[1], 1280)
+        for n in range(rights[i].shape[1] // wide):
+            cols = slice(n * wide, (n + 1) * wide)
+            copy = pltpu.make_async_copy(rights[i].at[:, cols], rights_v[i].at[:, cols], right_sems.at[len(right_copies)])
+            copy.start()
+            right_copies.append((copy, i, n, wide))
+
+    def put(row, depth, col, value):
+        for more, offset in zip(added, offsets):
+            value = value + more[offset + row:offset + row + depth, col:col + value.shape[1]].astype(F32)
+        start = 0
+        for out in outs:
+            low, high = max(col, start), min(col + value.shape[1], start + out.shape[1])
+            if low < high:
+                out[row:row + depth, low - start:high - start] = value[:, low - col:high - col].astype(out.dtype)
+            start += out.shape[1]
+
+    deep = min(share, 256)
+    first_col = 0
+    for copy, i, n, wide in right_copies:
+        copy.wait()
+        for b in range(blocks):
+            if n == 0:
+                left_copies[i * blocks + b].wait()
+            for m in range(share // deep):
+                value = lax.dot_general(
+                    lefts_v[i][b, :, m * deep:(m + 1) * deep], rights_v[i][:, n * wide:(n + 1) * wide],
+                    (((0,), (0,)), ((), ())), preferred_element_type=F32,
+                )
+                put(b * share + m * deep, deep, first_col, value)
+        first_col += wide
+    if extras:
+        for b in range(blocks):
+            put(b * share, share, first_col, extras[0][pl.ds(pl.multiple_of(meta[b], 8), share), :])
+
+
+def products(share, firsts, lefts, rights, extra, added, dtype, gates, widths):
+    vmem = pl.BlockSpec(memory_space=pltpu.VMEM)
+    hbm = pl.BlockSpec(memory_space=pltpu.HBM)
+    count = len(firsts)
+    if share % 128:
+        blocks = [[lax.dynamic_slice_in_dim(left, first, share, 1) for first in firsts] for left in lefts]
+        if count > 1:
+            parts = [
+                products(
+                    share, firsts[b:b + 1], lefts, rights, extra, [(more, at + b * share) for more, at in added], dtype,
+                    gates, widths,
+                )
+                for b in range(count)
+            ]
+            return [jnp.concatenate(part, axis=0) for part in zip(*parts)]
+        lefts = [block[0] for block in blocks]
+    depth = lefts[0].shape[0]
+    extras = [] if extra is None else [extra]
+    total = sum(right.shape[1] for right in rights) + sum(more.shape[1] for more in extras)
+    return pl.pallas_call(
+        functools.partial(product_kernel, len(lefts), tuple(at for unused, at in added), len(gates), share),
+        out_shape=[jax.ShapeDtypeStruct((count * share, width), dtype) for width in widths or [total]],
+        in_specs=[pl.BlockSpec(memory_space=pltpu.SMEM)] + [pl.BlockSpec(memory_space=pl.ANY)] * len(gates)
+        + [hbm] * (2 * len(lefts)) + [vmem] * (len(extras) + len(added)),
+        out_specs=[vmem] * len(widths or [total]),
+        scratch_shapes=[pltpu.VMEM((count, depth, share), BF16) for _ in lefts]
+        + [pltpu.VMEM(right.shape, BF16) for right in rights]
+        + [pltpu.SemaphoreType.DMA((len(lefts) * count,)), pltpu.SemaphoreType.DMA((8,))],
+        compiler_params=pltpu.CompilerParams(vmem_limit_bytes=24 * MIB),
+        cost_estimate=pl.CostEstimate(flops=10**11, bytes_accessed=1024, transcendentals=0),
+        name="products",
+    )(
+        jnp.stack(firsts).astype(jnp.int32), *gates, *map(in_hbm, lefts), *map(in_hbm, rights), *extras,
+        *(more for more, unused in added),
+    )
+
+
+def add_kernel(offset, kept, come, *outs):
+    start = 0
+    for out in outs:
+        cols = slice(start, start + out.shape[1])
+        out[...] = (kept[offset:offset + out.shape[0], cols].astype(F32) + come[:, cols].astype(F32)).astype(out.dtype)
+        start += out.shape[1]
+
+
+def add(kept, offset, come, dtype, widths):
+    vmem = pl.BlockSpec(memory_space=pltpu.VMEM)
+    return pl.pallas_call(
+        functools.partial(add_kernel, offset),
+        out_shape=[jax.ShapeDtypeStruct((come.shape[0], width), dtype) for width in widths or [come.shape[1]]],
+        in_specs=[vmem, vmem],
+        out_specs=[vmem] * len(widths or [1]),
+        compiler_params=pltpu.CompilerParams(vmem_limit_bytes=4 * MIB),
+        cost_estimate=pl.CostEstimate(flops=10**11, bytes_accessed=1024, transcendentals=0),
+        name="add",
+    )(kept, come)
+
+
+class RowSums:
+    def __init__(self, lefts, rights, extra=None):
+        self.lefts, self.rights, self.extra = lefts, rights, extra
+        self.share = lefts[0].shape[1] // lax.axis_size("dp")
+
+    def blocks(self, steps, half, gates, added, dtype, widths=None):
+        firsts = [(dest_chip(step) * 2 + half) * self.share for step in steps]
+        return products(self.share, firsts, self.lefts, self.rights, self.extra, added, dtype, gates, widths)
+
+    def other(self, steps, gates=()):
+        return self.blocks(steps, 1 - lax.axis_index("dp") % 2, gates, [], BF16)[0]
+
+    def own(self, steps, gates, added, dtype=BF16):
+        return self.blocks(steps, lax.axis_index("dp") % 2, gates, added, dtype)[0]
+
+
+def keep_last_kernel(rows, meta, incoming, unused, gbs, sem):
+    @pl.when(meta[0] == 1)
+    def _():
+        at = pl.ds(pl.multiple_of(meta[1] * rows, rows), rows)
+        copy = pltpu.make_async_copy(incoming, gbs.at[at], sem)
+        copy.start()
+        copy.wait()
+
+
+def keep_last(meta, incoming, gbs):
+    anywhere = pl.BlockSpec(memory_space=pltpu.HBM)
+    return pl.pallas_call(
+        functools.partial(keep_last_kernel, incoming.shape[0]),
+        out_shape=pltpu.HBM(gbs.shape, gbs.dtype),
+        in_specs=[pl.BlockSpec(memory_space=pltpu.SMEM), pl.BlockSpec(memory_space=pl.ANY), anywhere],
+        out_specs=anywhere,
+        input_output_aliases={2: 0},
+        scratch_shapes=[pltpu.SemaphoreType.DMA],
+        compiler_params=pltpu.CompilerParams(vmem_limit_bytes=2 * MIB),
+        name="keep_last",
+    )(meta, incoming, gbs)
 
 
 def body(
@@ -432,10 +686,7 @@
     count = micro * row_len
     sections = lax.axis_size("section")
     place = lax.axis_index("section")
-    weights = (
-        gain_attn, w_query[0], jnp.concatenate([w_key[0], w_value[0]], axis=1), w_out[0],
-        gain_ffn, w_up[0], w_down[0],
-    )
+    weights = load_weights(gain_attn, w_query[0], w_key[0], w_value[0], w_out[0], gain_ffn, w_up[0], w_down[0])
     token_rows = tokens.reshape(count, width)
     cotangent_rows = cotangent.reshape(count, width)
     starts = segment_starts(lengths[:, 0], row_len).reshape(count, 1)
@@ -482,41 +733,78 @@
     bwd_geometry = (BWD_ROWS, row_len, heads, size)
     bwd_chunks = count // BWD_ROWS
     parts = row_len // BWD_ROWS
-    saved = [
-        empty(count, width), empty(count, ffn), empty(count, width), empty(count, heads * size),
-        empty(count, 2 * size), empty(count, width), empty(bwd_chunks, 8, width, dtype=F32),
-        empty(2 * size, row_len, dtype=F32),
-    ]
-    saved = unwritten(saved)
+    saved = unwritten([
+        empty(count, width), empty(count, ffn), empty(count, width), empty(count, (heads + 2) * size),
+        empty(count, width), empty(bwd_chunks, 8, width, dtype=F32), empty(2 * size, row_len, dtype=F32),
+    ])
     received = {}
     nothing = jnp.zeros((BWD_ROWS, width), BF16)
-    for tick in range(bwd_chunks + SKEW * (sections - 1)):
+    ticks = bwd_chunks + SKEW * (sections - 1)
+    down_sums = None
+    for tick in range(ticks):
         meta = meta_of(
             tick, bwd_chunks, sections - 1 - place, lambda step: step // parts * parts + parts - 1 - step % parts
         )
         incoming = received.pop(tick - SKEW, None)
+        if incoming is None:
+            incoming = nothing
+        if tick == ticks - 1:
+            gbs = keep_last(meta, incoming, saved[0])
+            down_sums = RowSums([kept["acts"]], [gbs])
+            swapped = swap_cores(down_sums.other([0]))
+            first_total = down_sums.own([0], (), [(swapped, 0)])
+            down_ring = next_chip(first_total)
+            ready = down_sums.other([1], [first_total])
+            swapped = swap_cores(ready)
+            out, *rest = backward_chunk(
+                bwd_geometry, True, meta, starts, cotangent_rows, incoming, needed, weights, saved[1:],
+                [first_total, ready],
+            )
+            saved = [gbs] + rest
+            continue
         out, *saved = backward_chunk(
-            bwd_geometry, meta, starts, cotangent_rows, nothing if incoming is None else incoming, needed, weights,
-            saved,
+            bwd_geometry, False, meta, starts, cotangent_rows, incoming, needed, weights, saved
         )
         received[tick] = hop(out, tick, bwd_chunks, lambda s: sections - 1 - s, -1)
     done = dict(zip(BWD_SAVED, saved))
 
     gains = jnp.sum(done["gains"], axis=0)
-    dkv = done["dkvs"]
-    grads = (
-        gains[0],
-        contract_rows(kept["n1s"], done["dqs"]),
-        contract_rows(kept["n1s"], dkv[:, :size]),
-        contract_rows(kept["n1s"], dkv[:, size:]),
-        contract_rows(kept["os"], done["gms"]),
-        gains[1],
-        contract_rows(kept["n2s"], done["dus"]),
-        contract_rows(kept["acts"], done["gbs"]),
-    )
-    shares = tuple(
-        lax.psum_scatter(grad.astype(BF16), "dp", scatter_dimension=0, tiled=True).astype(F32) for grad in grads
-    )
+    gains = jnp.pad(gains.T, ((0, 0), (0, 128 - gains.shape[0])))
+    rest_sums = RowSums([kept["n2s"], kept["n1s"], kept["os"]], [done["dus"], done["dqkvs"], done["gms"]], gains)
+    chips = lax.axis_size("dp") // 2
+    later = list(range(1, chips))
+    widths = [ffn, heads * size, size, size, width, 128]
+
+    down = down_sums.own([1], [out], [(swapped, 0), (down_ring, 0)], BF16 if chips > 2 else F32)
+    if chips > 2:
+        down_ring = next_chip(down)
+    swapped = swap_cores(rest_sums.other([0], [down]))
+    down_others = down_sums.other(later[1:], [down]) if chips > 2 else None
+    rest = rest_sums.own([0], [down] if down_others is None else [down_others], [(swapped, 0)])
+    rest_ring = next_chip(rest)
+    if chips > 2:
+        down_swapped = swap_cores(down_others)
+    rest_others = rest_sums.other(later, [rest])
+    rest_swapped = swap_cores(rest_others)
+    if chips > 2:
+        down_kept = down_sums.own(later[1:], [rest_others], [(down_swapped, 0)])
+    rest_kept = None
+    for step in range(1, chips):
+        if step + 1 < chips:
+            last = step + 1 == chips - 1
+            down = add(down_kept, (step - 1) * down_sums.share, down_ring, F32 if last else BF16, None)[0]
+            if not last:
+                down_ring = next_chip(down)
+        if rest_kept is None:
+            rest_kept = rest_sums.own(later, [down], [(rest_swapped, 0)])
+        last = step == chips - 1
+        rest = add(
+            rest_kept, (step - 1) * rest_sums.share, rest_ring, F32 if last else BF16, widths if last else None
+        )
+        if not last:
+            rest_ring = next_chip(rest[0])
+    up, query, key, value, out, gains = rest
+    shares = (gains[:, 0], query, key, value, out, gains[:, 1], up, down)
     shape = (1, micro, row_len, width)
     return (layer_outs.reshape(shape), done["igs"].reshape(shape)) + tuple(share[None] for share in shares)
 

time: 667 us -> 549 us (0.82)
  waiting for transfers between devices: 296 us -> 199 us
  Pallas kernels: 223 us -> 284 us
  matrix products: 44.5 us -> 0 us
  between operations: 16.1 us -> 2.12 us
  blocking collectives: 13.6 us -> 0 us
  other arithmetic: 17.4 us -> 4.44 us
    reduce_scatter x6 -> x0, waiting for transfers between devices: 242 us -> none  [body(): lax.psum_scatter(grad.astype(BF16), 'dp', scatter_dimension=0, tiled=True)]
    ppermute x0 -> x11, waiting for transfers between devices: none -> 106 us  [the longest x6 103 us: next_chip(): lax.ppermute(block, 'dp', [(i, (i + 2) % devices) for i in range(devices)])]
    pallas_call x10 -> x27, Pallas kernels: 106 us -> 177 us  [the longest x10 88.8 us: backward_chunk(): pl.pallas_call(functools.partial(backward_kernel, geometry, last_call, le...]
    dot_general x6 -> x0, matrix products: 44.5 us -> none  [contract_rows(): lax.dot_general(left, right, (((0,), (0,)), ((), ())), preferred_element_...]
    ppermute x20, waiting for transfers between devices: 53.9 us -> 93 us  [hop(): return lax.ppermute(block, 'section', route) if route else None]
    unnamed x1 -> x0, blocking collectives: 13.6 us -> none
    broadcast_in_dim x8 -> x0, other arithmetic: 13.1 us -> none  [body(): share[None]]
    pallas_call x14, Pallas kernels: 117 us -> 108 us  [forward_chunk(): pl.pallas_call(functools.partial(forward_kernel, geometry), out_shape=[ja...]
  transfers between devices with their start and end apart: 26 -> 31, of which waited for: 7 -> 8; matrix products, arithmetic and copies ran while one was open for 8% -> 1% of each run, Pallas kernels for 27% -> 43%
where the time goes in v2:
time: 549 us; the launch traced here: 540 us
  Pallas kernels  284 us (52%)
  waiting for transfers between devices  199 us (36%)
  starting transfers between devices  25.5 us (5%)
  local copies, waits for them, and re-layouts  24.9 us (5%)
    pallas_call x14, Pallas kernels, forward_chunk(): pl.pallas_call(functools.partial(forward_kernel, geometry), out_shape=[ja...  108 us
    ppermute x6, waiting for transfers between devices, next_chip(): lax.ppermute(block, 'dp', [(i, (i + 2) % devices) for i in range(devices)])  103 us
    ppermute x20, waiting for transfers between devices, hop(): return lax.ppermute(block, 'section', route) if route else None  93 us
    pallas_call x10, Pallas kernels, backward_chunk(): pl.pallas_call(functools.partial(backward_kernel, geometry, last_call, le...  88.8 us
    pallas_call x10, Pallas kernels, products(): pl.pallas_call(functools.partial(product_kernel, len(lefts), tuple((at fo...  71.6 us
    unnamed x50, local copies, waits for them, and re-layouts  23.9 us
    ppermute x20, starting transfers between devices, hop(): return lax.ppermute(block, 'section', route) if route else None  21.8 us
  transfers between devices with their start and end apart: 31, of which 8 were waited for; matrix products, arithmetic and copies ran while one was open for 1% of the time, Pallas kernels for 43%

profile of v2, /device:TPU:0, one launch (start us, length us, event | category | flops | bytes accessed | tf_op | source)
XLA Modules:
  0.0 540.1 jit_solution(269183793927777058)
XLA Ops:
  4.0 7.2 %load_weights.1 = (bf16[1,1024]{1,0:T(2,128)(2,1)S(1)}, bf16[1024,1024]{1,0:T(8,128)(2,1)S(1)}, bf16[1024,256]{1,0:T(8,128)(2,1)S(1)}, bf16[1024,1024]{1,0:T(8,1...) custom-call(bf16[1,1024]{1,0:T(2,128)(2,1)S(1)} %copy-done.16, ...), custom_call_target="tpu_custom_call" | custom-call | tf_op jit(solution)/shard_map/load_weights/pallas_call | solution.py:489
  11.3 10.1 %forward_chunk.14 = (bf16[128,1024]{1,0:T(8,128)(2,1)}, bf16[1024,1024]{1,0:T(8,128)(2,1)}, bf16[1024,1024]{1,0:T(8,128)(2,1)}, bf16[1024,1024]{1,0:T(8,128)(2,1...) custom-call(s32[3]{0:T(128)S(1)} %get-tuple-element.651.meta, ...), custom_call_target="tpu_custom_call", output_to_operand_aliasing={{1}: (11, {}), {2}: (12, {}), {3}: (13, {}), {4}: (14, {}),... | custom-call | flops 2885681152 | bytes 8388608 | tf_op jit(solution)/shard_map/forward_chunk/pallas_call | solution.py:218
  23.4 9.8 %forward_chunk.15 = (bf16[128,1024]{1,0:T(8,128)(2,1)}, bf16[1024,1024]{1,0:T(8,128)(2,1)}, bf16[1024,1024]{1,0:T(8,128)(2,1)}, bf16[1024,1024]{1,0:T(8,128)(2,1...) custom-call(s32[3]{0:T(128)S(1)} %get-tuple-element.650.meta, ...), custom_call_target="tpu_custom_call", output_to_operand_aliasing={{1}: (11, {}), {2}: (12, {}), {3}: (13, {}), {4}: (14, {}),... | custom-call | flops 2885681152 | bytes 8388608 | tf_op jit(solution)/shard_map/forward_chunk/pallas_call | solution.py:218
  44.8 13.1 %forward_chunk.16 = (bf16[128,1024]{1,0:T(8,128)(2,1)S(1)}, bf16[1024,1024]{1,0:T(8,128)(2,1)}, bf16[1024,1024]{1,0:T(8,128)(2,1)}, bf16[1024,1024]{1,0:T(8,128)...) custom-call(s32[3]{0:T(128)S(1)} %add_add_fusion.8.meta, ...), custom_call_target="tpu_custom_call", output_to_operand_aliasing={{1}: (11, {}), {2}: (12, {}), {3}: (13, {}), {4}: (14, {}),... | custom-call | flops 2885681152 | bytes 8388608 | tf_op jit(solution)/shard_map/forward_chunk/pallas_call | solution.py:218
  59.3 10.6 %forward_chunk.17 = (bf16[128,1024]{1,0:T(8,128)(2,1)S(1)}, bf16[1024,1024]{1,0:T(8,128)(2,1)}, bf16[1024,1024]{1,0:T(8,128)(2,1)}, bf16[1024,1024]{1,0:T(8,128)...) custom-call(s32[3]{0:T(128)S(1)} %add_add_fusion.5.meta, ...), custom_call_target="tpu_custom_call", output_to_operand_aliasing={{1}: (11, {}), {2}: (12, {}), {3}: (13, {}), {4}: (14, {}),... | custom-call | flops 2885681152 | bytes 8388608 | tf_op jit(solution)/shard_map/forward_chunk/pallas_call | solution.py:218
  71.2 9.2 %forward_chunk.18 = (bf16[128,1024]{1,0:T(8,128)(2,1)S(1)}, bf16[1024,1024]{1,0:T(8,128)(2,1)}, bf16[1024,1024]{1,0:T(8,128)(2,1)}, bf16[1024,1024]{1,0:T(8,128)...) custom-call(s32[3]{0:T(128)S(1)} %add_add_fusion.9.meta, ...), custom_call_target="tpu_custom_call", output_to_operand_aliasing={{1}: (11, {}), {2}: (12, {}), {3}: (13, {}), {4}: (14, {}),... | custom-call | flops 2885681152 | bytes 8388608 | tf_op jit(solution)/shard_map/forward_chunk/pallas_call | solution.py:218
  81.7 11.1 %forward_chunk.19 = (bf16[128,1024]{1,0:T(8,128)(2,1)S(1)}, bf16[1024,1024]{1,0:T(8,128)(2,1)}, bf16[1024,1024]{1,0:T(8,128)(2,1)}, bf16[1024,1024]{1,0:T(8,128)...) custom-call(s32[3]{0:T(128)S(1)} %add_add_fusion.4.meta, ...), custom_call_target="tpu_custom_call", output_to_operand_aliasing={{1}: (11, {}), {2}: (12, {}), {3}: (13, {}), {4}: (14, {}),... | custom-call | flops 2885681152 | bytes 8388608 | tf_op jit(solution)/shard_map/forward_chunk/pallas_call | solution.py:218
  94.2 10.6 %forward_chunk.20 = (bf16[128,1024]{1,0:T(8,128)(2,1)S(1)}, bf16[1024,1024]{1,0:T(8,128)(2,1)}, bf16[1024,1024]{1,0:T(8,128)(2,1)}, bf16[1024,1024]{1,0:T(8,128)...) custom-call(s32[3]{0:T(128)S(1)} %add_add_fusion.10.meta, ...), custom_call_target="tpu_custom_call", output_to_operand_aliasing={{1}: (11, {}), {2}: (12, {}), {3}: (13, {}), {4}: (14, {}),... | custom-call | flops 2885681152 | bytes 8388608 | tf_op jit(solution)/shard_map/forward_chunk/pallas_call | solution.py:218
  106.1 10.6 %forward_chunk.21 = (bf16[128,1024]{1,0:T(8,128)(2,1)S(1)}, bf16[1024,1024]{1,0:T(8,128)(2,1)}, bf16[1024,1024]{1,0:T(8,128)(2,1)}, bf16[1024,1024]{1,0:T(8,128)...) custom-call(s32[3]{0:T(128)S(1)} %add_add_fusion.3.meta, ...), custom_call_target="tpu_custom_call", output_to_operand_aliasing={{1}: (11, {}), {2}: (12, {}), {3}: (13, {}), {4}: (14, {}),... | custom-call | flops 2885681152 | bytes 8388608 | tf_op jit(solution)/shard_map/forward_chunk/pallas_call | solution.py:218
  118.1 8.7 %forward_chunk.22 = (bf16[128,1024]{1,0:T(8,128)(2,1)S(1)}, bf16[1024,1024]{1,0:T(8,128)(2,1)}, bf16[1024,1024]{1,0:T(8,128)(2,1)}, bf16[1024,1024]{1,0:T(8,128)...) custom-call(s32[3]{0:T(128)S(1)} %add_add_fusion.11.meta, ...), custom_call_target="tpu_custom_call", output_to_operand_aliasing={{1}: (11, {}), {2}: (12, {}), {3}: (13, {}), {4}: (14, {}),... | custom-call | flops 2885681152 | bytes 8388608 | tf_op jit(solution)/shard_map/forward_chunk/pallas_call | solution.py:218
  130.3 9.3 %forward_chunk.25 = (bf16[128,1024]{1,0:T(8,128)(2,1)S(1)}, bf16[1024,1024]{1,0:T(8,128)(2,1)}, bf16[1024,1024]{1,0:T(8,128)(2,1)}, bf16[1024,1024]{1,0:T(8,128)...) custom-call(s32[3]{0:T(128)S(1)} %add_add_fusion.1.meta, ...), custom_call_target="tpu_custom_call", output_to_operand_aliasing={{1}: (11, {}), {2}: (12, {}), {3}: (13, {}), {4}: (14, {}),... | custom-call | flops 2885681152 | bytes 8388608 | tf_op jit(solution)/shard_map/forward_chunk/pallas_call | solution.py:218
  145.9 10.0 %backward_chunk.10 = (bf16[256,1024]{1,0:T(8,128)(2,1)S(1)}, bf16[1024,1024]{1,0:T(8,128)(2,1)}, bf16[1024,4096]{1,0:T(8,128)(2,1)}, bf16[1024,1024]{1,0:T(8,128...) custom-call(s32[3]{0:T(128)S(1)} %get-tuple-element.653.meta, ...), custom_call_target="tpu_custom_call", output_to_operand_aliasing={{1}: (19, {}), {2}: (20, {}), {3}: (21, {}), {4}: (22, {}),... | custom-call | flops 6308233216 | bytes 8388608 | tf_op jit(solution)/shard_map/backward_chunk/pallas_call | solution.py:409
  158.2 6.8 %backward_chunk.12 = (bf16[256,1024]{1,0:T(8,128)(2,1)S(1)}, bf16[1024,1024]{1,0:T(8,128)(2,1)}, bf16[1024,4096]{1,0:T(8,128)(2,1)}, bf16[1024,1024]{1,0:T(8,128...) custom-call(s32[3]{0:T(128)S(1)} %add_add_fusion.20.meta, ...), custom_call_target="tpu_custom_call", output_to_operand_aliasing={{1}: (19, {}), {2}: (20, {}), {3}: (21, {}), {4}: (22, {}),... | custom-call | flops 6308233216 | bytes 8388608 | tf_op jit(solution)/shard_map/backward_chunk/pallas_call | solution.py:409
  167.1 7.0 %backward_chunk.14 = (bf16[256,1024]{1,0:T(8,128)(2,1)S(1)}, bf16[1024,1024]{1,0:T(8,128)(2,1)}, bf16[1024,4096]{1,0:T(8,128)(2,1)}, bf16[1024,1024]{1,0:T(8,128...) custom-call(s32[3]{0:T(128)S(1)} %add_add_fusion.21.meta, ...), custom_call_target="tpu_custom_call", output_to_operand_aliasing={{1}: (19, {}), {2}: (20, {}), {3}: (21, {}), {4}: (22, {}),... | custom-call | flops 6308233216 | bytes 8388608 | tf_op jit(solution)/shard_map/backward_chunk/pallas_call | solution.py:409
  177.5 92.3 %collective-permute-done.17.incoming = bf16[256,1024]{1,0:T(8,128)(2,1)S(1)} collective-permute-done((bf16[256,1024]{1,0:T(8,128)(2,1)S(1)}, bf16[256,1024]{1,0:T(8,128)(2,1)S(1)}, u32[]{:S(2)}, u32[]{:S(2)}) %collective-permute-start.17) | collective-permute-done | bytes 524320 | tf_op jit(solution)/shard_map/ppermute | solution.py:709
  269.8 16.3 %backward_chunk.16 = (bf16[256,1024]{1,0:T(8,128)(2,1)S(1)}, bf16[1024,1024]{1,0:T(8,128)(2,1)}, bf16[1024,4096]{1,0:T(8,128)(2,1)}, bf16[1024,1024]{1,0:T(8,128...) custom-call(s32[3]{0:T(128)S(1)} %add_add_fusion.22.meta, ...), custom_call_target="tpu_custom_call", output_to_operand_aliasing={{1}: (19, {}), {2}: (20, {}), {3}: (21, {}), {4}: (22, {}),... | custom-call | flops 6308233216 | bytes 8388608 | tf_op jit(solution)/shard_map/backward_chunk/pallas_call | solution.py:409
  287.4 14.8 %backward_chunk.17 = (bf16[256,1024]{1,0:T(8,128)(2,1)S(1)}, bf16[1024,1024]{1,0:T(8,128)(2,1)}, bf16[1024,4096]{1,0:T(8,128)(2,1)}, bf16[1024,1024]{1,0:T(8,128...) custom-call(s32[3]{0:T(128)S(1)} %add_add_fusion.15.meta, ...), custom_call_target="tpu_custom_call", output_to_operand_aliasing={{1}: (19, {}), {2}: (20, {}), {3}: (21, {}), {4}: (22, {}),... | custom-call | flops 6308233216 | bytes 8388608 | tf_op jit(solution)/shard_map/backward_chunk/pallas_call | solution.py:409
  304.2 17.1 %backward_chunk.18 = (bf16[256,1024]{1,0:T(8,128)(2,1)}, bf16[1024,1024]{1,0:T(8,128)(2,1)}, bf16[1024,4096]{1,0:T(8,128)(2,1)}, bf16[1024,1024]{1,0:T(8,128)(2,...) custom-call(s32[3]{0:T(128)S(1)} %add_add_fusion.23.meta, ...), custom_call_target="tpu_custom_call", output_to_operand_aliasing={{1}: (19, {}), {2}: (20, {}), {3}: (21, {}), {4}: (22, {}),... | custom-call | flops 6308233216 | bytes 8388608 | tf_op jit(solution)/shard_map/backward_chunk/pallas_call | solution.py:409
  322.7 4.3 products.10
  330.0 5.5 %products.11.refs_0_ = bf16[512,1024]{1,0:T(8,128)(2,1)} custom-call(s32[1]{0:T(128)} %bitcast.58.meta, bf16[1024,4096]{1,0:T(8,128)(2,1)} %get-tuple-element.615.refs_0_.refs_1_, bf16[1024,1024]{1,0:T(8,128)(2,1)} %keep_last.1.refs_1_.refs_2_, bf16[512,1024]{1,0:T(8,128)(2,1)} %collective-permute-done.20.refs_2_), custom_call_target="tpu_custom_call" | custom-call | flops 99999997952 | bytes 1024 | tf_op jit(solution)/shard_map/products/pallas_call | solution.py:601
  349.7 14.6 %backward_chunk.19 = (bf16[256,1024]{1,0:T(8,128)(2,1)S(1)}, bf16[1024,4096]{1,0:T(8,128)(2,1)}, bf16[1024,1024]{1,0:T(8,128)(2,1)}, bf16[1024,1280]{1,0:T(8,128...) custom-call(s32[3]{0:T(128)S(1)} %copy-done.15, ...), custom_call_target="tpu_custom_call", output_to_operand_aliasing={{1}: (21, {}), {2}: (22, {}), {3}: (23, {}), {4}: (24, {}),... | custom-call | flops 1024 | bytes 1024 | tf_op jit(solution)/shard_map/backward_chunk/pallas_call | solution.py:409
  368.6 5.9 %products.13.refs_0_ = bf16[512,1024]{1,0:T(8,128)(2,1)} custom-call(s32[1]{0:T(128)} %bitcast.75.meta, bf16[256,1024]{1,0:T(8,128)(2,1)S(1)} %copy-done.19, bf16[1024,4096]{1,0:T(8,128)(2,1)} %get-tuple-element.615.refs_0_.refs_1_, bf16[1024,1024]{1,0:T(8,128)(2,1)} %keep_last.1.refs_1_.refs_2_, bf16[512,1024]{1,0:T(8,128)(2,1)} %collective-permute-done.21.refs_3_, ...), custom_call_target="tpu_custom_call" | custom-call | flops 99999997952 | bytes 1024 | tf_op jit(solution)/shard_map/products/pallas_call | solution.py:601
  375.0 6.0 %products.15 = bf16[128,6528]{1,0:T(8,128)(2,1)S(1)} custom-call(s32[1]{0:T(128)} %bitcast.77.meta, bf16[512,1024]{1,0:T(8,128)(2,1)} %products.13.refs_0_, bf16[1024,1024]{1,0:T(8,128)(2,1)} %get-tuple-element.633.refs_1_, bf16[1024,1024]{1,0:T(8,128)(2,1)} %get-tuple-element.634.refs_2_, bf16[1024,1024]{1,0:T(8,128)(2,1)} %get-tuple-element.635.refs_3_, ...), custom_call_target="tpu_custom_call" | custom-call | flops 99999997952 | bytes 1024 | tf_op jit(solution)/shard_map/products/pallas_call | solution.py:601
  381.1 6.8 %products.14.refs_0_ = bf16[1024,1024]{1,0:T(8,128)(2,1)} custom-call(s32[2]{0:T(128)S(1)} %pad_add_fusion.3.meta, bf16[512,1024]{1,0:T(8,128)(2,1)} %products.13.refs_0_, bf16[1024,4096]{1,0:T(8,128)(2,1)} %get-tuple-element.615.refs_0_.refs_1_, bf16[1024,1024]{1,0:T(8,128)(2,1)} %keep_last.1.refs_1_.refs_2_), custom_call_target="tpu_custom_call" | custom-call | flops 99999997952 | bytes 1024 | tf_op jit(solution)/shard_map/products/pallas_call | solution.py:601
  388.4 7.2 %products.16.refs_0_ = bf16[128,6528]{1,0:T(8,128)(2,1)} custom-call(s32[1]{0:T(128)} %bitcast.72.meta, bf16[1024,1024]{1,0:T(8,128)(2,1)} %products.14.refs_0_, bf16[1024,1024]{1,0:T(8,128)(2,1)} %get-tuple-element.633.refs_1_, bf16[1024,1024]{1,0:T(8,128)(2,1)} %get-tuple-element.634.refs_2_, bf16[1024,1024]{1,0:T(8,128)(2,1)} %get-tuple-element.635.refs_3_, ...), custom_call_target="tpu_custom_call" | custom-call | flops 99999997952 | bytes 1024 | tf_op jit(solution)/shard_map/products/pallas_call | solution.py:601
  396.9 12.7 %products.17.refs_0_ = bf16[384,6528]{1,0:T(8,128)(2,1)} custom-call(s32[3]{0:T(128)S(1)} %pad_add_fusion.2.meta, bf16[128,6528]{1,0:T(8,128)(2,1)} %products.16.refs_0_, bf16[1024,1024]{1,0:T(8,128)(2,1)} %get-tuple-element.633.refs_1_, bf16[1024,1024]{1,0:T(8,128)(2,1)} %get-tuple-element.634.refs_2_, bf16[1024,1024]{1,0:T(8,128)(2,1)} %get-tuple-element.635.refs_3_, ...), custom_call_target="tpu_custom_call" | custom-call | flops 99999997952 | bytes 1024 | tf_op jit(solution)/shard_map/products/pallas_call | solution.py:601
  409.7 6.5 %products.18.kept = bf16[1024,1024]{1,0:T(8,128)(2,1)S(1)} custom-call(s32[2]{0:T(128)S(1)} %pad_add_fusion.1.meta, bf16[384,6528]{1,0:T(8,128)(2,1)} %products.17.refs_0_, bf16[1024,4096]{1,0:T(8,128)(2,1)} %get-tuple-element.615.refs_0_.refs_1_, bf16[1024,1024]{1,0:T(8,128)(2,1)} %keep_last.1.refs_1_.refs_2_, ...), custom_call_target="tpu_custom_call" | custom-call | flops 99999997952 | bytes 1024 | tf_op jit(solution)/shard_map/products/pallas_call | solution.py:601
  418.5 12.5 %products.19.kept = bf16[384,6528]{1,0:T(8,128)(2,1)S(1)} custom-call(s32[3]{0:T(128)S(1)} %pad_add_fusion.meta, bf16[512,1024]{1,0:T(8,128)(2,1)S(1)} %add.290.refs_0_, bf16[1024,1024]{1,0:T(8,128)(2,1)} %get-tuple-element.633.refs_1_, bf16[1024,1024]{1,0:T(8,128)(2,1)} %get-tuple-element.634.refs_2_, bf16[1024,1024]{1,0:T(8,128)(2,1)} %get-tuple-element.635.refs_3_, ...), custom_call_target="tpu_custom_call" | custom-call | flops 99999997952 | bytes 1024 | tf_op jit(solution)/shard_map/products/pallas_call | solution.py:601
  431.0 6.5 %collective-permute-done.27.come = bf16[128,6528]{1,0:T(8,128)(2,1)} collective-permute-done((bf16[128,6528]{1,0:T(8,128)(2,1)}, bf16[128,6528]{1,0:T(8,128)(2,1)}, u32[]{:S(2)}, u32[]{:S(2)}) %collective-permute-start.27) | collective-permute-done | bytes 1671200 | tf_op jit(solution)/shard_map/ppermute | solution.py:522
  440.4 40.3 %collective-permute-done.28.come = bf16[128,6528]{1,0:T(8,128)(2,1)S(1)} collective-permute-done((bf16[128,6528]{1,0:T(8,128)(2,1)S(1)}, bf16[128,6528]{1,0:T(8,128)(2,1)S(1)}, u32[]{:S(2)}, u32[]{:S(2)}) %collective-permute-start.28) | collective-permute-done | bytes 1671200 | tf_op jit(solution)/shard_map/ppermute | solution.py:522
  481.1 22.0 %collective-permute-done.30.come = bf16[512,1024]{1,0:T(8,128)(2,1)S(1)} collective-permute-done((bf16[512,1024]{1,0:T(8,128)(2,1)S(1)}, bf16[512,1024]{1,0:T(8,128)(2,1)S(1)}, u32[]{:S(2)}, u32[]{:S(2)}) %collective-permute-start.30) | collective-permute-done | bytes 1048608 | tf_op jit(solution)/shard_map/ppermute | solution.py:522
  504.7 32.6 %collective-permute-done.29.come = bf16[128,6528]{1,0:T(8,128)(2,1)S(1)} collective-permute-done((bf16[128,6528]{1,0:T(8,128)(2,1)S(1)}, bf16[128,6528]{1,0:T(8,128)(2,1)S(1)}, u32[]{:S(2)}, u32[]{:S(2)}) %collective-permute-start.29) | collective-permute-done | bytes 1671200 | tf_op jit(solution)/shard_map/ppermute | solution.py:522
  (160 shorter events, 80.0 us)
Async XLA Ops:
  21.4 15.1 %collective-permute-start.1 = (bf16[128,1024]{1,0:T(8,128)(2,1)}, bf16[128,1024]{1,0:T(8,128)(2,1)}, u32[]{:S(2)}, u32[]{:S(2)}) collective-permute-start(bf16[128,1024]{1,0:T(8,128)(2,1)} %get-tuple-element.364), channel_id=1, source_target_pairs={{0,8},{1,9},{2,10},{3,11},{4,12},{5,13},{6,14},{7,15}} | collective-permute-start | bytes 786440 | tf_op jit(solution)/shard_map/ppermute | solution.py:709
  33.3 26.0 %collective-permute-start = (bf16[128,1024]{1,0:T(8,128)(2,1)}, bf16[128,1024]{1,0:T(8,128)(2,1)S(1)}, u32[]{:S(2)}, u32[]{:S(2)}) collective-permute-start(bf16[128,1024]{1,0:T(8,128)(2,1)} %get-tuple-element.363), channel_id=1, source_target_pairs={{0,8},{1,9},{2,10},{3,11},{4,12},{5,13},{6,14},{7,15}} | collective-permute-start | bytes 786440 | tf_op jit(solution)/shard_map/ppermute | solution.py:709
  36.4 284.9 %copy-start.14 = (s32[3]{0:T(128)}, s32[3]{0:T(128)S(1)}, u32[]{:S(2)}) copy-start(s32[3]{0:T(128)S(1)} %add_add_fusion.14.meta) | copy-start | bytes 40
  57.9 13.3 %collective-permute-start.3 = (bf16[128,1024]{1,0:T(8,128)(2,1)S(1)}, bf16[128,1024]{1,0:T(8,128)(2,1)S(1)}, u32[]{:S(2)}, u32[]{:S(2)}) collective-permute-start(bf16[128,1024]{1,0:T(8,128)(2,1)S(1)} %get-tuple-element.394), channel_id=1, source_target_pairs={{0,8},{8,16},{1,9},{9,17},{2,10},{10,18},{3,11},{11,19},{4,12},{12... | collective-permute-start | bytes 786440 | tf_op jit(solution)/shard_map/ppermute | solution.py:709
  69.9 11.9 %collective-permute-start.2 = (bf16[128,1024]{1,0:T(8,128)(2,1)S(1)}, bf16[128,1024]{1,0:T(8,128)(2,1)S(1)}, u32[]{:S(2)}, u32[]{:S(2)}) collective-permute-start(bf16[128,1024]{1,0:T(8,128)(2,1)S(1)} %get-tuple-element.393), channel_id=1, source_target_pairs={{0,8},{8,16},{1,9},{9,17},{2,10},{10,18},{3,11},{11,19},{4,12},{12... | collective-permute-start | bytes 786440 | tf_op jit(solution)/shard_map/ppermute | solution.py:709
  80.4 13.7 %collective-permute-start.5 = (bf16[128,1024]{1,0:T(8,128)(2,1)S(1)}, bf16[128,1024]{1,0:T(8,128)(2,1)S(1)}, u32[]{:S(2)}, u32[]{:S(2)}) collective-permute-start(bf16[128,1024]{1,0:T(8,128)(2,1)S(1)} %get-tuple-element.424), channel_id=1, source_target_pairs={{0,8},{8,16},{16,24},{1,9},{9,17},{17,25},{2,10},{10,18},{18,26},{... | collective-permute-start | bytes 786440 | tf_op jit(solution)/shard_map/ppermute | solution.py:709
  92.8 13.3 %collective-permute-start.4 = (bf16[128,1024]{1,0:T(8,128)(2,1)S(1)}, bf16[128,1024]{1,0:T(8,128)(2,1)S(1)}, u32[]{:S(2)}, u32[]{:S(2)}) collective-permute-start(bf16[128,1024]{1,0:T(8,128)(2,1)S(1)} %get-tuple-element.423), channel_id=1, source_target_pairs={{0,8},{8,16},{16,24},{1,9},{9,17},{17,25},{2,10},{10,18},{18,26},{... | collective-permute-start | bytes 786440 | tf_op jit(solution)/shard_map/ppermute | solution.py:709
  104.8 13.3 %collective-permute-start.7 = (bf16[128,1024]{1,0:T(8,128)(2,1)S(1)}, bf16[128,1024]{1,0:T(8,128)(2,1)S(1)}, u32[]{:S(2)}, u32[]{:S(2)}) collective-permute-start(bf16[128,1024]{1,0:T(8,128)(2,1)S(1)} %get-tuple-element.454), channel_id=1, source_target_pairs={{0,8},{8,16},{16,24},{1,9},{9,17},{17,25},{2,10},{10,18},{18,26},{... | collective-permute-start | bytes 786440 | tf_op jit(solution)/shard_map/ppermute | solution.py:709
  116.8 10.7 %collective-permute-start.6 = (bf16[128,1024]{1,0:T(8,128)(2,1)S(1)}, bf16[128,1024]{1,0:T(8,128)(2,1)S(1)}, u32[]{:S(2)}, u32[]{:S(2)}) collective-permute-start(bf16[128,1024]{1,0:T(8,128)(2,1)S(1)} %get-tuple-element.453), channel_id=1, source_target_pairs={{0,8},{8,16},{16,24},{1,9},{9,17},{17,25},{2,10},{10,18},{18,26},{... | collective-permute-start | bytes 786440 | tf_op jit(solution)/shard_map/ppermute | solution.py:709
  126.7 2.1 collective-permute-start.9
  128.2 2.1 collective-permute-start.8
  129.6 10.7 %collective-permute-start.11 = (bf16[128,1024]{1,0:T(8,128)(2,1)S(1)}, bf16[128,1024]{1,0:T(8,128)(2,1)S(1)}, u32[]{:S(2)}, u32[]{:S(2)}) collective-permute-start(bf16[128,1024]{1,0:T(8,128)(2,1)S(1)} %get-tuple-element.514), channel_id=1, source_target_pairs={{16,24},{17,25},{18,26},{19,27},{20,28},{21,29},{22,30},{23,31}} | collective-permute-start | bytes 786440 | tf_op jit(solution)/shard_map/ppermute | solution.py:709
  139.6 2.1 collective-permute-start.10
  156.0 2.2 collective-permute-start.13
  157.4 8.2 %collective-permute-start.12 = (bf16[256,1024]{1,0:T(8,128)(2,1)S(1)}, bf16[256,1024]{1,0:T(8,128)(2,1)S(1)}, u32[]{:S(2)}, u32[]{:S(2)}) collective-permute-start(bf16[256,1024]{1,0:T(8,128)(2,1)S(1)} %get-tuple-element.566), channel_id=1, source_target_pairs={{24,16},{25,17},{26,18},{27,19},{28,20},{29,21},{30,22},{31,23}} | collective-permute-start | bytes 1572872 | tf_op jit(solution)/shard_map/ppermute | solution.py:709
  165.0 2.2 collective-permute-start.15
  166.4 9.0 %collective-permute-start.14 = (bf16[256,1024]{1,0:T(8,128)(2,1)S(1)}, bf16[256,1024]{1,0:T(8,128)(2,1)S(1)}, u32[]{:S(2)}, u32[]{:S(2)}) collective-permute-start(bf16[256,1024]{1,0:T(8,128)(2,1)S(1)} %get-tuple-element.582), channel_id=1, source_target_pairs={{16,8},{24,16},{17,9},{25,17},{18,10},{26,18},{19,11},{27,19},{20,... | collective-permute-start | bytes 1572872 | tf_op jit(solution)/shard_map/ppermute | solution.py:709
  174.2 95.7 %collective-permute-start.17 = (bf16[256,1024]{1,0:T(8,128)(2,1)S(1)}, bf16[256,1024]{1,0:T(8,128)(2,1)S(1)}, u32[]{:S(2)}, u32[]{:S(2)}) collective-permute-start(bf16[256,1024]{1,0:T(8,128)(2,1)S(1)} %get-tuple-element.599), channel_id=1, source_target_pairs={{8,0},{16,8},{9,1},{17,9},{10,2},{18,10},{11,3},{19,11},{12,4},{20... | collective-permute-start | bytes 1572872 | tf_op jit(solution)/shard_map/ppermute | solution.py:709
  176.2 111.2 %collective-permute-start.16 = (bf16[256,1024]{1,0:T(8,128)(2,1)S(1)}, bf16[256,1024]{1,0:T(8,128)(2,1)S(1)}, u32[]{:S(2)}, u32[]{:S(2)}) collective-permute-start(bf16[256,1024]{1,0:T(8,128)(2,1)S(1)} %get-tuple-element.598), channel_id=1, source_target_pairs={{8,0},{16,8},{9,1},{17,9},{10,2},{18,10},{11,3},{19,11},{12,4},{20... | collective-permute-start | bytes 1572872 | tf_op jit(solution)/shard_map/ppermute | solution.py:709
  286.1 18.1 %collective-permute-start.19 = (bf16[256,1024]{1,0:T(8,128)(2,1)S(1)}, bf16[256,1024]{1,0:T(8,128)(2,1)S(1)}, u32[]{:S(2)}, u32[]{:S(2)}) collective-permute-start(bf16[256,1024]{1,0:T(8,128)(2,1)S(1)} %get-tuple-element.616), channel_id=1, source_target_pairs={{8,0},{9,1},{10,2},{11,3},{12,4},{13,5},{14,6},{15,7}} | collective-permute-start | bytes 1572872 | tf_op jit(solution)/shard_map/ppermute | solution.py:709
  302.2 19.1 %collective-permute-start.18 = (bf16[256,1024]{1,0:T(8,128)(2,1)S(1)}, bf16[256,1024]{1,0:T(8,128)(2,1)S(1)}, u32[]{:S(2)}, u32[]{:S(2)}) collective-permute-start(bf16[256,1024]{1,0:T(8,128)(2,1)S(1)} %get-tuple-element.614), channel_id=1, source_target_pairs={{8,0},{9,1},{10,2},{11,3},{12,4},{13,5},{14,6},{15,7}} | collective-permute-start | bytes 1572872 | tf_op jit(solution)/shard_map/ppermute | solution.py:709
  327.0 3.1 collective-permute-start.20
  339.8 26.5 %collective-permute-start.21 = (bf16[512,1024]{1,0:T(8,128)(2,1)}, bf16[512,1024]{1,0:T(8,128)(2,1)}, u32[]{:S(2)}, u32[]{:S(2)}) collective-permute-start(bf16[512,1024]{1,0:T(8,128)(2,1)} %products.12.refs_1_), channel_id=1, source_target_pairs={{0,1},{1,0},{2,3},{3,2},{4,5},{5,4},{6,7},{7,6},{8,9},{9,8},{10,11... | collective-permute-start | bytes 3145736 | tf_op jit(solution)/shard_map/ppermute | solution.py:517
  340.0 27.5 %collective-permute-start.22 = (bf16[512,1024]{1,0:T(8,128)(2,1)}, bf16[512,1024]{1,0:T(8,128)(2,1)}, u32[]{:S(2)}, u32[]{:S(2)}) collective-permute-start(bf16[512,1024]{1,0:T(8,128)(2,1)} %products.11.refs_0_), channel_id=1, source_target_pairs={{0,2},{1,3},{2,4},{3,5},{4,6},{5,7},{6,0},{7,1},{8,10},{9,11},{10,... | collective-permute-start | bytes 3145736 | tf_op jit(solution)/shard_map/ppermute | solution.py:522
  374.5 41.7 %collective-permute-start.25 = (bf16[512,1024]{1,0:T(8,128)(2,1)}, bf16[512,1024]{1,0:T(8,128)(2,1)}, u32[]{:S(2)}, u32[]{:S(2)}) collective-permute-start(bf16[512,1024]{1,0:T(8,128)(2,1)} %products.13.refs_0_), channel_id=1, source_target_pairs={{0,2},{1,3},{2,4},{3,5},{4,6},{5,7},{6,0},{7,1},{8,10},{9,11},{10,... | collective-permute-start | bytes 3145736 | tf_op jit(solution)/shard_map/ppermute | solution.py:522
  381.0 7.4 %collective-permute-start.23 = (bf16[128,6528]{1,0:T(8,128)(2,1)S(1)}, bf16[128,6528]{1,0:T(8,128)(2,1)S(1)}, u32[]{:S(2)}, u32[]{:S(2)}) collective-permute-start(bf16[128,6528]{1,0:T(8,128)(2,1)S(1)} %products.15), channel_id=1, source_target_pairs={{0,1},{1,0},{2,3},{3,2},{4,5},{5,4},{6,7},{7,6},{8,9},{9,8},{10,11... | collective-permute-start | bytes 5013512 | tf_op jit(solution)/shard_map/ppermute | solution.py:517
  387.9 21.8 %collective-permute-start.24 = (bf16[1024,1024]{1,0:T(8,128)(2,1)}, bf16[1024,1024]{1,0:T(8,128)(2,1)}, u32[]{:S(2)}, u32[]{:S(2)}) collective-permute-start(bf16[1024,1024]{1,0:T(8,128)(2,1)} %products.14.refs_0_), channel_id=1, source_target_pairs={{0,1},{1,0},{2,3},{3,2},{4,5},{5,4},{6,7},{7,6},{8,9},{9,8},{10,11... | collective-permute-start | bytes 6291464 | tf_op jit(solution)/shard_map/ppermute | solution.py:517
  395.6 41.9 %collective-permute-start.27 = (bf16[128,6528]{1,0:T(8,128)(2,1)}, bf16[128,6528]{1,0:T(8,128)(2,1)}, u32[]{:S(2)}, u32[]{:S(2)}) collective-permute-start(bf16[128,6528]{1,0:T(8,128)(2,1)} %products.16.refs_0_), channel_id=1, source_target_pairs={{0,2},{1,3},{2,4},{3,5},{4,6},{5,7},{6,0},{7,1},{8,10},{9,11},{10,... | collective-permute-start | bytes 5013512 | tf_op jit(solution)/shard_map/ppermute | solution.py:522
  409.6 8.9 %collective-permute-start.26 = (bf16[384,6528]{1,0:T(8,128)(2,1)}, bf16[384,6528]{1,0:T(8,128)(2,1)}, u32[]{:S(2)}, u32[]{:S(2)}) collective-permute-start(bf16[384,6528]{1,0:T(8,128)(2,1)} %products.17.refs_0_), channel_id=1, source_target_pairs={{0,1},{1,0},{2,3},{3,2},{4,5},{5,4},{6,7},{7,6},{8,9},{9,8},{10,11... | collective-permute-start | bytes 15040520 | tf_op jit(solution)/shard_map/ppermute | solution.py:517
  439.4 41.3 %collective-permute-start.28 = (bf16[128,6528]{1,0:T(8,128)(2,1)S(1)}, bf16[128,6528]{1,0:T(8,128)(2,1)S(1)}, u32[]{:S(2)}, u32[]{:S(2)}) collective-permute-start(bf16[128,6528]{1,0:T(8,128)(2,1)S(1)} %add.291), channel_id=1, source_target_pairs={{0,2},{1,3},{2,4},{3,5},{4,6},{5,7},{6,0},{7,1},{8,10},{9,11},{10,... | collective-permute-start | bytes 5013512 | tf_op jit(solution)/shard_map/ppermute | solution.py:522
  439.4 63.7 %collective-permute-start.30 = (bf16[512,1024]{1,0:T(8,128)(2,1)S(1)}, bf16[512,1024]{1,0:T(8,128)(2,1)S(1)}, u32[]{:S(2)}, u32[]{:S(2)}) collective-permute-start(bf16[512,1024]{1,0:T(8,128)(2,1)S(1)} %add.290.refs_0_), channel_id=1, source_target_pairs={{0,2},{1,3},{2,4},{3,5},{4,6},{5,7},{6,0},{7,1},{8,10},{9,11},{10,... | collective-permute-start | bytes 3145736 | tf_op jit(solution)/shard_map/ppermute | solution.py:522
  481.0 56.2 %collective-permute-start.29 = (bf16[128,6528]{1,0:T(8,128)(2,1)S(1)}, bf16[128,6528]{1,0:T(8,128)(2,1)S(1)}, u32[]{:S(2)}, u32[]{:S(2)}) collective-permute-start(bf16[128,6528]{1,0:T(8,128)(2,1)S(1)} %add.292), channel_id=1, source_target_pairs={{0,2},{1,3},{2,4},{3,5},{4,6},{5,7},{6,0},{7,1},{8,10},{9,11},{10,... | collective-permute-start | bytes 5013512 | tf_op jit(solution)/shard_map/ppermute | solution.py:522
  (23 other events, 172.6 us)

commit v3 on v2

v3 whole, which is shorter than its diff:
```python
import functools

import jax
import jax.numpy as jnp
from jax import lax
from jax.experimental import pallas as pl
from jax.experimental.pallas import tpu as pltpu
from jax.sharding import PartitionSpec as P

NORM_EPS = 1e-06
MASKED = -1e30
LOG2E = 1.4426950408889634
FWD_ROWS = 128
BWD_ROWS = 256
FFN_TILE = 2048
BWD_TILE = 2048
SKEW = 2
FWD_HEADS = 4
BWD_HEADS = 2
NORM_BLOCK = 128
NORM_UNROLL = 2
SOFTMAX_BLOCK = 128
SOFTMAX_UNROLL = 2
SIDE_TILE = 512
MIB = 1 << 20
LIGHT = 5 * 10**9
HEAVY = 10**11

BF16 = jnp.bfloat16
F32 = jnp.float32


def in_hbm(array):
    return pltpu.with_memory_space_constraint(array, pltpu.HBM)


def in_vmem(array):
    return pltpu.with_memory_space_constraint(array, pltpu.VMEM)


def dot(left, right):
    return jnp.dot(left, right, preferred_element_type=F32)


def dot_t(left, right):
    return lax.dot_general(left, right, (((1,), (1,)), ((), ())), preferred_element_type=F32)


def inverse_rms(rows):
    return lax.rsqrt(jnp.mean(rows * rows, axis=-1, keepdims=True) + NORM_EPS)


def gelu_parts(u):
    t = pl.reciprocal(1.0 + jnp.abs(u) * 0.23164190, approx=True)
    bell = jnp.exp2(u * u * (-0.5 * LOG2E))
    poly = t * (0.127414796 + t * (-0.142248368 + t * (0.7107068705 + t * (-0.7265760135 + t * 0.5307027145))))
    tail = poly * bell
    cdf = jnp.where(u >= 0, 1.0 - tail, tail)
    return u * cdf, cdf + u * bell * 0.3989422804014327


def each_block(rows, block, work, unroll=1):
    def step(i, unused):
        work(pl.ds(pl.multiple_of(i * block, block), block))
        return unused

    lax.fori_loop(0, rows // block, step, 0, unroll=unroll)


def weight_copies(sources, targets, sems):
    w_query, w_key, w_value, w_out, w_up, w_down = sources
    w_query_v, w_kv_v, w_out_v, w_up_v, w_down_v = targets
    size = w_key.shape[1]
    half = w_up.shape[1] // 2
    low, high = slice(0, half), slice(half, 2 * half)
    pieces = {
        "query": (w_query, w_query_v),
        "key": (w_key, w_kv_v.at[:, :size]),
        "value": (w_value, w_kv_v.at[:, size:]),
        "out": (w_out, w_out_v),
        "up0": (w_up.at[:, low], w_up_v.at[:, low]),
        "up1": (w_up.at[:, high], w_up_v.at[:, high]),
        "down0": (w_down.at[low, :], w_down_v.at[low, :]),
        "down1": (w_down.at[high, :], w_down_v.at[high, :]),
    }
    return {name: pltpu.make_async_copy(*piece, sems.at[i]) for i, (name, piece) in enumerate(pieces.items())}


FWD_LOADS = ("query", "key", "value", "out", "up0", "up1", "down0", "down1")
BWD_LOADS = ("down0", "up0", "down1", "up1", "out", "query", "key", "value")


def position_bias(meta, spot, count, first_row, rows, length):
    place = first_row + lax.broadcasted_iota(jnp.int32, (rows, 1), 0)
    start = jnp.zeros((rows, 1), jnp.int32)
    end = 0
    for i in range(count - 1):
        end = end + meta[spot + i]
        start = jnp.where(place >= end, end, start)
    start = jnp.where(place >= end, place, start)
    own = first_row + lax.broadcasted_iota(jnp.int32, (rows, length), 0)
    other = lax.broadcasted_iota(jnp.int32, (rows, length), 1)
    return jnp.where((other >= start) & (other <= own), 0.0, MASKED)


def forward_kernel(geometry, loading, places, spots, meta, tokens, incoming, gain_attn, gain_ffn, *refs):
    rows, row_len, heads, size, segments = geometry
    spot, lengths_spot = spots
    if loading:
        sources, refs = refs[:6], refs[6:]
        load_sems = refs[-1]
        w_query, w_kv, w_out, w_up, w_down = refs[2 * len(FWD_SAVED) + 1:2 * len(FWD_SAVED) + 6]
        refs = refs[:2 * len(FWD_SAVED) + 1] + refs[2 * len(FWD_SAVED) + 6:-1]
        weight_loads = weight_copies(sources, (w_query, w_kv, w_out, w_up, w_down), load_sems)
        for name in FWD_LOADS:
            weight_loads[name].start()
    else:
        w_query, w_kv, w_out, w_up, w_down = refs[:5]
        refs = refs[5:]

    def loaded(*names):
        for name in names if loading else ():
            weight_loads[name].wait()

    saved = refs[len(FWD_SAVED):2 * len(FWD_SAVED) + 1]
    out, hs, n1s, qs, ks, vs, kts, vts, os_, mids, n2s, acts, slopes, lses, outs = saved
    (h_v, n1_v, q_v, k_v, v_v, kt_v, vt_v, o_v, mid_v, n2_v, act_v, slope_v, lse_v, out_v, bias_v, total_v, s_v, p_v, sems) = (
        refs[2 * len(FWD_SAVED) + 1:]
    )
    parts = row_len // rows
    active, chunk, first = meta[spot], meta[spot + 1], meta[spot + 2]
    width = heads * size
    scale = size**-0.5 * LOG2E

    @pl.when(active == 0)
    def _():
        loaded(*FWD_LOADS)

    @pl.when(active == 1)
    def _():
        row = chunk // parts
        place = chunk % parts
        at = pl.ds(pl.multiple_of(chunk * rows, rows), rows)
        within = pl.ds(pl.multiple_of(place * rows, rows), rows)
        whole = pl.ds(pl.multiple_of(row * row_len, row_len), row_len)

        @pl.when(first == 1)
        def _():
            pltpu.make_async_copy(tokens.at[at], h_v, sems.at[0]).start()

        load_v = pltpu.make_async_copy(vs.at[whole], v_v, sems.at[1])
        load_kt = pltpu.make_async_copy(kts.at[row], kt_v, sems.at[2])
        load_v.start()
        load_kt.start()
        pending = []

        def keep(source, target, slot):
            copy = pltpu.make_async_copy(source, target, sems.at[slot])
            copy.start()
            pending.append(copy)

        @pl.when(first == 1)
        def _():
            pltpu.make_async_copy(tokens.at[at], h_v, sems.at[0]).wait()

        @pl.when(first == 0)
        def _():
            h_v[...] = incoming[...]

        keep(h_v, hs.at[at], 3)

        def norm_attn(block):
            h = h_v[block, :].astype(F32)
            n1_v[block, :] = (h * inverse_rms(h) * gain_attn[...].astype(F32)).astype(BF16)

        each_block(rows, NORM_BLOCK, norm_attn, rows // NORM_BLOCK)
        keep(n1_v, n1s.at[at], 4)
        loaded("query", "key", "value")
        kv = dot(n1_v[...], w_kv[...]).astype(BF16)
        q_v[...] = dot(n1_v[...], w_query[...]).astype(BF16)
        k_v[...] = kv[:, :size]
        keep(k_v, ks.at[at], 5)
        keep(q_v, qs.at[at], 6)
        load_v.wait()
        load_kt.wait()
        v_v[within, :] = kv[:, size:]
        kt_v[:, within] = kv[:, :size].T
        vt_v[...] = kv[:, size:].T
        keep(v_v.at[within], vs.at[at], 7)
        keep(kt_v.at[:, within], kts.at[row, :, within], 8)
        keep(vt_v, vts.at[row, :, within], 9)

        lse_v[...] = jnp.zeros((rows, size), F32)

        def attend(static_place):
            length = (static_place + 1) * rows
            lane = lax.broadcasted_iota(jnp.int32, (SOFTMAX_BLOCK, size), 1)
            bias_v[:, :length] = position_bias(
                meta, lengths_spot + row * segments, segments, static_place * rows, rows, length
            )

            def some_heads(step, carry):
                group = [step * FWD_HEADS + i for i in range(FWD_HEADS)]
                for i, head in enumerate(group):
                    cols = pl.ds(pl.multiple_of(head * size, size), size)
                    s_v[i, :, :length] = dot(q_v[:, cols], kt_v[:, :length])
                for i, head in enumerate(group):
                    cols = pl.ds(pl.multiple_of(head * size, size), size)

                    def soften(block, i=i, head=head):
                        scores = s_v[i, block, :length] * scale + bias_v[block, :length]
                        top = jnp.max(scores, axis=1, keepdims=True)
                        weights = jnp.exp2(scores - top)
                        total = jnp.sum(weights, axis=1, keepdims=True)
                        p_v[i, block, :length] = (weights * (1.0 / total)).astype(BF16)
                        lse_v[block, :] = jnp.where(lane == head, top + jnp.log2(total), lse_v[block, :])

                    each_block(rows, SOFTMAX_BLOCK, soften, rows // SOFTMAX_BLOCK)
                    o_v[:, cols] = dot(p_v[i, :, :length], v_v[:length, :]).astype(BF16)
                return carry

            lax.fori_loop(0, heads // FWD_HEADS, some_heads, 0)

        for static_place in places:
            if len(places) == 1:
                attend(static_place)
            else:
                pl.when(place == static_place)(functools.partial(attend, static_place))

        keep(lse_v, lses.at[at], 10)
        keep(o_v, os_.at[at], 11)
        loaded("out")
        total_v[...] = dot(o_v[...], w_out[...])

        def norm_ffn(block):
            mid = h_v[block, :].astype(F32) + total_v[block, :]
            mid_v[block, :] = mid
            total_v[block, :] = mid
            n2_v[block, :] = (mid * inverse_rms(mid) * gain_ffn[...].astype(F32)).astype(BF16)

        each_block(rows, NORM_BLOCK, norm_ffn, rows // NORM_BLOCK)
        keep(mid_v, mids.at[at], 12)
        keep(n2_v, n2s.at[at], 13)
        ffn = w_up.shape[1]
        tile = min(FFN_TILE, ffn)


        def columns(f):
            return pl.ds(pl.multiple_of(f * tile, tile), tile)

        def rise(f):
            return dot(n2_v[...], w_up[:, columns(f)])

        def bend(f, u):
            act, slope = gelu_parts(u)
            act_v[:, columns(f)] = act.astype(BF16)
            slope_v[:, columns(f)] = slope.astype(BF16)
            pltpu.make_async_copy(act_v.at[:, columns(f)], acts.at[at, columns(f)], sems.at[14]).start()
            pltpu.make_async_copy(slope_v.at[:, columns(f)], slopes.at[at, columns(f)], sems.at[15]).start()

        def fall(f):
            return dot(act_v[:, columns(f)], w_down[columns(f), :])

        def both(f, carry):
            u = rise(f)
            part = fall(f - 1)
            bend(f, u)
            total_v[...] += part
            return carry

        loaded("up0")
        bend(0, rise(0))
        loaded("up1", "down0")
        lax.fori_loop(1, ffn // tile, both, 0)
        loaded("down1")
        total_v[...] += fall(ffn // tile - 1)
        total = total_v[...]
        pending.append(pltpu.make_async_copy(act_v, acts.at[at], sems.at[14]))
        pending.append(pltpu.make_async_copy(slope_v, slopes.at[at], sems.at[15]))
        result = total.astype(BF16)
        out[...] = result
        out_v[...] = result
        keep(out_v, outs.at[at], 16)
        for copy in pending:
            copy.wait()


FWD_SAVED = ("hs", "n1s", "qs", "ks", "vs", "kts", "vts", "os", "mids", "n2s", "acts", "slopes", "lses", "outs")


def forward_chunk(geometry, places, spots, meta, tokens, incoming, weights, saved, given=None):
    rows, row_len, heads, size, unused = geometry
    gain_attn, gain_ffn, *matrices = weights
    loading = given is not None
    width = tokens.shape[1]
    ffn = (given[4] if loading else matrices[3]).shape[1]
    vmem = pl.BlockSpec(memory_space=pltpu.VMEM)
    hbm = pl.BlockSpec(memory_space=pltpu.HBM)
    loads = [pltpu.VMEM(shape, BF16) for shape in weight_shapes(given)] if loading else []
    operands = list(map(in_hbm, given)) if loading else list(map(in_vmem, matrices))
    lead = 5 + len(operands)
    flops = 2 * rows * (2 * width * heads * size + 2 * width * size + 2 * width * ffn + row_len * heads * size)
    out, *rest = pl.pallas_call(
        functools.partial(forward_kernel, geometry, loading, places, spots),
        out_shape=[jax.ShapeDtypeStruct((rows, width), BF16)]
        + [pltpu.HBM(array.shape, array.dtype) for array in saved] + loads,
        in_specs=[pl.BlockSpec(memory_space=pltpu.SMEM), hbm, vmem, vmem, vmem]
        + [hbm if loading else vmem] * len(operands) + [hbm] * len(saved),
        out_specs=[vmem] + [hbm] * len(saved) + [vmem] * len(loads),
        input_output_aliases={lead + i: 1 + i for i in range(len(saved))},
        scratch_shapes=[
            pltpu.VMEM((rows, width), BF16),
            pltpu.VMEM((rows, width), BF16),
            pltpu.VMEM((rows, heads * size), BF16),
            pltpu.VMEM((rows, size), BF16),
            pltpu.VMEM((row_len, size), BF16),
            pltpu.VMEM((size, row_len), BF16),
            pltpu.VMEM((size, rows), BF16),
            pltpu.VMEM((rows, heads * size), BF16),
            pltpu.VMEM((rows, width), F32),
            pltpu.VMEM((rows, width), BF16),
            pltpu.VMEM((rows, ffn), BF16),
            pltpu.VMEM((rows, ffn), BF16),
            pltpu.VMEM((rows, size), F32),
            pltpu.VMEM((rows, width), BF16),
            pltpu.VMEM((rows, row_len), F32),
            pltpu.VMEM((rows, width), F32),
            pltpu.VMEM((FWD_HEADS, rows, row_len), F32),
            pltpu.VMEM((FWD_HEADS, rows, row_len), BF16),
            pltpu.SemaphoreType.DMA((17,)),
        ]
        + [pltpu.SemaphoreType.DMA((8,))] * loading,
        compiler_params=pltpu.CompilerParams(vmem_limit_bytes=12 * MIB),
        cost_estimate=pl.CostEstimate(flops=flops, bytes_accessed=8 * MIB, transcendentals=0),
        name="forward_chunk",
    )(meta, in_hbm(tokens), in_vmem(incoming), gain_attn, gain_ffn, *operands, *saved)
    return out, rest[:len(saved)], rest[len(saved):]


def weight_shapes(given):
    w_query, w_key, w_value, w_out, w_up, w_down = given
    return w_query.shape, (w_key.shape[0], 2 * w_key.shape[1]), w_out.shape, w_up.shape, w_down.shape


BWD_SAVED = ("gbs", "dus", "gms", "dqkvs", "igs", "gains", "carry")


def norm_backward(rows, gain, upstream):
    inverse = inverse_rms(rows)
    unit = rows * inverse
    steered = upstream * gain
    grad = inverse * (steered - unit * jnp.mean(steered * unit, axis=-1, keepdims=True))
    return grad, jnp.sum((upstream * unit).reshape(-1, 8, rows.shape[1]), axis=0)


def backward_kernel(
    geometry, last_call, gates, static_place, spots, meta, cotangent, incoming, hs, qs, ks, kts, vts, mids, slopes, lses,
    gain_attn, gain_ffn, *refs,
):
    rows, row_len, heads, size, segments = geometry
    spot, lengths_spot = spots
    if last_call:
        sources, refs = refs[:6], refs[6:]
        w_query, w_kv, w_out, w_up, w_down, load_sems = refs[-6:]
        refs = refs[:-6]
        weight_loads = weight_copies(sources, (w_query, w_kv, w_out, w_up, w_down), load_sems)
    else:
        w_query, w_kv, w_out, w_up, w_down = refs[:5]
        refs = refs[5:]

    def loaded(*names):
        for name in names if last_call else ():
            weight_loads[name].wait()

    refs = refs[gates:]
    count = len(BWD_SAVED) - last_call
    out, *gbs, dus, gms, dqkvs, igs, gains, carry = refs[count:2 * count + 1]
    (g_v, h_v, q_v, k_v, kt_v, vt_v, mid_v, slope_v, lse_v, du_v, gm_v, do_v, dqkv_v, ig_v, gain_v, carry_v,
     bias_v, total_v, s_v, dp_v, p_v, ds_v, sems) = refs[2 * count + 1:]
    parts = row_len // rows
    active, chunk, first = meta[spot], meta[spot + 1], meta[spot + 2]
    scale = size**-0.5
    width = heads * size

    @pl.when(active == 1)
    def _():
        row = chunk // parts
        at = pl.ds(pl.multiple_of(chunk * rows, rows), rows)
        whole = pl.ds(pl.multiple_of(row * row_len, row_len), row_len)

        @pl.when(first == 1)
        def _():
            pltpu.make_async_copy(cotangent.at[at], g_v, sems.at[0]).start()

        loads = [
            pltpu.make_async_copy(source, target, sems.at[1 + i])
            for i, (source, target) in enumerate((
                (slopes.at[at], slope_v),
                (mids.at[at], mid_v),
                (qs.at[at], q_v),
                (lses.at[at], lse_v),
                (kts.at[row], kt_v),
                (vts.at[row], vt_v),
                (ks.at[whole], k_v),
                (carry, carry_v),
                (hs.at[at], h_v),
            ))
        ]
        for load in loads[:1]:
            load.start()
        for name in BWD_LOADS[:2] if last_call else ():
            weight_loads[name].start()
        for load in loads[1:]:
            load.start()
        for name in BWD_LOADS[2:] if last_call else ():
            weight_loads[name].start()
        pending = []

        def keep(source, target, slot):
            copy = pltpu.make_async_copy(source, target, sems.at[slot])
            copy.start()
            pending.append(copy)

        length = (static_place + 1) * rows
        bias_v[:, :length] = position_bias(
            meta, lengths_spot + row * segments, segments, static_place * rows, rows, length
        )
        @pl.when(first == 1)
        def _():
            pltpu.make_async_copy(cotangent.at[at], g_v, sems.at[0]).wait()

        @pl.when(first == 0)
        def _():
            g_v[...] = incoming[...]

        if not last_call:
            keep(g_v, gbs[0].at[at], 10)
        loads[0].wait()
        ffn = w_up.shape[1]
        tile = min(BWD_TILE, ffn)

        def rise(f):
            cols = pl.ds(pl.multiple_of(f * tile, tile), tile)
            return dot_t(g_v[...], w_down[cols, :])

        def bend(f, da):
            cols = pl.ds(pl.multiple_of(f * tile, tile), tile)
            du_v[:, cols] = (slope_v[:, cols].astype(F32) * da).astype(BF16)

        def fall(f):
            cols = pl.ds(pl.multiple_of(f * tile, tile), tile)
            return dot_t(du_v[:, cols], w_up[:, cols])

        def both(f, carry):
            da = rise(f)
            part = fall(f - 1)
            bend(f, da)
            total_v[...] = jnp.where(f == 1, part, total_v[...] + part)
            return carry

        loaded("down0")
        bend(0, rise(0))
        loaded("up0", "down1")
        lax.fori_loop(1, ffn // tile, both, 0)
        loaded("up1")
        total_v[...] += fall(ffn // tile - 1)
        keep(du_v, dus.at[at], 11)
        loads[1].wait()
        gain_v[...] = jnp.zeros(gain_v.shape, F32)

        def norm_ffn(block):
            dv, dgain = norm_backward(mid_v[block, :], gain_ffn[...].astype(F32), total_v[block, :])
            dmid = g_v[block, :].astype(F32) + dv
            mid_v[block, :] = dmid
            gm_v[block, :] = dmid.astype(BF16)
            gain_v[8:, :] += dgain

        each_block(rows, NORM_BLOCK, norm_ffn, rows // NORM_BLOCK)
        keep(gm_v, gms.at[at], 12)
        loaded("out")
        do_v[...] = dot_t(gm_v[...], w_out[...]).astype(BF16)
        for load in loads[2:8]:
            load.wait()

        if static_place == parts - 1:
            carry_v[...] = jnp.zeros(carry_v.shape, F32)

        def attend():
            lane = lax.broadcasted_iota(jnp.int32, (SOFTMAX_BLOCK, size), 1)

            def some_heads(step, unused):
                group = [step * BWD_HEADS + i for i in range(BWD_HEADS)]
                for i, head in enumerate(group):
                    cols = pl.ds(pl.multiple_of(head * size, size), size)
                    s_v[i, :, :length] = dot(q_v[:, cols], kt_v[:, :length])
                    dp_v[i, :, :length] = dot(do_v[:, cols], vt_v[:, :length])
                for i, head in enumerate(group):
                    cols = pl.ds(pl.multiple_of(head * size, size), size)

                    def steepen(block, i=i, head=head):
                        lse = jnp.sum(jnp.where(lane == head, lse_v[block, :], 0.0), axis=1, keepdims=True)
                        scores = s_v[i, block, :length] * (scale * LOG2E) + bias_v[block, :length]
                        probs = jnp.exp2(scores - lse)
                        p_v[i, block, :length] = probs.astype(BF16)
                        dprobs = dp_v[i, block, :length]
                        mean = jnp.sum(probs * dprobs, axis=1, keepdims=True)
                        ds_v[i, block, :length] = (probs * (dprobs - mean)).astype(BF16)

                    each_block(rows, SOFTMAX_BLOCK, steepen, rows // SOFTMAX_BLOCK)
                    dqkv_v[:, cols] = (dot(ds_v[i, :, :length], k_v[:length, :]) * scale).astype(BF16)
                    carry_v[:size, :length] += dot(q_v[:, cols].T, ds_v[i, :, :length])
                    carry_v[size:, :length] += dot(do_v[:, cols].T, p_v[i, :, :length])
                return unused

            lax.fori_loop(0, heads // BWD_HEADS, some_heads, 0)
            own = slice(length - rows, length)
            dqkv_v[:, width:width + size] = (carry_v[:size, own].T * scale).astype(BF16)
            dqkv_v[:, width + size:] = carry_v[size:, own].T.astype(BF16)

        attend()

        keep(carry_v, carry, 13)
        keep(dqkv_v, dqkvs.at[at], 14)
        loaded("query", "key", "value")
        dn1 = dot_t(dqkv_v[:, :width], w_query[...]) + dot_t(dqkv_v[:, width:], w_kv[...])
        loads[8].wait()
        total_v[...] = dn1

        def norm_attn(block):
            dv, dgain = norm_backward(h_v[block, :].astype(F32), gain_attn[...].astype(F32), total_v[block, :])
            ig_v[block, :] = (mid_v[block, :] + dv).astype(BF16)
            gain_v[:8, :] += dgain

        each_block(rows, NORM_BLOCK, norm_attn, rows // NORM_BLOCK)
        out[...] = ig_v[...]
        keep(ig_v, igs.at[at], 16)
        keep(gain_v, gains.at[chunk], 17)
        for copy in pending:
            copy.wait()


def backward_chunk(geometry, last_call, static_place, spots, meta, cotangent, incoming, kept, weights, saved, gates=()):
    rows, row_len, heads, size, unused = geometry
    gain_attn, gain_ffn, *matrices = weights
    width = cotangent.shape[1]
    ffn = matrices[4 if last_call else 3].shape[1]
    vmem = pl.BlockSpec(memory_space=pltpu.VMEM)
    hbm = pl.BlockSpec(memory_space=pltpu.HBM)
    lead = 3 + len(kept) + len(weights) + len(gates)
    flops = 2 * rows * (2 * width * heads * size + 2 * width * size + 2 * width * ffn + 3 * row_len * heads * size)
    return pl.pallas_call(
        functools.partial(backward_kernel, geometry, last_call, len(gates), static_place, spots),
        out_shape=[jax.ShapeDtypeStruct((rows, width), BF16)]
        + [pltpu.HBM(array.shape, array.dtype) for array in saved],
        in_specs=[pl.BlockSpec(memory_space=pltpu.SMEM), hbm, vmem]
        + [hbm] * len(kept) + [vmem] * 2 + [hbm if last_call else vmem] * len(matrices)
        + [pl.BlockSpec(memory_space=pl.ANY)] * len(gates) + [hbm] * len(saved),
        out_specs=[vmem] + [hbm] * len(saved),
        input_output_aliases={lead + i: 1 + i for i in range(len(saved))},
        scratch_shapes=[
            pltpu.VMEM((rows, width), BF16),
            pltpu.VMEM((rows, width), BF16),
            pltpu.VMEM((rows, heads * size), BF16),
            pltpu.VMEM((row_len, size), BF16),
            pltpu.VMEM((size, row_len), BF16),
            pltpu.VMEM((size, row_len), BF16),
            pltpu.VMEM((rows, width), F32),
            pltpu.VMEM((rows, ffn), BF16),
            pltpu.VMEM((rows, size), F32),
            pltpu.VMEM((rows, ffn), BF16),
            pltpu.VMEM((rows, width), BF16),
            pltpu.VMEM((rows, heads * size), BF16),
            pltpu.VMEM((rows, (heads + 2) * size), BF16),
            pltpu.VMEM((rows, width), BF16),
            pltpu.VMEM((16, width), F32),
            pltpu.VMEM((2 * size, row_len), F32),
            pltpu.VMEM((rows, row_len), F32),
            pltpu.VMEM((rows, width), F32),
            pltpu.VMEM((BWD_HEADS, rows, row_len), F32),
            pltpu.VMEM((BWD_HEADS, rows, row_len), F32),
            pltpu.VMEM((BWD_HEADS, rows, row_len), BF16),
            pltpu.VMEM((BWD_HEADS, rows, row_len), BF16),
            pltpu.SemaphoreType.DMA((18,)),
        ]
        + [pltpu.VMEM(shape, BF16) for shape in (weight_shapes(matrices) if last_call else ())]
        + [pltpu.SemaphoreType.DMA((8,))] * last_call,
        compiler_params=pltpu.CompilerParams(vmem_limit_bytes=(42 if last_call else 20) * MIB),
        cost_estimate=pl.CostEstimate(
            flops=1024 if last_call else flops, bytes_accessed=1024 if last_call else 8 * MIB, transcendentals=0
        ),
        name="backward_chunk",
    )(
        meta, in_hbm(cotangent), in_vmem(incoming), *map(in_hbm, kept), gain_attn, gain_ffn,
        *map(in_hbm if last_call else in_vmem, matrices), *gates, *saved,
    )


def unwritten(shapes):
    return pl.pallas_call(
        lambda *refs: None,
        out_shape=shapes,
        out_specs=[pl.BlockSpec(memory_space=pltpu.HBM)] * len(shapes),
        compiler_params=pltpu.CompilerParams(vmem_limit_bytes=2 * MIB),
        name="unwritten",
    )()


def dest_chip(step):
    chips = lax.axis_size("dp") // 2
    return lax.rem(lax.axis_index("dp") // 2 + 2 * chips - 1 - step, chips)


def swap_cores(block):
    return lax.ppermute(block, "dp", [(i, i ^ 1) for i in range(lax.axis_size("dp"))])


def next_chip(block):
    devices = lax.axis_size("dp")
    return lax.ppermute(block, "dp", [(i, (i + 2) % devices) for i in range(devices)])


def largest_tile(width, most):
    return max(tile for tile in range(128, most + 1, 128) if width % tile == 0)


def product_kernel(pairs, offsets, gates, share, spots, meta, *refs):
    refs = refs[gates:]
    lefts, rights, refs = refs[:pairs], refs[pairs:2 * pairs], refs[2 * pairs:]
    extras = refs[:1] if pairs > 1 else ()
    refs = refs[len(extras):]
    added, refs = refs[:len(offsets)], refs[len(offsets):]
    outs, refs = refs[:len(refs) - 2 * pairs - 2], refs[len(refs) - 2 * pairs - 2:]
    lefts_v, rights_v, left_sems, right_sems = refs[:pairs], refs[pairs:2 * pairs], refs[-2], refs[-1]
    blocks = lefts_v[0].shape[0]
    left_copies, right_copies = [], []
    for i in range(pairs):
        for b in range(blocks):
            source = lefts[i]
            if source.shape[1] != share:
                source = source.at[:, pl.ds(pl.multiple_of(meta[spots[b]] * share, 128), share)]
            left_copies.append(pltpu.make_async_copy(source, lefts_v[i].at[b], left_sems.at[i * blocks + b]))
            left_copies[-1].start()
        wide = largest_tile(rights[i].shape[1], 1280)
        for n in range(rights[i].shape[1] // wide):
            cols = slice(n * wide, (n + 1) * wide)
            copy = pltpu.make_async_copy(rights[i].at[:, cols], rights_v[i].at[:, cols], right_sems.at[len(right_copies)])
            copy.start()
            right_copies.append((copy, i, n, wide))

    def put(row, depth, col, value):
        for more, offset in zip(added, offsets):
            value = value + more[offset + row:offset + row + depth, col:col + value.shape[1]].astype(F32)
        start = 0
        for out in outs:
            low, high = max(col, start), min(col + value.shape[1], start + out.shape[1])
            if low < high:
                out[row:row + depth, low - start:high - start] = value[:, low - col:high - col].astype(out.dtype)
            start += out.shape[1]

    deep = min(share, 256)
    first_col = 0
    for copy, i, n, wide in right_copies:
        copy.wait()
        for b in range(blocks):
            if n == 0:
                left_copies[i * blocks + b].wait()
            for m in range(share // deep):
                value = lax.dot_general(
                    lefts_v[i][b, :, m * deep:(m + 1) * deep], rights_v[i][:, n * wide:(n + 1) * wide],
                    (((0,), (0,)), ((), ())), preferred_element_type=F32,
                )
                put(b * share + m * deep, deep, first_col, value)
        first_col += wide
    if extras:
        for b in range(blocks):
            put(b * share, share, first_col, extras[0][pl.ds(pl.multiple_of(meta[spots[b]] * share, 8), share), :])


def products(share, spots, meta, lefts, rights, extra, added, dtype, gates, widths, cost):
    vmem = pl.BlockSpec(memory_space=pltpu.VMEM)
    hbm = pl.BlockSpec(memory_space=pltpu.HBM)
    count = len(spots)
    if share % 128:
        blocks = [[lax.dynamic_slice_in_dim(left, meta[spot] * share, share, 1) for spot in spots] for left in lefts]
        if count > 1:
            parts = [
                products(
                    share, spots[b:b + 1], meta, lefts, rights, extra, [(more, at + b * share) for more, at in added], dtype,
                    gates, widths, cost,
                )
                for b in range(count)
            ]
            return [jnp.concatenate(part, axis=0) for part in zip(*parts)]
        lefts = [block[0] for block in blocks]
    depth = lefts[0].shape[0]
    extras = [] if extra is None else [extra]
    total = sum(right.shape[1] for right in rights) + sum(more.shape[1] for more in extras)
    return pl.pallas_call(
        functools.partial(product_kernel, len(lefts), tuple(at for unused, at in added), len(gates), share, spots),
        out_shape=[jax.ShapeDtypeStruct((count * share, width), dtype) for width in widths or [total]],
        in_specs=[pl.BlockSpec(memory_space=pltpu.SMEM)] + [pl.BlockSpec(memory_space=pl.ANY)] * len(gates)
        + [hbm] * (2 * len(lefts)) + [vmem] * (len(extras) + len(added)),
        out_specs=[vmem] * len(widths or [total]),
        scratch_shapes=[pltpu.VMEM((count, depth, share), BF16) for _ in lefts]
        + [pltpu.VMEM(right.shape, BF16) for right in rights]
        + [pltpu.SemaphoreType.DMA((len(lefts) * count,)), pltpu.SemaphoreType.DMA((8,))],
        compiler_params=pltpu.CompilerParams(vmem_limit_bytes=24 * MIB),
        cost_estimate=pl.CostEstimate(flops=cost, bytes_accessed=1024, transcendentals=0),
        name="products",
    )(
        meta, *gates, *map(in_hbm, lefts), *map(in_hbm, rights), *extras,
        *(more for more, unused in added),
    )


def add_kernel(offset, kept, come, *outs):
    start = 0
    for out in outs:
        cols = slice(start, start + out.shape[1])
        out[...] = (kept[offset:offset + out.shape[0], cols].astype(F32) + come[:, cols].astype(F32)).astype(out.dtype)
        start += out.shape[1]


def add(kept, offset, come, dtype, widths):
    vmem = pl.BlockSpec(memory_space=pltpu.VMEM)
    return pl.pallas_call(
        functools.partial(add_kernel, offset),
        out_shape=[jax.ShapeDtypeStruct((come.shape[0], width), dtype) for width in widths or [come.shape[1]]],
        in_specs=[vmem, vmem],
        out_specs=[vmem] * len(widths or [1]),
        compiler_params=pltpu.CompilerParams(vmem_limit_bytes=4 * MIB),
        cost_estimate=pl.CostEstimate(flops=10**11, bytes_accessed=1024, transcendentals=0),
        name="add",
    )(kept, come)


class RowSums:
    def __init__(self, meta, spot, lefts, rights, extra=None):
        self.meta, self.spot, self.lefts, self.rights, self.extra = meta, spot, lefts, rights, extra
        self.share = lefts[0].shape[1] // lax.axis_size("dp")

    def blocks(self, steps, half, gates, added, dtype, cost):
        spots = [self.spot + 2 * step + half for step in steps]
        return products(self.share, spots, self.meta, self.lefts, self.rights, self.extra, added, dtype, gates, None, cost)

    def other(self, steps, gates=(), cost=LIGHT):
        return self.blocks(steps, 1, gates, [], BF16, cost)[0]

    def own(self, steps, gates, added, dtype=BF16, cost=LIGHT):
        return self.blocks(steps, 0, gates, added, dtype, cost)[0]


def keep_last_kernel(rows, spot, meta, incoming, unused, gbs, sem):
    @pl.when(meta[spot] == 1)
    def _():
        at = pl.ds(pl.multiple_of(meta[spot + 1] * rows, rows), rows)
        copy = pltpu.make_async_copy(incoming, gbs.at[at], sem)
        copy.start()
        copy.wait()


def keep_last(spot, meta, incoming, gbs):
    anywhere = pl.BlockSpec(memory_space=pltpu.HBM)
    return pl.pallas_call(
        functools.partial(keep_last_kernel, incoming.shape[0], spot),
        out_shape=pltpu.HBM(gbs.shape, gbs.dtype),
        in_specs=[pl.BlockSpec(memory_space=pltpu.SMEM), pl.BlockSpec(memory_space=pl.ANY), anywhere],
        out_specs=anywhere,
        input_output_aliases={2: 0},
        scratch_shapes=[pltpu.SemaphoreType.DMA],
        compiler_params=pltpu.CompilerParams(vmem_limit_bytes=2 * MIB),
        name="keep_last",
    )(meta, incoming, gbs)


def body(
    tokens, lengths, gain_attn, w_query, w_key, w_value, w_out, gain_ffn, w_up, w_down, cotangent
):
    micro, row_len, width = tokens.shape
    size = w_key.shape[2]
    heads = w_query.shape[2] // size
    ffn = w_up.shape[2]
    count = micro * row_len
    sections = lax.axis_size("section")
    place = lax.axis_index("section")
    gains = [gain_attn, gain_ffn]
    given = [w_query[0], w_key[0], w_value[0], w_out[0], w_up[0], w_down[0]]
    weights = gains
    token_rows = tokens.reshape(count, width)
    cotangent_rows = cotangent.reshape(count, width)
    segments = lengths.shape[2]

    def empty(*shape, dtype=BF16):
        return pltpu.HBM(shape, dtype)

    def meta_of(tick, chunks, rank, order):
        step = tick - SKEW * rank
        active = (step >= 0) & (step < chunks)
        return [active, order(jnp.clip(step, 0, chunks - 1)), rank == 0]

    def hop(block, tick, chunks, rank_of, shift):
        route = [
            (s, s + shift)
            for s in range(sections)
            if 0 <= s + shift < sections and 0 <= tick - SKEW * rank_of(s) < chunks
        ]
        return lax.ppermute(block, "section", route) if route else None

    fwd_geometry = (FWD_ROWS, row_len, heads, size, segments)
    fwd_chunks = count // FWD_ROWS
    fwd_ticks = fwd_chunks + SKEW * (sections - 1)
    bwd_geometry = (BWD_ROWS, row_len, heads, size, segments)
    bwd_chunks = count // BWD_ROWS
    bwd_ticks = bwd_chunks + SKEW * (sections - 1)
    parts = row_len // BWD_ROWS
    chips = lax.axis_size("dp") // 2
    core = lax.axis_index("dp") % 2
    meta = []
    for tick in range(fwd_ticks):
        meta += meta_of(tick, fwd_chunks, place, lambda step: step)
    for tick in range(bwd_ticks):
        meta += meta_of(
            tick, bwd_chunks, sections - 1 - place, lambda step: step // parts * parts + parts - 1 - step % parts
        )
    for step in range(chips):
        meta += [dest_chip(step) * 2 + core, dest_chip(step) * 2 + 1 - core]
    blocks_spot = 3 * (fwd_ticks + bwd_ticks)
    lengths_spot = len(meta)
    meta = jnp.concatenate([jnp.stack([jnp.asarray(entry, jnp.int32) for entry in meta]), lengths.reshape(-1)])
    saved = [
        empty(count, width), empty(count, width), empty(count, heads * size), empty(count, size), empty(count, size),
        empty(micro, size, row_len), empty(micro, size, row_len), empty(count, heads * size),
        empty(count, width, dtype=F32), empty(count, width), empty(count, ffn), empty(count, ffn),
        empty(count, size, dtype=F32), empty(count, width),
    ]
    saved = unwritten(saved)
    received = {}
    nothing = jnp.zeros((FWD_ROWS, width), BF16)
    for tick in range(fwd_ticks):
        incoming = received.pop(tick - SKEW, None)
        at_work = [tick - SKEW * s for s in range(sections) if 0 <= tick - SKEW * s < fwd_chunks]
        places = sorted({chunk % (row_len // FWD_ROWS) for chunk in at_work})
        out, saved, loads = forward_chunk(
            fwd_geometry, places, (3 * tick, lengths_spot), meta, token_rows, nothing if incoming is None else incoming, weights, saved,
            None if tick else given,
        )
        weights = weights + loads
        received[tick] = hop(out, tick, fwd_chunks, lambda s: s, 1)

    kept = dict(zip(FWD_SAVED, saved))
    layer_outs = kept["outs"]
    needed = [kept[name] for name in ("hs", "qs", "ks", "kts", "vts", "mids", "slopes", "lses")]
    saved = unwritten([
        empty(count, width), empty(count, ffn), empty(count, width), empty(count, (heads + 2) * size),
        empty(count, width), empty(bwd_chunks, 16, width, dtype=F32), empty(2 * size, row_len, dtype=F32),
    ])
    received = {}
    nothing = jnp.zeros((BWD_ROWS, width), BF16)
    down_sums = None
    for tick in range(bwd_ticks):
        spot = 3 * (fwd_ticks + tick)
        static_place = parts - 1 - tick % parts
        incoming = received.pop(tick - SKEW, None)
        if incoming is None:
            incoming = nothing
        if tick == bwd_ticks - 1:
            gbs = keep_last(spot, meta, incoming, saved[0])
            down_sums = RowSums(meta, blocks_spot, [kept["acts"]], [gbs])
            swapped = swap_cores(down_sums.other([0]))
            first_total = down_sums.own([0], (), [(swapped, 0)])
            down_ring = next_chip(first_total)
            ready = down_sums.other([1], [first_total])
            swapped = swap_cores(ready)
            out, *rest = backward_chunk(
                bwd_geometry, True, static_place, (spot, lengths_spot), meta, cotangent_rows, incoming, needed, gains + given, saved[1:],
                [first_total, ready],
            )
            saved = [gbs] + rest
            continue
        out, *saved = backward_chunk(
            bwd_geometry, False, static_place, (spot, lengths_spot), meta, cotangent_rows, incoming, needed, weights, saved
        )
        received[tick] = hop(out, tick, bwd_chunks, lambda s: sections - 1 - s, -1)
    done = dict(zip(BWD_SAVED, saved))

    gains = jnp.sum(done["gains"].reshape(bwd_chunks, 2, 8, width), axis=(0, 2))
    gains = jnp.pad(gains.T, ((0, 0), (0, 128 - gains.shape[0])))
    rest_sums = RowSums(
        meta, blocks_spot, [kept["n2s"], kept["n1s"], kept["os"]], [done["dus"], done["dqkvs"], done["gms"]], gains
    )
    later = list(range(1, chips))
    widths = [ffn, heads * size, size, size, width, 128]

    rest_other = rest_sums.other([0])
    down = down_sums.own([1], [rest_other], [(swapped, 0), (down_ring, 0)], BF16 if chips > 2 else F32)
    if chips > 2:
        down_ring = next_chip(down)
    swapped = swap_cores(rest_other)
    down_others = down_sums.other(later[1:], [down]) if chips > 2 else None
    rest = rest_sums.own([0], [down] if down_others is None else [down_others], [(swapped, 0)], cost=HEAVY)
    rest_ring = next_chip(rest)
    if chips > 2:
        down_swapped = swap_cores(down_others)
    if chips > 2:
        down_kept = down_sums.own(later[1:], [rest], [(down_swapped, 0)], cost=HEAVY)
    rest_others = rest_sums.other(later, [rest, down_ring], cost=HEAVY)
    rest_swapped = swap_cores(rest_others)
    rest_kept = None
    for step in range(1, chips):
        if step + 1 < chips:
            last = step + 1 == chips - 1
            down = add(down_kept, (step - 1) * down_sums.share, down_ring, F32 if last else BF16, None)[0]
            if not last:
                down_ring = next_chip(down)
        if rest_kept is None:
            rest_kept = rest_sums.own(later, [down], [(rest_swapped, 0)], cost=HEAVY)
        last = step == chips - 1
        rest = add(
            rest_kept, (step - 1) * rest_sums.share, rest_ring, F32 if last else BF16, widths if last else None
        )
        if not last:
            rest_ring = next_chip(rest[0])
    up, query, key, value, out, gains = rest
    shares = (gains[:, 0], query, key, value, out, gains[:, 1], up, down)
    shape = (1, micro, row_len, width)
    return (layer_outs.reshape(shape), done["igs"].reshape(shape)) + tuple(share[None] for share in shares)


def solution(mesh):
    return jax.shard_map(
        body,
        mesh=mesh,
        in_specs=(
            P(None, "dp", None),
            P(None, "dp", None),
            P("section", None),
            P("section", None, None),
            P("section", None, None),
            P("section", None, None),
            P("section", None, None),
            P("section", None),
            P("section", None, None),
            P("section", None, None),
            P(None, "dp", None),
        ),
        out_specs=(
            P("section", None, "dp", None),
            P("section", None, "dp", None),
            P("section", "dp"),
            P("section", "dp", None),
            P("section", "dp", None),
            P("section", "dp", None),
            P("section", "dp", None),
            P("section", "dp"),
            P("section", "dp", None),
            P("section", "dp", None),
        ),
        check_vma=False,
    )
```

time: 549 us -> 499 us (0.909)
  local copies, waits for them, and re-layouts: 24.9 us -> 6.12 us
  Pallas kernels: 284 us -> 266 us
  waiting for transfers between devices: 199 us -> 189 us
    unnamed x50 -> x17, local copies, waits for them, and re-layouts: 23.9 us -> 2.98 us
    ppermute x20, waiting for transfers between devices: 93 us -> 77.6 us  [hop(): return lax.ppermute(block, 'section', route) if route else None]
    pallas_call x16 -> x15, Pallas kernels: 116 us -> 104 us  [the longest x14 103 us: forward_chunk(): pl.pallas_call(functools.partial(forward_kernel, geometry, loading, place...]
  transfers between devices with their start and end apart: 31 -> 31, of which waited for: 8 -> 9; matrix products, arithmetic and copies ran while one was open for 1% -> 1% of each run, Pallas kernels for 43% -> 46%
where the time goes in v3:
time: 499 us; the launch traced here: 490 us
  Pallas kernels  266 us (53%)
  waiting for transfers between devices  189 us (38%)
  starting transfers between devices  24.8 us (5%)
  local copies, waits for them, and re-layouts  6.12 us (1%)
    ppermute x6, waiting for transfers between devices, next_chip(): lax.ppermute(block, 'dp', [(i, (i + 2) % devices) for i in range(devices)])  108 us
    pallas_call x14, Pallas kernels, forward_chunk(): pl.pallas_call(functools.partial(forward_kernel, geometry, loading, place...  103 us
    pallas_call x10, Pallas kernels, backward_chunk(): pl.pallas_call(functools.partial(backward_kernel, geometry, last_call, le...  87 us
    ppermute x20, waiting for transfers between devices, hop(): return lax.ppermute(block, 'section', route) if route else None  77.6 us
    pallas_call x10, Pallas kernels, products(): pl.pallas_call(functools.partial(product_kernel, len(lefts), tuple((at fo...  68.4 us
    ppermute x20, starting transfers between devices, hop(): return lax.ppermute(block, 'section', route) if route else None  21.1 us
  transfers between devices with their start and end apart: 31, of which 9 were waited for; matrix products, arithmetic and copies ran while one was open for 1% of the time, Pallas kernels for 46%

profile of v3, /device:TPU:0, one launch (start us, length us, event | category | flops | bytes accessed | tf_op | source)
XLA Modules:
  0.0 489.8 jit_solution(9556976825682769831)
XLA Ops:
  4.6 15.1 %forward_chunk.14 = (bf16[128,1024]{1,0:T(8,128)(2,1)S(1)}, bf16[1024,1024]{1,0:T(8,128)(2,1)}, bf16[1024,1024]{1,0:T(8,128)(2,1)}, bf16[1024,1024]{1,0:T(8,128)...) custom-call(s32[112]{0:T(128)S(1)} %concatenate.3.meta, ...), custom_call_target="tpu_custom_call", output_to_operand_aliasing={{1}: (11, {}), {2}: (12, {}), {3}: (13, {}), {4}: (14, {}),... | custom-call | flops 2885681152 | bytes 8388608 | tf_op jit(solution)/shard_map/forward_chunk/pallas_call | solution.py:303
  21.0 8.6 %forward_chunk.15 = (bf16[128,1024]{1,0:T(8,128)(2,1)S(1)}, bf16[1024,1024]{1,0:T(8,128)(2,1)}, bf16[1024,1024]{1,0:T(8,128)(2,1)}, bf16[1024,1024]{1,0:T(8,128)...) custom-call(s32[112]{0:T(128)S(1)} %concatenate.3.meta, ...), custom_call_target="tpu_custom_call", output_to_operand_aliasing={{1}: (10, {}), {2}: (11, {}), {3}: (12, {}), {4}: (13, {}),... | custom-call | flops 2885681152 | bytes 8388608 | tf_op jit(solution)/shard_map/forward_chunk/pallas_call | solution.py:303
  30.9 10.9 %forward_chunk.16 = (bf16[128,1024]{1,0:T(8,128)(2,1)S(1)}, bf16[1024,1024]{1,0:T(8,128)(2,1)}, bf16[1024,1024]{1,0:T(8,128)(2,1)}, bf16[1024,1024]{1,0:T(8,128)...) custom-call(s32[112]{0:T(128)S(1)} %concatenate.3.meta, ...), custom_call_target="tpu_custom_call", output_to_operand_aliasing={{1}: (10, {}), {2}: (11, {}), {3}: (12, {}), {4}: (13, {}),... | custom-call | flops 2885681152 | bytes 8388608 | tf_op jit(solution)/shard_map/forward_chunk/pallas_call | solution.py:303
  43.2 8.9 %forward_chunk.17 = (bf16[128,1024]{1,0:T(8,128)(2,1)S(1)}, bf16[1024,1024]{1,0:T(8,128)(2,1)}, bf16[1024,1024]{1,0:T(8,128)(2,1)}, bf16[1024,1024]{1,0:T(8,128)...) custom-call(s32[112]{0:T(128)S(1)} %concatenate.3.meta, ...), custom_call_target="tpu_custom_call", output_to_operand_aliasing={{1}: (10, {}), {2}: (11, {}), {3}: (12, {}), {4}: (13, {}),... | custom-call | flops 2885681152 | bytes 8388608 | tf_op jit(solution)/shard_map/forward_chunk/pallas_call | solution.py:303
  53.5 8.6 %forward_chunk.18 = (bf16[128,1024]{1,0:T(8,128)(2,1)S(1)}, bf16[1024,1024]{1,0:T(8,128)(2,1)}, bf16[1024,1024]{1,0:T(8,128)(2,1)}, bf16[1024,1024]{1,0:T(8,128)...) custom-call(s32[112]{0:T(128)S(1)} %concatenate.3.meta, ...), custom_call_target="tpu_custom_call", output_to_operand_aliasing={{1}: (10, {}), {2}: (11, {}), {3}: (12, {}), {4}: (13, {}),... | custom-call | flops 2885681152 | bytes 8388608 | tf_op jit(solution)/shard_map/forward_chunk/pallas_call | solution.py:303
  63.4 10.4 %forward_chunk.19 = (bf16[128,1024]{1,0:T(8,128)(2,1)S(1)}, bf16[1024,1024]{1,0:T(8,128)(2,1)}, bf16[1024,1024]{1,0:T(8,128)(2,1)}, bf16[1024,1024]{1,0:T(8,128)...) custom-call(s32[112]{0:T(128)S(1)} %concatenate.3.meta, ...), custom_call_target="tpu_custom_call", output_to_operand_aliasing={{1}: (10, {}), {2}: (11, {}), {3}: (12, {}), {4}: (13, {}),... | custom-call | flops 2885681152 | bytes 8388608 | tf_op jit(solution)/shard_map/forward_chunk/pallas_call | solution.py:303
  75.1 8.9 %forward_chunk.20 = (bf16[128,1024]{1,0:T(8,128)(2,1)S(1)}, bf16[1024,1024]{1,0:T(8,128)(2,1)}, bf16[1024,1024]{1,0:T(8,128)(2,1)}, bf16[1024,1024]{1,0:T(8,128)...) custom-call(s32[112]{0:T(128)S(1)} %concatenate.3.meta, ...), custom_call_target="tpu_custom_call", output_to_operand_aliasing={{1}: (10, {}), {2}: (11, {}), {3}: (12, {}), {4}: (13, {}),... | custom-call | flops 2885681152 | bytes 8388608 | tf_op jit(solution)/shard_map/forward_chunk/pallas_call | solution.py:303
  85.4 8.9 %forward_chunk.21 = (bf16[128,1024]{1,0:T(8,128)(2,1)S(1)}, bf16[1024,1024]{1,0:T(8,128)(2,1)}, bf16[1024,1024]{1,0:T(8,128)(2,1)}, bf16[1024,1024]{1,0:T(8,128)...) custom-call(s32[112]{0:T(128)S(1)} %concatenate.3.meta, ...), custom_call_target="tpu_custom_call", output_to_operand_aliasing={{1}: (10, {}), {2}: (11, {}), {3}: (12, {}), {4}: (13, {}),... | custom-call | flops 2885681152 | bytes 8388608 | tf_op jit(solution)/shard_map/forward_chunk/pallas_call | solution.py:303
  95.6 9.2 %forward_chunk.22 = (bf16[128,1024]{1,0:T(8,128)(2,1)S(1)}, bf16[1024,1024]{1,0:T(8,128)(2,1)}, bf16[1024,1024]{1,0:T(8,128)(2,1)}, bf16[1024,1024]{1,0:T(8,128)...) custom-call(s32[112]{0:T(128)S(1)} %concatenate.3.meta, ...), custom_call_target="tpu_custom_call", output_to_operand_aliasing={{1}: (10, {}), {2}: (11, {}), {3}: (12, {}), {4}: (13, {}),... | custom-call | flops 2885681152 | bytes 8388608 | tf_op jit(solution)/shard_map/forward_chunk/pallas_call | solution.py:303
  108.4 8.9 %forward_chunk.25 = (bf16[128,1024]{1,0:T(8,128)(2,1)S(1)}, bf16[1024,1024]{1,0:T(8,128)(2,1)}, bf16[1024,1024]{1,0:T(8,128)(2,1)}, bf16[1024,1024]{1,0:T(8,128)...) custom-call(s32[112]{0:T(128)S(1)} %concatenate.3.meta, ...), custom_call_target="tpu_custom_call", output_to_operand_aliasing={{1}: (10, {}), {2}: (11, {}), {3}: (12, {}), {4}: (13, {}),... | custom-call | flops 2885681152 | bytes 8388608 | tf_op jit(solution)/shard_map/forward_chunk/pallas_call | solution.py:303
  121.0 7.1 %backward_chunk.10 = (bf16[256,1024]{1,0:T(8,128)(2,1)S(1)}, bf16[1024,1024]{1,0:T(8,128)(2,1)}, bf16[1024,4096]{1,0:T(8,128)(2,1)}, bf16[1024,1024]{1,0:T(8,128...) custom-call(s32[112]{0:T(128)S(1)} %concatenate.3.meta, ...), custom_call_target="tpu_custom_call", output_to_operand_aliasing={{1}: (18, {}), {2}: (19, {}), {3}: (20, {}), {4}: (21, {}),... | custom-call | flops 6308233216 | bytes 8388608 | tf_op jit(solution)/shard_map/backward_chunk/pallas_call | solution.py:551
  130.3 8.8 %backward_chunk.12 = (bf16[256,1024]{1,0:T(8,128)(2,1)S(1)}, bf16[1024,1024]{1,0:T(8,128)(2,1)}, bf16[1024,4096]{1,0:T(8,128)(2,1)}, bf16[1024,1024]{1,0:T(8,128...) custom-call(s32[112]{0:T(128)S(1)} %concatenate.3.meta, ...), custom_call_target="tpu_custom_call", output_to_operand_aliasing={{1}: (18, {}), {2}: (19, {}), {3}: (20, {}), {4}: (21, {}),... | custom-call | flops 6308233216 | bytes 8388608 | tf_op jit(solution)/shard_map/backward_chunk/pallas_call | solution.py:551
  141.3 8.6 %backward_chunk.14 = (bf16[256,1024]{1,0:T(8,128)(2,1)S(1)}, bf16[1024,1024]{1,0:T(8,128)(2,1)}, bf16[1024,4096]{1,0:T(8,128)(2,1)}, bf16[1024,1024]{1,0:T(8,128...) custom-call(s32[112]{0:T(128)S(1)} %concatenate.3.meta, ...), custom_call_target="tpu_custom_call", output_to_operand_aliasing={{1}: (18, {}), {2}: (19, {}), {3}: (20, {}), {4}: (21, {}),... | custom-call | flops 6308233216 | bytes 8388608 | tf_op jit(solution)/shard_map/backward_chunk/pallas_call | solution.py:551
  153.3 76.9 %collective-permute-done.17.incoming = bf16[256,1024]{1,0:T(8,128)(2,1)S(1)} collective-permute-done((bf16[256,1024]{1,0:T(8,128)(2,1)S(1)}, bf16[256,1024]{1,0:T(8,128)(2,1)S(1)}, u32[]{:S(2)}, u32[]{:S(2)}) %collective-permute-start.17) | collective-permute-done | bytes 524320 | tf_op jit(solution)/shard_map/ppermute | solution.py:807
  230.1 14.7 %backward_chunk.16 = (bf16[256,1024]{1,0:T(8,128)(2,1)S(1)}, bf16[1024,1024]{1,0:T(8,128)(2,1)}, bf16[1024,4096]{1,0:T(8,128)(2,1)}, bf16[1024,1024]{1,0:T(8,128...) custom-call(s32[112]{0:T(128)S(1)} %concatenate.3.meta, ...), custom_call_target="tpu_custom_call", output_to_operand_aliasing={{1}: (18, {}), {2}: (19, {}), {3}: (20, {}), {4}: (21, {}),... | custom-call | flops 6308233216 | bytes 8388608 | tf_op jit(solution)/shard_map/backward_chunk/pallas_call | solution.py:551
  246.2 13.0 %backward_chunk.17 = (bf16[256,1024]{1,0:T(8,128)(2,1)S(1)}, bf16[1024,1024]{1,0:T(8,128)(2,1)}, bf16[1024,4096]{1,0:T(8,128)(2,1)}, bf16[1024,1024]{1,0:T(8,128...) custom-call(s32[112]{0:T(128)S(1)} %concatenate.3.meta, ...), custom_call_target="tpu_custom_call", output_to_operand_aliasing={{1}: (18, {}), {2}: (19, {}), {3}: (20, {}), {4}: (21, {}),... | custom-call | flops 6308233216 | bytes 8388608 | tf_op jit(solution)/shard_map/backward_chunk/pallas_call | solution.py:551
  261.2 15.2 %backward_chunk.18 = (bf16[256,1024]{1,0:T(8,128)(2,1)}, bf16[1024,1024]{1,0:T(8,128)(2,1)}, bf16[1024,4096]{1,0:T(8,128)(2,1)}, bf16[1024,1024]{1,0:T(8,128)(2,...) custom-call(s32[112]{0:T(128)S(1)} %concatenate.3.meta, ...), custom_call_target="tpu_custom_call", output_to_operand_aliasing={{1}: (18, {}), {2}: (19, {}), {3}: (20, {}), {4}: (21, {}),... | custom-call | flops 6308233216 | bytes 8388608 | tf_op jit(solution)/shard_map/backward_chunk/pallas_call | solution.py:551
  277.8 3.8 products.10
  284.3 3.8 products.11.refs_0_.refs_6_
  288.0 3.8 products.12.refs_7_
  292.1 17.3 %backward_chunk.19 = (bf16[256,1024]{1,0:T(8,128)(2,1)}, bf16[1024,4096]{1,0:T(8,128)(2,1)}, bf16[1024,1024]{1,0:T(8,128)(2,1)}, bf16[1024,1280]{1,0:T(8,128)(2,...) custom-call(s32[112]{0:T(128)S(1)} %concatenate.3.meta, ...), custom_call_target="tpu_custom_call", output_to_operand_aliasing={{1}: (21, {}), {2}: (22, {}), {3}: (23, {}), {4}: (24, {}),... | custom-call | flops 1024 | bytes 1024 | tf_op jit(solution)/shard_map/backward_chunk/pallas_call | solution.py:551
  312.5 6.5 %products.13.refs_0_ = bf16[128,6528]{1,0:T(8,128)(2,1)S(1)} custom-call(s32[112]{0:T(128)S(1)} %concatenate.3.meta, bf16[1024,1024]{1,0:T(8,128)(2,1)} %get-tuple-element.627.refs_0_.refs_1_.refs_2_, bf16[1024,1024]{1,0:T(8,128)(2,1)} %get-tuple-element.628.refs_1_.refs_2_.refs_3_, bf16[1024,1024]{1,0:T(8,128)(2,1)} %get-tuple-element.629.refs_2_.refs_3_.refs_4_, ...), custom_call_target="tpu_custom_call" | custom-call | flops 5000000000 | bytes 1024 | tf_op jit(solution)/shard_map/products/pallas_call | solution.py:698
  319.5 4.6 products.14.refs_0_
  324.6 6.8 %products.15.refs_0_ = bf16[1024,1024]{1,0:T(8,128)(2,1)} custom-call(s32[112]{0:T(128)S(1)} %concatenate.3.meta, bf16[512,1024]{1,0:T(8,128)(2,1)S(1)} %products.14.refs_0_, bf16[1024,4096]{1,0:T(8,128)(2,1)} %get-tuple-element.610.refs_0_.refs_1_, bf16[1024,1024]{1,0:T(8,128)(2,1)} %keep_last.1.refs_1_.refs_2_), custom_call_target="tpu_custom_call" | custom-call | flops 5000000000 | bytes 1024 | tf_op jit(solution)/shard_map/products/pallas_call | solution.py:698
  331.4 7.7 %products.16.refs_0_ = bf16[128,6528]{1,0:T(8,128)(2,1)} custom-call(s32[112]{0:T(128)S(1)} %concatenate.3.meta, bf16[1024,1024]{1,0:T(8,128)(2,1)} %products.15.refs_0_, bf16[1024,1024]{1,0:T(8,128)(2,1)} %get-tuple-element.627.refs_0_.refs_1_.refs_2_, bf16[1024,1024]{1,0:T(8,128)(2,1)} %get-tuple-element.628.refs_1_.refs_2_.refs_3_, ...), custom_call_target="tpu_custom_call" | custom-call | flops 99999997952 | bytes 1024 | tf_op jit(solution)/shard_map/products/pallas_call | solution.py:698
  340.9 10.9 %collective-permute-done.25.come.refs_1_ = bf16[512,1024]{1,0:T(8,128)(2,1)S(1)} collective-permute-done((bf16[512,1024]{1,0:T(8,128)(2,1)S(1)}, bf16[512,1024]{1,0:T(8,128)(2,1)S(1)}, u32[]{:S(2)}, u32[]{:S(2)}) %collective-permute-start.25) | collective-permute-done | bytes 1048608 | tf_op jit(solution)/shard_map/ppermute | solution.py:619
  351.9 12.7 %products.18 = bf16[384,6528]{1,0:T(8,128)(2,1)} custom-call(s32[112]{0:T(128)S(1)} %concatenate.3.meta, bf16[128,6528]{1,0:T(8,128)(2,1)} %products.16.refs_0_, bf16[512,1024]{1,0:T(8,128)(2,1)S(1)} %collective-permute-done.25.come.refs_1_, bf16[1024,1024]{1,0:T(8,128)(2,1)} %get-tuple-element.627.refs_0_.refs_1_.refs_2_, ...), custom_call_target="tpu_custom_call" | custom-call | flops 99999997952 | bytes 1024 | tf_op jit(solution)/shard_map/products/pallas_call | solution.py:698
  364.7 6.5 %products.17.kept = bf16[1024,1024]{1,0:T(8,128)(2,1)S(1)} custom-call(s32[112]{0:T(128)S(1)} %concatenate.3.meta, bf16[128,6528]{1,0:T(8,128)(2,1)} %products.16.refs_0_, bf16[1024,4096]{1,0:T(8,128)(2,1)} %get-tuple-element.610.refs_0_.refs_1_, bf16[1024,1024]{1,0:T(8,128)(2,1)} %keep_last.1.refs_1_.refs_2_, bf16[1024,1024]{1,0:T(8,128)(2,1)} %collective-permute-done.24.refs_3_), custom_call_target="tpu_custom_call" | custom-call | flops 99999997952 | bytes 1024 | tf_op jit(solution)/shard_map/products/pallas_call | solution.py:698
  373.3 12.4 %products.19.kept = bf16[384,6528]{1,0:T(8,128)(2,1)S(1)} custom-call(s32[112]{0:T(128)S(1)} %concatenate.3.meta, bf16[512,1024]{1,0:T(8,128)(2,1)S(1)} %add.161.refs_0_, bf16[1024,1024]{1,0:T(8,128)(2,1)} %get-tuple-element.627.refs_0_.refs_1_.refs_2_, bf16[1024,1024]{1,0:T(8,128)(2,1)} %get-tuple-element.628.refs_1_.refs_2_.refs_3_, ...), custom_call_target="tpu_custom_call" | custom-call | flops 99999997952 | bytes 1024 | tf_op jit(solution)/shard_map/products/pallas_call | solution.py:698
  389.4 40.8 %collective-permute-done.28.come = bf16[128,6528]{1,0:T(8,128)(2,1)S(1)} collective-permute-done((bf16[128,6528]{1,0:T(8,128)(2,1)S(1)}, bf16[128,6528]{1,0:T(8,128)(2,1)S(1)}, u32[]{:S(2)}, u32[]{:S(2)}) %collective-permute-start.28) | collective-permute-done | bytes 1671200 | tf_op jit(solution)/shard_map/ppermute | solution.py:619
  430.7 22.0 %collective-permute-done.30.come = bf16[512,1024]{1,0:T(8,128)(2,1)S(1)} collective-permute-done((bf16[512,1024]{1,0:T(8,128)(2,1)S(1)}, bf16[512,1024]{1,0:T(8,128)(2,1)S(1)}, u32[]{:S(2)}, u32[]{:S(2)}) %collective-permute-start.30) | collective-permute-done | bytes 1048608 | tf_op jit(solution)/shard_map/ppermute | solution.py:619
  454.3 32.7 %collective-permute-done.29.come = bf16[128,6528]{1,0:T(8,128)(2,1)S(1)} collective-permute-done((bf16[128,6528]{1,0:T(8,128)(2,1)S(1)}, bf16[128,6528]{1,0:T(8,128)(2,1)S(1)}, u32[]{:S(2)}, u32[]{:S(2)}) %collective-permute-start.29) | collective-permute-done | bytes 1671200 | tf_op jit(solution)/shard_map/ppermute | solution.py:619
  (99 shorter events, 52.8 us)
Async XLA Ops:
  19.7 11.2 %collective-permute-start.1 = (bf16[128,1024]{1,0:T(8,128)(2,1)S(1)}, bf16[128,1024]{1,0:T(8,128)(2,1)S(1)}, u32[]{:S(2)}, u32[]{:S(2)}) collective-permute-start(bf16[128,1024]{1,0:T(8,128)(2,1)S(1)} %get-tuple-element.359), channel_id=1, source_target_pairs={{0,8},{1,9},{2,10},{3,11},{4,12},{5,13},{6,14},{7,15}} | collective-permute-start | bytes 786440 | tf_op jit(solution)/shard_map/ppermute | solution.py:807
  29.6 13.6 %collective-permute-start = (bf16[128,1024]{1,0:T(8,128)(2,1)S(1)}, bf16[128,1024]{1,0:T(8,128)(2,1)S(1)}, u32[]{:S(2)}, u32[]{:S(2)}) collective-permute-start(bf16[128,1024]{1,0:T(8,128)(2,1)S(1)} %get-tuple-element.358), channel_id=1, source_target_pairs={{0,8},{1,9},{2,10},{3,11},{4,12},{5,13},{6,14},{7,15}} | collective-permute-start | bytes 786440 | tf_op jit(solution)/shard_map/ppermute | solution.py:807
  41.9 11.6 %collective-permute-start.3 = (bf16[128,1024]{1,0:T(8,128)(2,1)S(1)}, bf16[128,1024]{1,0:T(8,128)(2,1)S(1)}, u32[]{:S(2)}, u32[]{:S(2)}) collective-permute-start(bf16[128,1024]{1,0:T(8,128)(2,1)S(1)} %get-tuple-element.389), channel_id=1, source_target_pairs={{0,8},{8,16},{1,9},{9,17},{2,10},{10,18},{3,11},{11,19},{4,12},{12... | collective-permute-start | bytes 786440 | tf_op jit(solution)/shard_map/ppermute | solution.py:807
  52.1 11.2 %collective-permute-start.2 = (bf16[128,1024]{1,0:T(8,128)(2,1)S(1)}, bf16[128,1024]{1,0:T(8,128)(2,1)S(1)}, u32[]{:S(2)}, u32[]{:S(2)}) collective-permute-start(bf16[128,1024]{1,0:T(8,128)(2,1)S(1)} %get-tuple-element.388), channel_id=1, source_target_pairs={{0,8},{8,16},{1,9},{9,17},{2,10},{10,18},{3,11},{11,19},{4,12},{12... | collective-permute-start | bytes 786440 | tf_op jit(solution)/shard_map/ppermute | solution.py:807
  62.1 13.1 %collective-permute-start.5 = (bf16[128,1024]{1,0:T(8,128)(2,1)S(1)}, bf16[128,1024]{1,0:T(8,128)(2,1)S(1)}, u32[]{:S(2)}, u32[]{:S(2)}) collective-permute-start(bf16[128,1024]{1,0:T(8,128)(2,1)S(1)} %get-tuple-element.419), channel_id=1, source_target_pairs={{0,8},{8,16},{16,24},{1,9},{9,17},{17,25},{2,10},{10,18},{18,26},{... | collective-permute-start | bytes 786440 | tf_op jit(solution)/shard_map/ppermute | solution.py:807
  73.8 11.5 %collective-permute-start.4 = (bf16[128,1024]{1,0:T(8,128)(2,1)S(1)}, bf16[128,1024]{1,0:T(8,128)(2,1)S(1)}, u32[]{:S(2)}, u32[]{:S(2)}) collective-permute-start(bf16[128,1024]{1,0:T(8,128)(2,1)S(1)} %get-tuple-element.418), channel_id=1, source_target_pairs={{0,8},{8,16},{16,24},{1,9},{9,17},{17,25},{2,10},{10,18},{18,26},{... | collective-permute-start | bytes 786440 | tf_op jit(solution)/shard_map/ppermute | solution.py:807
  84.0 11.6 %collective-permute-start.7 = (bf16[128,1024]{1,0:T(8,128)(2,1)S(1)}, bf16[128,1024]{1,0:T(8,128)(2,1)S(1)}, u32[]{:S(2)}, u32[]{:S(2)}) collective-permute-start(bf16[128,1024]{1,0:T(8,128)(2,1)S(1)} %get-tuple-element.449), channel_id=1, source_target_pairs={{0,8},{8,16},{16,24},{1,9},{9,17},{17,25},{2,10},{10,18},{18,26},{... | collective-permute-start | bytes 786440 | tf_op jit(solution)/shard_map/ppermute | solution.py:807
  94.3 11.2 %collective-permute-start.6 = (bf16[128,1024]{1,0:T(8,128)(2,1)S(1)}, bf16[128,1024]{1,0:T(8,128)(2,1)S(1)}, u32[]{:S(2)}, u32[]{:S(2)}) collective-permute-start(bf16[128,1024]{1,0:T(8,128)(2,1)S(1)} %get-tuple-element.448), channel_id=1, source_target_pairs={{0,8},{8,16},{16,24},{1,9},{9,17},{17,25},{2,10},{10,18},{18,26},{... | collective-permute-start | bytes 786440 | tf_op jit(solution)/shard_map/ppermute | solution.py:807
  104.8 2.1 collective-permute-start.9
  106.3 2.1 collective-permute-start.8
  107.7 10.2 %collective-permute-start.11 = (bf16[128,1024]{1,0:T(8,128)(2,1)S(1)}, bf16[128,1024]{1,0:T(8,128)(2,1)S(1)}, u32[]{:S(2)}, u32[]{:S(2)}) collective-permute-start(bf16[128,1024]{1,0:T(8,128)(2,1)S(1)} %get-tuple-element.509), channel_id=1, source_target_pairs={{16,24},{17,25},{18,26},{19,27},{20,28},{21,29},{22,30},{23,31}} | collective-permute-start | bytes 786440 | tf_op jit(solution)/shard_map/ppermute | solution.py:807
  117.3 2.2 collective-permute-start.10
  128.1 2.2 collective-permute-start.13
  129.5 10.3 %collective-permute-start.12 = (bf16[256,1024]{1,0:T(8,128)(2,1)S(1)}, bf16[256,1024]{1,0:T(8,128)(2,1)S(1)}, u32[]{:S(2)}, u32[]{:S(2)}) collective-permute-start(bf16[256,1024]{1,0:T(8,128)(2,1)S(1)} %get-tuple-element.561), channel_id=1, source_target_pairs={{24,16},{25,17},{26,18},{27,19},{28,20},{29,21},{30,22},{31,23}} | collective-permute-start | bytes 1572872 | tf_op jit(solution)/shard_map/ppermute | solution.py:807
  139.1 2.2 collective-permute-start.15
  140.6 10.7 %collective-permute-start.14 = (bf16[256,1024]{1,0:T(8,128)(2,1)S(1)}, bf16[256,1024]{1,0:T(8,128)(2,1)S(1)}, u32[]{:S(2)}, u32[]{:S(2)}) collective-permute-start(bf16[256,1024]{1,0:T(8,128)(2,1)S(1)} %get-tuple-element.577), channel_id=1, source_target_pairs={{16,8},{24,16},{17,9},{25,17},{18,10},{26,18},{19,11},{27,19},{20,... | collective-permute-start | bytes 1572872 | tf_op jit(solution)/shard_map/ppermute | solution.py:807
  149.9 80.2 %collective-permute-start.17 = (bf16[256,1024]{1,0:T(8,128)(2,1)S(1)}, bf16[256,1024]{1,0:T(8,128)(2,1)S(1)}, u32[]{:S(2)}, u32[]{:S(2)}) collective-permute-start(bf16[256,1024]{1,0:T(8,128)(2,1)S(1)} %get-tuple-element.594), channel_id=1, source_target_pairs={{8,0},{16,8},{9,1},{17,9},{10,2},{18,10},{11,3},{19,11},{12,4},{20... | collective-permute-start | bytes 1572872 | tf_op jit(solution)/shard_map/ppermute | solution.py:807
  152.0 94.2 %collective-permute-start.16 = (bf16[256,1024]{1,0:T(8,128)(2,1)S(1)}, bf16[256,1024]{1,0:T(8,128)(2,1)S(1)}, u32[]{:S(2)}, u32[]{:S(2)}) collective-permute-start(bf16[256,1024]{1,0:T(8,128)(2,1)S(1)} %get-tuple-element.593), channel_id=1, source_target_pairs={{8,0},{16,8},{9,1},{17,9},{10,2},{18,10},{11,3},{19,11},{12,4},{20... | collective-permute-start | bytes 1572872 | tf_op jit(solution)/shard_map/ppermute | solution.py:807
  244.9 16.3 %collective-permute-start.19 = (bf16[256,1024]{1,0:T(8,128)(2,1)S(1)}, bf16[256,1024]{1,0:T(8,128)(2,1)S(1)}, u32[]{:S(2)}, u32[]{:S(2)}) collective-permute-start(bf16[256,1024]{1,0:T(8,128)(2,1)S(1)} %get-tuple-element.611), channel_id=1, source_target_pairs={{8,0},{9,1},{10,2},{11,3},{12,4},{13,5},{14,6},{15,7}} | collective-permute-start | bytes 1572872 | tf_op jit(solution)/shard_map/ppermute | solution.py:807
  259.2 17.2 %collective-permute-start.18 = (bf16[256,1024]{1,0:T(8,128)(2,1)S(1)}, bf16[256,1024]{1,0:T(8,128)(2,1)S(1)}, u32[]{:S(2)}, u32[]{:S(2)}) collective-permute-start(bf16[256,1024]{1,0:T(8,128)(2,1)S(1)} %get-tuple-element.609), channel_id=1, source_target_pairs={{8,0},{9,1},{10,2},{11,3},{12,4},{13,5},{14,6},{15,7}} | collective-permute-start | bytes 1572872 | tf_op jit(solution)/shard_map/ppermute | solution.py:807
  281.5 2.7 collective-permute-start.20
  291.8 27.7 %collective-permute-start.22 = (bf16[512,1024]{1,0:T(8,128)(2,1)S(1)}, bf16[512,1024]{1,0:T(8,128)(2,1)S(1)}, u32[]{:S(2)}, u32[]{:S(2)}) collective-permute-start(bf16[512,1024]{1,0:T(8,128)(2,1)S(1)} %products.11.refs_0_.refs_6_), channel_id=1, source_target_pairs={{0,2},{1,3},{2,4},{3,5},{4,6},{5,7},{6,0},{7,1},{8,10},{9,11},{10,... | collective-permute-start | bytes 3145736 | tf_op jit(solution)/shard_map/ppermute | solution.py:619
  291.9 27.6 %collective-permute-start.21 = (bf16[512,1024]{1,0:T(8,128)(2,1)S(1)}, bf16[512,1024]{1,0:T(8,128)(2,1)}, u32[]{:S(2)}, u32[]{:S(2)}) collective-permute-start(bf16[512,1024]{1,0:T(8,128)(2,1)S(1)} %products.12.refs_7_), channel_id=1, source_target_pairs={{0,1},{1,0},{2,3},{3,2},{4,5},{5,4},{6,7},{7,6},{8,9},{9,8},{10,11... | collective-permute-start | bytes 3145736 | tf_op jit(solution)/shard_map/ppermute | solution.py:614
  319.0 12.4 %collective-permute-start.23 = (bf16[128,6528]{1,0:T(8,128)(2,1)S(1)}, bf16[128,6528]{1,0:T(8,128)(2,1)S(1)}, u32[]{:S(2)}, u32[]{:S(2)}) collective-permute-start(bf16[128,6528]{1,0:T(8,128)(2,1)S(1)} %products.13.refs_0_), channel_id=1, source_target_pairs={{0,1},{1,0},{2,3},{3,2},{4,5},{5,4},{6,7},{7,6},{8,9},{9,8},{10,11... | collective-permute-start | bytes 5013512 | tf_op jit(solution)/shard_map/ppermute | solution.py:614
  324.0 27.8 %collective-permute-start.25 = (bf16[512,1024]{1,0:T(8,128)(2,1)S(1)}, bf16[512,1024]{1,0:T(8,128)(2,1)S(1)}, u32[]{:S(2)}, u32[]{:S(2)}) collective-permute-start(bf16[512,1024]{1,0:T(8,128)(2,1)S(1)} %products.14.refs_0_), channel_id=1, source_target_pairs={{0,2},{1,3},{2,4},{3,5},{4,6},{5,7},{6,0},{7,1},{8,10},{9,11},{10,... | collective-permute-start | bytes 3145736 | tf_op jit(solution)/shard_map/ppermute | solution.py:619
  331.4 33.3 %collective-permute-start.24 = (bf16[1024,1024]{1,0:T(8,128)(2,1)}, bf16[1024,1024]{1,0:T(8,128)(2,1)}, u32[]{:S(2)}, u32[]{:S(2)}) collective-permute-start(bf16[1024,1024]{1,0:T(8,128)(2,1)} %products.15.refs_0_), channel_id=1, source_target_pairs={{0,1},{1,0},{2,3},{3,2},{4,5},{5,4},{6,7},{7,6},{8,9},{9,8},{10,11... | collective-permute-start | bytes 6291464 | tf_op jit(solution)/shard_map/ppermute | solution.py:614
  339.1 48.0 %collective-permute-start.27 = (bf16[128,6528]{1,0:T(8,128)(2,1)}, bf16[128,6528]{1,0:T(8,128)(2,1)}, u32[]{:S(2)}, u32[]{:S(2)}) collective-permute-start(bf16[128,6528]{1,0:T(8,128)(2,1)} %products.16.refs_0_), channel_id=1, source_target_pairs={{0,2},{1,3},{2,4},{3,5},{4,6},{5,7},{6,0},{7,1},{8,10},{9,11},{10,... | collective-permute-start | bytes 5013512 | tf_op jit(solution)/shard_map/ppermute | solution.py:619
  364.6 8.7 %collective-permute-start.26 = (bf16[384,6528]{1,0:T(8,128)(2,1)}, bf16[384,6528]{1,0:T(8,128)(2,1)}, u32[]{:S(2)}, u32[]{:S(2)}) collective-permute-start(bf16[384,6528]{1,0:T(8,128)(2,1)} %products.18), channel_id=1, source_target_pairs={{0,1},{1,0},{2,3},{3,2},{4,5},{5,4},{6,7},{7,6},{8,9},{9,8},{10,11... | collective-permute-start | bytes 15040520 | tf_op jit(solution)/shard_map/ppermute | solution.py:614
  389.0 63.8 %copy-start.7 = (bf16[1024,1024]{1,0:T(8,128)(2,1)S(1)}, bf16[1024,1024]{1,0:T(8,128)(2,1)}, u32[]{:S(2)}) copy-start(bf16[1024,1024]{1,0:T(8,128)(2,1)} %copy-done.6) | copy-start | bytes 6291460
  389.0 41.3 %collective-permute-start.28 = (bf16[128,6528]{1,0:T(8,128)(2,1)S(1)}, bf16[128,6528]{1,0:T(8,128)(2,1)S(1)}, u32[]{:S(2)}, u32[]{:S(2)}) collective-permute-start(bf16[128,6528]{1,0:T(8,128)(2,1)S(1)} %add.162), channel_id=1, source_target_pairs={{0,2},{1,3},{2,4},{3,5},{4,6},{5,7},{6,0},{7,1},{8,10},{9,11},{10,... | collective-permute-start | bytes 5013512 | tf_op jit(solution)/shard_map/ppermute | solution.py:619
  389.0 63.7 %collective-permute-start.30 = (bf16[512,1024]{1,0:T(8,128)(2,1)S(1)}, bf16[512,1024]{1,0:T(8,128)(2,1)S(1)}, u32[]{:S(2)}, u32[]{:S(2)}) collective-permute-start(bf16[512,1024]{1,0:T(8,128)(2,1)S(1)} %add.161.refs_0_), channel_id=1, source_target_pairs={{0,2},{1,3},{2,4},{3,5},{4,6},{5,7},{6,0},{7,1},{8,10},{9,11},{10,... | collective-permute-start | bytes 3145736 | tf_op jit(solution)/shard_map/ppermute | solution.py:619
  430.6 56.3 %collective-permute-start.29 = (bf16[128,6528]{1,0:T(8,128)(2,1)S(1)}, bf16[128,6528]{1,0:T(8,128)(2,1)S(1)}, u32[]{:S(2)}, u32[]{:S(2)}) collective-permute-start(bf16[128,6528]{1,0:T(8,128)(2,1)S(1)} %add.163), channel_id=1, source_target_pairs={{0,2},{1,3},{2,4},{3,5},{4,6},{5,7},{6,0},{7,1},{8,10},{9,11},{10,... | collective-permute-start | bytes 5013512 | tf_op jit(solution)/shard_map/ppermute | solution.py:619
  (7 other events, 47.3 us)

commit v4 on v3

--- a/solution.py
+++ b/solution.py
@@ -15,7 +15,7 @@
 FFN_TILE = 2048
 BWD_TILE = 2048
 SKEW = 2
-FWD_HEADS = 4
+FWD_HEADS = 8
 BWD_HEADS = 2
 NORM_BLOCK = 128
 NORM_UNROLL = 2
@@ -23,6 +23,7 @@
 SOFTMAX_UNROLL = 2
 SIDE_TILE = 512
 MIB = 1 << 20
+GAIN_COLS = 128
 LIGHT = 5 * 10**9
 HEAVY = 10**11
 
@@ -648,14 +649,14 @@
             right_copies.append((copy, i, n, wide))
 
     def put(row, depth, col, value):
-        for more, offset in zip(added, offsets):
-            value = value + more[offset + row:offset + row + depth, col:col + value.shape[1]].astype(F32)
-        start = 0
-        for out in outs:
-            low, high = max(col, start), min(col + value.shape[1], start + out.shape[1])
-            if low < high:
-                out[row:row + depth, low - start:high - start] = value[:, low - col:high - col].astype(out.dtype)
-            start += out.shape[1]
+        cols = slice(col, col + value.shape[1])
+        if row < outs[0].shape[0]:
+            for more, offset in zip(added, offsets):
+                value = value + more[offset + row:offset + row + depth, cols].astype(F32)
+            outs[0][row:row + depth, cols] = value.astype(outs[0].dtype)
+        else:
+            row -= outs[0].shape[0]
+            outs[1][row:row + depth, cols] = value.astype(outs[1].dtype)
 
     deep = min(share, 256)
     first_col = 0
@@ -672,11 +673,17 @@
                 put(b * share + m * deep, deep, first_col, value)
         first_col += wide
     if extras:
+        gains = extras[0]
         for b in range(blocks):
-            put(b * share, share, first_col, extras[0][pl.ds(pl.multiple_of(meta[spots[b]] * share, 8), share), :])
-
-
-def products(share, spots, meta, lefts, rights, extra, added, dtype, gates, widths, cost):
+            own = gains[...]
+            if gains.shape[2] != share:
+                own = gains[:, :, pl.ds(pl.multiple_of(meta[spots[b]] * share, 128), share)]
+            own = jnp.sum(own, axis=0).reshape(2, 8, share)
+            own = jnp.concatenate([jnp.sum(own, axis=1), jnp.zeros((GAIN_COLS - 2, share), F32)], axis=0)
+            put(b * share, share, first_col, own.T)
+
+
+def products(share, spots, meta, lefts, rights, extra, added, dtype, gates, split, cost):
     vmem = pl.BlockSpec(memory_space=pltpu.VMEM)
     hbm = pl.BlockSpec(memory_space=pltpu.HBM)
     count = len(spots)
@@ -685,22 +692,23 @@
         if count > 1:
             parts = [
                 products(
-                    share, spots[b:b + 1], meta, lefts, rights, extra, [(more, at + b * share) for more, at in added], dtype,
-                    gates, widths, cost,
-                )
+                    share, spots[b:b + 1], meta, lefts, rights, extra,
+                    [] if split and b else [(more, at + b * share) for more, at in added], dtype, gates, False, cost,
+                )[0]
                 for b in range(count)
             ]
-            return [jnp.concatenate(part, axis=0) for part in zip(*parts)]
+            return parts if split else [jnp.concatenate(parts, axis=0)]
         lefts = [block[0] for block in blocks]
+        extra = None if extra is None else lax.dynamic_slice_in_dim(extra, meta[spots[0]] * share, share, 2)
     depth = lefts[0].shape[0]
     extras = [] if extra is None else [extra]
-    total = sum(right.shape[1] for right in rights) + sum(more.shape[1] for more in extras)
+    total = sum(right.shape[1] for right in rights) + GAIN_COLS * len(extras)
     return pl.pallas_call(
         functools.partial(product_kernel, len(lefts), tuple(at for unused, at in added), len(gates), share, spots),
-        out_shape=[jax.ShapeDtypeStruct((count * share, width), dtype) for width in widths or [total]],
+        out_shape=[jax.ShapeDtypeStruct((share if split else count * share, total), dtype)] * (2 if split else 1),
         in_specs=[pl.BlockSpec(memory_space=pltpu.SMEM)] + [pl.BlockSpec(memory_space=pl.ANY)] * len(gates)
         + [hbm] * (2 * len(lefts)) + [vmem] * (len(extras) + len(added)),
-        out_specs=[vmem] * len(widths or [total]),
+        out_specs=[vmem] * (2 if split else 1),
         scratch_shapes=[pltpu.VMEM((count, depth, share), BF16) for _ in lefts]
         + [pltpu.VMEM(right.shape, BF16) for right in rights]
         + [pltpu.SemaphoreType.DMA((len(lefts) * count,)), pltpu.SemaphoreType.DMA((8,))],
@@ -741,10 +749,16 @@
 
     def blocks(self, steps, half, gates, added, dtype, cost):
         spots = [self.spot + 2 * step + half for step in steps]
-        return products(self.share, spots, self.meta, self.lefts, self.rights, self.extra, added, dtype, gates, None, cost)
+        return products(self.share, spots, self.meta, self.lefts, self.rights, self.extra, added, dtype, gates, False, cost)
 
     def other(self, steps, gates=(), cost=LIGHT):
         return self.blocks(steps, 1, gates, [], BF16, cost)[0]
+
+    def own_and_other(self, own_step, other_step, added):
+        spots = [self.spot + 2 * own_step, self.spot + 2 * other_step + 1]
+        return products(
+            self.share, spots, self.meta, self.lefts, self.rights, self.extra, added, BF16, (), True, LIGHT
+        )
 
     def own(self, steps, gates, added, dtype=BF16, cost=LIGHT):
         return self.blocks(steps, 0, gates, added, dtype, cost)[0]
@@ -867,9 +881,8 @@
             gbs = keep_last(spot, meta, incoming, saved[0])
             down_sums = RowSums(meta, blocks_spot, [kept["acts"]], [gbs])
             swapped = swap_cores(down_sums.other([0]))
-            first_total = down_sums.own([0], (), [(swapped, 0)])
+            first_total, ready = down_sums.own_and_other(0, 1, [(swapped, 0)])
             down_ring = next_chip(first_total)
-            ready = down_sums.other([1], [first_total])
             swapped = swap_cores(ready)
             out, *rest = backward_chunk(
                 bwd_geometry, True, static_place, (spot, lengths_spot), meta, cotangent_rows, incoming, needed, gains + given, saved[1:],
@@ -883,10 +896,8 @@
         received[tick] = hop(out, tick, bwd_chunks, lambda s: sections - 1 - s, -1)
     done = dict(zip(BWD_SAVED, saved))
 
-    gains = jnp.sum(done["gains"].reshape(bwd_chunks, 2, 8, width), axis=(0, 2))
-    gains = jnp.pad(gains.T, ((0, 0), (0, 128 - gains.shape[0])))
     rest_sums = RowSums(
-        meta, blocks_spot, [kept["n2s"], kept["n1s"], kept["os"]], [done["dus"], done["dqkvs"], done["gms"]], gains
+        meta, blocks_spot, [kept["n2s"], kept["n1s"], kept["os"]], [done["dus"], done["dqkvs"], done["gms"]], done["gains"]
     )
     later = list(range(1, chips))
     widths = [ffn, heads * size, size, size, width, 128]

time: 499 us -> 495 us (level)
    pallas_call x10 -> x9, Pallas kernels: 68.4 us -> 65.8 us  [products(): pl.pallas_call(functools.partial(product_kernel, len(lefts), tuple((at fo...]
  transfers between devices with their start and end apart: 31 -> 31, of which waited for: 9 -> 10; matrix products, arithmetic and copies ran while one was open for 1% -> 0% of each run, Pallas kernels for 46% -> 47%
where the time goes in v4:
time: 495 us; the launch traced here: 486 us
  Pallas kernels  265 us (54%)
  waiting for transfers between devices  189 us (38%)
  starting transfers between devices  22.5 us (5%)
  local copies, waits for them, and re-layouts  4.99 us (1%)
    ppermute x6, waiting for transfers between devices, next_chip(): lax.ppermute(block, 'dp', [(i, (i + 2) % devices) for i in range(devices)])  112 us
    pallas_call x14, Pallas kernels, forward_chunk(): pl.pallas_call(functools.partial(forward_kernel, geometry, loading, place...  105 us
    pallas_call x10, Pallas kernels, backward_chunk(): pl.pallas_call(functools.partial(backward_kernel, geometry, last_call, le...  87.7 us
    ppermute x20, waiting for transfers between devices, hop(): return lax.ppermute(block, 'section', route) if route else None  74 us
    pallas_call x9, Pallas kernels, products(): pl.pallas_call(functools.partial(product_kernel, len(lefts), tuple((at fo...  65.8 us
    ppermute x20, starting transfers between devices, hop(): return lax.ppermute(block, 'section', route) if route else None  21.1 us
  transfers between devices with their start and end apart: 31, of which 10 were waited for; matrix products, arithmetic and copies ran while one was open for 0% of the time, Pallas kernels for 47%

profile of v4, /device:TPU:0, one launch (start us, length us, event | category | flops | bytes accessed | tf_op | source)
XLA Modules:
  0.0 485.6 jit_solution(10690488981652399423)
XLA Ops:
  4.7 14.9 %forward_chunk.14 = (bf16[128,1024]{1,0:T(8,128)(2,1)S(1)}, bf16[1024,1024]{1,0:T(8,128)(2,1)}, bf16[1024,1024]{1,0:T(8,128)(2,1)}, bf16[1024,1024]{1,0:T(8,128)...) custom-call(s32[112]{0:T(128)S(1)} %concatenate.3.meta, ...), custom_call_target="tpu_custom_call", output_to_operand_aliasing={{1}: (11, {}), {2}: (12, {}), {3}: (13, {}), {4}: (14, {}),... | custom-call | flops 2885681152 | bytes 8388608 | tf_op jit(solution)/shard_map/forward_chunk/pallas_call | solution.py:304
  20.9 8.1 %forward_chunk.15 = (bf16[128,1024]{1,0:T(8,128)(2,1)S(1)}, bf16[1024,1024]{1,0:T(8,128)(2,1)}, bf16[1024,1024]{1,0:T(8,128)(2,1)}, bf16[1024,1024]{1,0:T(8,128)...) custom-call(s32[112]{0:T(128)S(1)} %concatenate.3.meta, ...), custom_call_target="tpu_custom_call", output_to_operand_aliasing={{1}: (10, {}), {2}: (11, {}), {3}: (12, {}), {4}: (13, {}),... | custom-call | flops 2885681152 | bytes 8388608 | tf_op jit(solution)/shard_map/forward_chunk/pallas_call | solution.py:304
  30.3 8.9 %forward_chunk.16 = (bf16[128,1024]{1,0:T(8,128)(2,1)S(1)}, bf16[1024,1024]{1,0:T(8,128)(2,1)}, bf16[1024,1024]{1,0:T(8,128)(2,1)}, bf16[1024,1024]{1,0:T(8,128)...) custom-call(s32[112]{0:T(128)S(1)} %concatenate.3.meta, ...), custom_call_target="tpu_custom_call", output_to_operand_aliasing={{1}: (10, {}), {2}: (11, {}), {3}: (12, {}), {4}: (13, {}),... | custom-call | flops 2885681152 | bytes 8388608 | tf_op jit(solution)/shard_map/forward_chunk/pallas_call | solution.py:304
  40.4 8.7 %forward_chunk.17 = (bf16[128,1024]{1,0:T(8,128)(2,1)S(1)}, bf16[1024,1024]{1,0:T(8,128)(2,1)}, bf16[1024,1024]{1,0:T(8,128)(2,1)}, bf16[1024,1024]{1,0:T(8,128)...) custom-call(s32[112]{0:T(128)S(1)} %concatenate.3.meta, ...), custom_call_target="tpu_custom_call", output_to_operand_aliasing={{1}: (10, {}), {2}: (11, {}), {3}: (12, {}), {4}: (13, {}),... | custom-call | flops 2885681152 | bytes 8388608 | tf_op jit(solution)/shard_map/forward_chunk/pallas_call | solution.py:304
  50.5 9.7 %forward_chunk.18 = (bf16[128,1024]{1,0:T(8,128)(2,1)S(1)}, bf16[1024,1024]{1,0:T(8,128)(2,1)}, bf16[1024,1024]{1,0:T(8,128)(2,1)}, bf16[1024,1024]{1,0:T(8,128)...) custom-call(s32[112]{0:T(128)S(1)} %concatenate.3.meta, ...), custom_call_target="tpu_custom_call", output_to_operand_aliasing={{1}: (10, {}), {2}: (11, {}), {3}: (12, {}), {4}: (13, {}),... | custom-call | flops 2885681152 | bytes 8388608 | tf_op jit(solution)/shard_map/forward_chunk/pallas_call | solution.py:304
  61.5 8.3 %forward_chunk.19 = (bf16[128,1024]{1,0:T(8,128)(2,1)S(1)}, bf16[1024,1024]{1,0:T(8,128)(2,1)}, bf16[1024,1024]{1,0:T(8,128)(2,1)}, bf16[1024,1024]{1,0:T(8,128)...) custom-call(s32[112]{0:T(128)S(1)} %concatenate.3.meta, ...), custom_call_target="tpu_custom_call", output_to_operand_aliasing={{1}: (10, {}), {2}: (11, {}), {3}: (12, {}), {4}: (13, {}),... | custom-call | flops 2885681152 | bytes 8388608 | tf_op jit(solution)/shard_map/forward_chunk/pallas_call | solution.py:304
  71.1 10.2 %forward_chunk.20 = (bf16[128,1024]{1,0:T(8,128)(2,1)S(1)}, bf16[1024,1024]{1,0:T(8,128)(2,1)}, bf16[1024,1024]{1,0:T(8,128)(2,1)}, bf16[1024,1024]{1,0:T(8,128)...) custom-call(s32[112]{0:T(128)S(1)} %concatenate.3.meta, ...), custom_call_target="tpu_custom_call", output_to_operand_aliasing={{1}: (10, {}), {2}: (11, {}), {3}: (12, {}), {4}: (13, {}),... | custom-call | flops 2885681152 | bytes 8388608 | tf_op jit(solution)/shard_map/forward_chunk/pallas_call | solution.py:304
  82.6 8.7 %forward_chunk.21 = (bf16[128,1024]{1,0:T(8,128)(2,1)S(1)}, bf16[1024,1024]{1,0:T(8,128)(2,1)}, bf16[1024,1024]{1,0:T(8,128)(2,1)}, bf16[1024,1024]{1,0:T(8,128)...) custom-call(s32[112]{0:T(128)S(1)} %concatenate.3.meta, ...), custom_call_target="tpu_custom_call", output_to_operand_aliasing={{1}: (10, {}), {2}: (11, {}), {3}: (12, {}), {4}: (13, {}),... | custom-call | flops 2885681152 | bytes 8388608 | tf_op jit(solution)/shard_map/forward_chunk/pallas_call | solution.py:304
  92.6 7.2 %forward_chunk.22 = (bf16[128,1024]{1,0:T(8,128)(2,1)S(1)}, bf16[1024,1024]{1,0:T(8,128)(2,1)}, bf16[1024,1024]{1,0:T(8,128)(2,1)}, bf16[1024,1024]{1,0:T(8,128)...) custom-call(s32[112]{0:T(128)S(1)} %concatenate.3.meta, ...), custom_call_target="tpu_custom_call", output_to_operand_aliasing={{1}: (10, {}), {2}: (11, {}), {3}: (12, {}), {4}: (13, {}),... | custom-call | flops 2885681152 | bytes 8388608 | tf_op jit(solution)/shard_map/forward_chunk/pallas_call | solution.py:304
  101.9 9.9 %forward_chunk.24 = (bf16[128,1024]{1,0:T(8,128)(2,1)S(1)}, bf16[1024,1024]{1,0:T(8,128)(2,1)}, bf16[1024,1024]{1,0:T(8,128)(2,1)}, bf16[1024,1024]{1,0:T(8,128)...) custom-call(s32[112]{0:T(128)S(1)} %concatenate.3.meta, ...), custom_call_target="tpu_custom_call", output_to_operand_aliasing={{1}: (10, {}), {2}: (11, {}), {3}: (12, {}), {4}: (13, {}),... | custom-call | flops 2885681152 | bytes 8388608 | tf_op jit(solution)/shard_map/forward_chunk/pallas_call | solution.py:304
  115.4 7.3 %forward_chunk.27 = (bf16[128,1024]{1,0:T(8,128)(2,1)}, bf16[1024,1024]{1,0:T(8,128)(2,1)}, bf16[1024,1024]{1,0:T(8,128)(2,1)}, bf16[1024,1024]{1,0:T(8,128)(2,1...) custom-call(s32[112]{0:T(128)S(1)} %concatenate.3.meta, ...), custom_call_target="tpu_custom_call", output_to_operand_aliasing={{1}: (10, {}), {2}: (11, {}), {3}: (12, {}), {4}: (13, {}),... | custom-call | flops 2885681152 | bytes 8388608 | tf_op jit(solution)/shard_map/forward_chunk/pallas_call | solution.py:304
  124.3 8.8 %backward_chunk.11 = (bf16[256,1024]{1,0:T(8,128)(2,1)S(1)}, bf16[1024,1024]{1,0:T(8,128)(2,1)}, bf16[1024,4096]{1,0:T(8,128)(2,1)}, bf16[1024,1024]{1,0:T(8,128...) custom-call(s32[112]{0:T(128)S(1)} %concatenate.3.meta, ...), custom_call_target="tpu_custom_call", output_to_operand_aliasing={{1}: (18, {}), {2}: (19, {}), {3}: (20, {}), {4}: (21, {}),... | custom-call | flops 6308233216 | bytes 8388608 | tf_op jit(solution)/shard_map/backward_chunk/pallas_call | solution.py:552
  135.3 8.6 %backward_chunk.13 = (bf16[256,1024]{1,0:T(8,128)(2,1)S(1)}, bf16[1024,1024]{1,0:T(8,128)(2,1)}, bf16[1024,4096]{1,0:T(8,128)(2,1)}, bf16[1024,1024]{1,0:T(8,128...) custom-call(s32[112]{0:T(128)S(1)} %concatenate.3.meta, ...), custom_call_target="tpu_custom_call", output_to_operand_aliasing={{1}: (18, {}), {2}: (19, {}), {3}: (20, {}), {4}: (21, {}),... | custom-call | flops 6308233216 | bytes 8388608 | tf_op jit(solution)/shard_map/backward_chunk/pallas_call | solution.py:552
  146.7 8.2 %backward_chunk.15 = (bf16[256,1024]{1,0:T(8,128)(2,1)S(1)}, bf16[1024,1024]{1,0:T(8,128)(2,1)}, bf16[1024,4096]{1,0:T(8,128)(2,1)}, bf16[1024,1024]{1,0:T(8,128...) custom-call(s32[112]{0:T(128)S(1)} %concatenate.3.meta, ...), custom_call_target="tpu_custom_call", output_to_operand_aliasing={{1}: (18, {}), {2}: (19, {}), {3}: (20, {}), {4}: (21, {}),... | custom-call | flops 6308233216 | bytes 8388608 | tf_op jit(solution)/shard_map/backward_chunk/pallas_call | solution.py:552
  156.2 73.5 %collective-permute-done.17.incoming = bf16[256,1024]{1,0:T(8,128)(2,1)S(1)} collective-permute-done((bf16[256,1024]{1,0:T(8,128)(2,1)S(1)}, bf16[256,1024]{1,0:T(8,128)(2,1)S(1)}, u32[]{:S(2)}, u32[]{:S(2)}) %collective-permute-start.17) | collective-permute-done | bytes 524320 | tf_op jit(solution)/shard_map/ppermute | solution.py:821
  229.7 14.3 %backward_chunk.16 = (bf16[256,1024]{1,0:T(8,128)(2,1)S(1)}, bf16[1024,1024]{1,0:T(8,128)(2,1)}, bf16[1024,4096]{1,0:T(8,128)(2,1)}, bf16[1024,1024]{1,0:T(8,128...) custom-call(s32[112]{0:T(128)S(1)} %concatenate.3.meta, ...), custom_call_target="tpu_custom_call", output_to_operand_aliasing={{1}: (18, {}), {2}: (19, {}), {3}: (20, {}), {4}: (21, {}),... | custom-call | flops 6308233216 | bytes 8388608 | tf_op jit(solution)/shard_map/backward_chunk/pallas_call | solution.py:552
  245.4 13.3 %backward_chunk.17 = (bf16[256,1024]{1,0:T(8,128)(2,1)S(1)}, bf16[1024,1024]{1,0:T(8,128)(2,1)}, bf16[1024,4096]{1,0:T(8,128)(2,1)}, bf16[1024,1024]{1,0:T(8,128...) custom-call(s32[112]{0:T(128)S(1)} %concatenate.3.meta, ...), custom_call_target="tpu_custom_call", output_to_operand_aliasing={{1}: (18, {}), {2}: (19, {}), {3}: (20, {}), {4}: (21, {}),... | custom-call | flops 6308233216 | bytes 8388608 | tf_op jit(solution)/shard_map/backward_chunk/pallas_call | solution.py:552
  260.5 15.1 %backward_chunk.18 = (bf16[256,1024]{1,0:T(8,128)(2,1)}, bf16[1024,1024]{1,0:T(8,128)(2,1)}, bf16[1024,4096]{1,0:T(8,128)(2,1)}, bf16[1024,1024]{1,0:T(8,128)(2,...) custom-call(s32[112]{0:T(128)S(1)} %concatenate.3.meta, ...), custom_call_target="tpu_custom_call", output_to_operand_aliasing={{1}: (18, {}), {2}: (19, {}), {3}: (20, {}), {4}: (21, {}),... | custom-call | flops 6308233216 | bytes 8388608 | tf_op jit(solution)/shard_map/backward_chunk/pallas_call | solution.py:552
  277.0 3.8 products.9
  283.5 5.5 %products.10 = (bf16[512,1024]{1,0:T(8,128)(2,1)S(1)}, bf16[512,1024]{1,0:T(8,128)(2,1)S(1)}) custom-call(s32[112]{0:T(128)S(1)} %concatenate.3.meta, bf16[1024,4096]{1,0:T(8,128)(2,1)} %get-tuple-element.612.refs_0_.refs_1_, bf16[1024,1024]{1,0:T(8,128)(2,1)} %keep_last.1.refs_1_.refs_2_, bf16[512,1024]{1,0:T(8,128)(2,1)S(1)} %collective-permute-done.20.refs_2_), custom_call_target="tpu_custom_call" | custom-call | flops 5000000000 | bytes 1024 | tf_op jit(solution)/shard_map/products/pallas_call | solution.py:706
  289.2 17.1 %backward_chunk.19 = (bf16[256,1024]{1,0:T(8,128)(2,1)}, bf16[1024,4096]{1,0:T(8,128)(2,1)}, bf16[1024,1024]{1,0:T(8,128)(2,1)}, bf16[1024,1280]{1,0:T(8,128)(2,...) custom-call(s32[112]{0:T(128)S(1)} %concatenate.3.meta, ...), custom_call_target="tpu_custom_call", output_to_operand_aliasing={{1}: (21, {}), {2}: (22, {}), {3}: (23, {}), {4}: (24, {}),... | custom-call | flops 1024 | bytes 1024 | tf_op jit(solution)/shard_map/backward_chunk/pallas_call | solution.py:552
  307.2 6.5 %products.11.refs_0_ = bf16[128,6528]{1,0:T(8,128)(2,1)S(1)} custom-call(s32[112]{0:T(128)S(1)} %concatenate.3.meta, bf16[1024,1024]{1,0:T(8,128)(2,1)} %get-tuple-element.631.refs_0_.refs_1_.refs_2_, bf16[1024,1024]{1,0:T(8,128)(2,1)} %get-tuple-element.632.refs_1_.refs_2_.refs_3_, bf16[1024,1024]{1,0:T(8,128)(2,1)} %get-tuple-element.633.refs_2_.refs_3_.refs_4_, ...), custom_call_target="tpu_custom_call" | custom-call | flops 5000000000 | bytes 1024 | tf_op jit(solution)/shard_map/products/pallas_call | solution.py:706
  316.4 3.9 products.12.refs_0_
  320.4 6.8 %products.13.refs_0_ = bf16[1024,1024]{1,0:T(8,128)(2,1)} custom-call(s32[112]{0:T(128)S(1)} %concatenate.3.meta, bf16[512,1024]{1,0:T(8,128)(2,1)S(1)} %products.12.refs_0_, bf16[1024,4096]{1,0:T(8,128)(2,1)} %get-tuple-element.612.refs_0_.refs_1_, bf16[1024,1024]{1,0:T(8,128)(2,1)} %keep_last.1.refs_1_.refs_2_), custom_call_target="tpu_custom_call" | custom-call | flops 5000000000 | bytes 1024 | tf_op jit(solution)/shard_map/products/pallas_call | solution.py:706
  327.3 7.8 %products.14.refs_0_ = bf16[128,6528]{1,0:T(8,128)(2,1)} custom-call(s32[112]{0:T(128)S(1)} %concatenate.3.meta, bf16[1024,1024]{1,0:T(8,128)(2,1)} %products.13.refs_0_, bf16[1024,1024]{1,0:T(8,128)(2,1)} %get-tuple-element.631.refs_0_.refs_1_.refs_2_, bf16[1024,1024]{1,0:T(8,128)(2,1)} %get-tuple-element.632.refs_1_.refs_2_.refs_3_, ...), custom_call_target="tpu_custom_call" | custom-call | flops 99999997952 | bytes 1024 | tf_op jit(solution)/shard_map/products/pallas_call | solution.py:706
  335.3 12.9 %collective-permute-done.25.come.refs_1_ = bf16[512,1024]{1,0:T(8,128)(2,1)S(1)} collective-permute-done((bf16[512,1024]{1,0:T(8,128)(2,1)S(1)}, bf16[512,1024]{1,0:T(8,128)(2,1)S(1)}, u32[]{:S(2)}, u32[]{:S(2)}) %collective-permute-start.25) | collective-permute-done | bytes 1048608 | tf_op jit(solution)/shard_map/ppermute | solution.py:620
  348.2 12.6 %products.16 = bf16[384,6528]{1,0:T(8,128)(2,1)} custom-call(s32[112]{0:T(128)S(1)} %concatenate.3.meta, bf16[128,6528]{1,0:T(8,128)(2,1)} %products.14.refs_0_, bf16[512,1024]{1,0:T(8,128)(2,1)S(1)} %collective-permute-done.25.come.refs_1_, bf16[1024,1024]{1,0:T(8,128)(2,1)} %get-tuple-element.631.refs_0_.refs_1_.refs_2_, ...), custom_call_target="tpu_custom_call" | custom-call | flops 99999997952 | bytes 1024 | tf_op jit(solution)/shard_map/products/pallas_call | solution.py:706
  360.9 6.5 %products.15.kept = bf16[1024,1024]{1,0:T(8,128)(2,1)S(1)} custom-call(s32[112]{0:T(128)S(1)} %concatenate.3.meta, bf16[128,6528]{1,0:T(8,128)(2,1)} %products.14.refs_0_, bf16[1024,4096]{1,0:T(8,128)(2,1)} %get-tuple-element.612.refs_0_.refs_1_, bf16[1024,1024]{1,0:T(8,128)(2,1)} %keep_last.1.refs_1_.refs_2_, bf16[1024,1024]{1,0:T(8,128)(2,1)} %collective-permute-done.24.refs_3_), custom_call_target="tpu_custom_call" | custom-call | flops 99999997952 | bytes 1024 | tf_op jit(solution)/shard_map/products/pallas_call | solution.py:706
  369.6 12.5 %products.17.kept = bf16[384,6528]{1,0:T(8,128)(2,1)S(1)} custom-call(s32[112]{0:T(128)S(1)} %concatenate.3.meta, bf16[512,1024]{1,0:T(8,128)(2,1)S(1)} %add.159.refs_0_, bf16[1024,1024]{1,0:T(8,128)(2,1)} %get-tuple-element.631.refs_0_.refs_1_.refs_2_, bf16[1024,1024]{1,0:T(8,128)(2,1)} %get-tuple-element.632.refs_1_.refs_2_.refs_3_, ...), custom_call_target="tpu_custom_call" | custom-call | flops 99999997952 | bytes 1024 | tf_op jit(solution)/shard_map/products/pallas_call | solution.py:706
  384.7 41.1 %collective-permute-done.28.come = bf16[128,6528]{1,0:T(8,128)(2,1)S(1)} collective-permute-done((bf16[128,6528]{1,0:T(8,128)(2,1)S(1)}, bf16[128,6528]{1,0:T(8,128)(2,1)S(1)}, u32[]{:S(2)}, u32[]{:S(2)}) %collective-permute-start.28) | collective-permute-done | bytes 1671200 | tf_op jit(solution)/shard_map/ppermute | solution.py:620
  426.2 22.0 %collective-permute-done.30.come = bf16[512,1024]{1,0:T(8,128)(2,1)S(1)} collective-permute-done((bf16[512,1024]{1,0:T(8,128)(2,1)S(1)}, bf16[512,1024]{1,0:T(8,128)(2,1)S(1)}, u32[]{:S(2)}, u32[]{:S(2)}) %collective-permute-start.30) | collective-permute-done | bytes 1048608 | tf_op jit(solution)/shard_map/ppermute | solution.py:620
  449.8 32.9 %collective-permute-done.29.come = bf16[128,6528]{1,0:T(8,128)(2,1)S(1)} collective-permute-done((bf16[128,6528]{1,0:T(8,128)(2,1)S(1)}, bf16[128,6528]{1,0:T(8,128)(2,1)S(1)}, u32[]{:S(2)}, u32[]{:S(2)}) %collective-permute-start.29) | collective-permute-done | bytes 1671200 | tf_op jit(solution)/shard_map/ppermute | solution.py:620
  (96 shorter events, 48.0 us)
Async XLA Ops:
  19.5 10.7 %collective-permute-start.1 = (bf16[128,1024]{1,0:T(8,128)(2,1)S(1)}, bf16[128,1024]{1,0:T(8,128)(2,1)S(1)}, u32[]{:S(2)}, u32[]{:S(2)}) collective-permute-start(bf16[128,1024]{1,0:T(8,128)(2,1)S(1)} %get-tuple-element.361), channel_id=1, source_target_pairs={{0,8},{1,9},{2,10},{3,11},{4,12},{5,13},{6,14},{7,15}} | collective-permute-start | bytes 786440 | tf_op jit(solution)/shard_map/ppermute | solution.py:821
  28.9 11.5 %collective-permute-start = (bf16[128,1024]{1,0:T(8,128)(2,1)S(1)}, bf16[128,1024]{1,0:T(8,128)(2,1)S(1)}, u32[]{:S(2)}, u32[]{:S(2)}) collective-permute-start(bf16[128,1024]{1,0:T(8,128)(2,1)S(1)} %get-tuple-element.360), channel_id=1, source_target_pairs={{0,8},{1,9},{2,10},{3,11},{4,12},{5,13},{6,14},{7,15}} | collective-permute-start | bytes 786440 | tf_op jit(solution)/shard_map/ppermute | solution.py:821
  39.1 11.3 %collective-permute-start.3 = (bf16[128,1024]{1,0:T(8,128)(2,1)S(1)}, bf16[128,1024]{1,0:T(8,128)(2,1)S(1)}, u32[]{:S(2)}, u32[]{:S(2)}) collective-permute-start(bf16[128,1024]{1,0:T(8,128)(2,1)S(1)} %get-tuple-element.391), channel_id=1, source_target_pairs={{0,8},{8,16},{1,9},{9,17},{2,10},{10,18},{3,11},{11,19},{4,12},{12... | collective-permute-start | bytes 786440 | tf_op jit(solution)/shard_map/ppermute | solution.py:821
  49.1 12.3 %collective-permute-start.2 = (bf16[128,1024]{1,0:T(8,128)(2,1)S(1)}, bf16[128,1024]{1,0:T(8,128)(2,1)S(1)}, u32[]{:S(2)}, u32[]{:S(2)}) collective-permute-start(bf16[128,1024]{1,0:T(8,128)(2,1)S(1)} %get-tuple-element.390), channel_id=1, source_target_pairs={{0,8},{8,16},{1,9},{9,17},{2,10},{10,18},{3,11},{11,19},{4,12},{12... | collective-permute-start | bytes 786440 | tf_op jit(solution)/shard_map/ppermute | solution.py:821
  60.2 10.9 %collective-permute-start.5 = (bf16[128,1024]{1,0:T(8,128)(2,1)S(1)}, bf16[128,1024]{1,0:T(8,128)(2,1)S(1)}, u32[]{:S(2)}, u32[]{:S(2)}) collective-permute-start(bf16[128,1024]{1,0:T(8,128)(2,1)S(1)} %get-tuple-element.421), channel_id=1, source_target_pairs={{0,8},{8,16},{16,24},{1,9},{9,17},{17,25},{2,10},{10,18},{18,26},{... | collective-permute-start | bytes 786440 | tf_op jit(solution)/shard_map/ppermute | solution.py:821
  69.7 12.8 %collective-permute-start.4 = (bf16[128,1024]{1,0:T(8,128)(2,1)S(1)}, bf16[128,1024]{1,0:T(8,128)(2,1)S(1)}, u32[]{:S(2)}, u32[]{:S(2)}) collective-permute-start(bf16[128,1024]{1,0:T(8,128)(2,1)S(1)} %get-tuple-element.420), channel_id=1, source_target_pairs={{0,8},{8,16},{16,24},{1,9},{9,17},{17,25},{2,10},{10,18},{18,26},{... | collective-permute-start | bytes 786440 | tf_op jit(solution)/shard_map/ppermute | solution.py:821
  81.2 11.3 %collective-permute-start.7 = (bf16[128,1024]{1,0:T(8,128)(2,1)S(1)}, bf16[128,1024]{1,0:T(8,128)(2,1)S(1)}, u32[]{:S(2)}, u32[]{:S(2)}) collective-permute-start(bf16[128,1024]{1,0:T(8,128)(2,1)S(1)} %get-tuple-element.451), channel_id=1, source_target_pairs={{0,8},{8,16},{16,24},{1,9},{9,17},{17,25},{2,10},{10,18},{18,26},{... | collective-permute-start | bytes 786440 | tf_op jit(solution)/shard_map/ppermute | solution.py:821
  91.2 9.2 %collective-permute-start.6 = (bf16[128,1024]{1,0:T(8,128)(2,1)S(1)}, bf16[128,1024]{1,0:T(8,128)(2,1)S(1)}, u32[]{:S(2)}, u32[]{:S(2)}) collective-permute-start(bf16[128,1024]{1,0:T(8,128)(2,1)S(1)} %get-tuple-element.450), channel_id=1, source_target_pairs={{0,8},{8,16},{16,24},{1,9},{9,17},{17,25},{2,10},{10,18},{18,26},{... | collective-permute-start | bytes 786440 | tf_op jit(solution)/shard_map/ppermute | solution.py:821
  99.7 2.1 collective-permute-start.9
  101.2 11.3 %collective-permute-start.8 = (bf16[128,1024]{1,0:T(8,128)(2,1)S(1)}, bf16[128,1024]{1,0:T(8,128)(2,1)S(1)}, u32[]{:S(2)}, u32[]{:S(2)}) collective-permute-start(bf16[128,1024]{1,0:T(8,128)(2,1)S(1)} %get-tuple-element.480), channel_id=1, source_target_pairs={{8,16},{16,24},{9,17},{17,25},{10,18},{18,26},{11,19},{19,27},{12,... | collective-permute-start | bytes 786440 | tf_op jit(solution)/shard_map/ppermute | solution.py:821
  111.8 2.1 collective-permute-start.11
  113.2 2.2 collective-permute-start.10
  123.6 10.2 %collective-permute-start.13 = (bf16[256,1024]{1,0:T(8,128)(2,1)S(1)}, bf16[256,1024]{1,0:T(8,128)(2,1)S(1)}, u32[]{:S(2)}, u32[]{:S(2)}) collective-permute-start(bf16[256,1024]{1,0:T(8,128)(2,1)S(1)} %get-tuple-element.564), channel_id=1, source_target_pairs={{24,16},{25,17},{26,18},{27,19},{28,20},{29,21},{30,22},{31,23}} | collective-permute-start | bytes 1572872 | tf_op jit(solution)/shard_map/ppermute | solution.py:821
  133.1 2.2 collective-permute-start.12
  134.5 10.1 %collective-permute-start.15 = (bf16[256,1024]{1,0:T(8,128)(2,1)S(1)}, bf16[256,1024]{1,0:T(8,128)(2,1)S(1)}, u32[]{:S(2)}, u32[]{:S(2)}) collective-permute-start(bf16[256,1024]{1,0:T(8,128)(2,1)S(1)} %get-tuple-element.580), channel_id=1, source_target_pairs={{16,8},{24,16},{17,9},{25,17},{18,10},{26,18},{19,11},{27,19},{20,... | collective-permute-start | bytes 1572872 | tf_op jit(solution)/shard_map/ppermute | solution.py:821
  143.9 2.8 collective-permute-start.14
  145.4 84.4 %collective-permute-start.17 = (bf16[256,1024]{1,0:T(8,128)(2,1)S(1)}, bf16[256,1024]{1,0:T(8,128)(2,1)S(1)}, u32[]{:S(2)}, u32[]{:S(2)}) collective-permute-start(bf16[256,1024]{1,0:T(8,128)(2,1)S(1)} %get-tuple-element.596), channel_id=1, source_target_pairs={{8,0},{16,8},{9,1},{17,9},{10,2},{18,10},{11,3},{19,11},{12,4},{20... | collective-permute-start | bytes 1572872 | tf_op jit(solution)/shard_map/ppermute | solution.py:821
  154.9 90.5 %collective-permute-start.16 = (bf16[256,1024]{1,0:T(8,128)(2,1)S(1)}, bf16[256,1024]{1,0:T(8,128)(2,1)S(1)}, u32[]{:S(2)}, u32[]{:S(2)}) collective-permute-start(bf16[256,1024]{1,0:T(8,128)(2,1)S(1)} %get-tuple-element.595), channel_id=1, source_target_pairs={{8,0},{16,8},{9,1},{17,9},{10,2},{18,10},{11,3},{19,11},{12,4},{20... | collective-permute-start | bytes 1572872 | tf_op jit(solution)/shard_map/ppermute | solution.py:821
  244.1 16.4 %collective-permute-start.19 = (bf16[256,1024]{1,0:T(8,128)(2,1)S(1)}, bf16[256,1024]{1,0:T(8,128)(2,1)S(1)}, u32[]{:S(2)}, u32[]{:S(2)}) collective-permute-start(bf16[256,1024]{1,0:T(8,128)(2,1)S(1)} %get-tuple-element.613), channel_id=1, source_target_pairs={{8,0},{9,1},{10,2},{11,3},{12,4},{13,5},{14,6},{15,7}} | collective-permute-start | bytes 1572872 | tf_op jit(solution)/shard_map/ppermute | solution.py:821
  258.8 16.9 %collective-permute-start.18 = (bf16[256,1024]{1,0:T(8,128)(2,1)S(1)}, bf16[256,1024]{1,0:T(8,128)(2,1)S(1)}, u32[]{:S(2)}, u32[]{:S(2)}) collective-permute-start(bf16[256,1024]{1,0:T(8,128)(2,1)S(1)} %get-tuple-element.611), channel_id=1, source_target_pairs={{8,0},{9,1},{10,2},{11,3},{12,4},{13,5},{14,6},{15,7}} | collective-permute-start | bytes 1572872 | tf_op jit(solution)/shard_map/ppermute | solution.py:821
  280.8 2.7 collective-permute-start.20
  289.0 25.2 %collective-permute-start.21 = (bf16[512,1024]{1,0:T(8,128)(2,1)S(1)}, bf16[512,1024]{1,0:T(8,128)(2,1)S(1)}, u32[]{:S(2)}, u32[]{:S(2)}) collective-permute-start(bf16[512,1024]{1,0:T(8,128)(2,1)S(1)} %get-tuple-element.623.refs_7_), channel_id=1, source_target_pairs={{0,1},{1,0},{2,3},{3,2},{4,5},{5,4},{6,7},{7,6},{8,9},{9,8},{10,11... | collective-permute-start | bytes 3145736 | tf_op jit(solution)/shard_map/ppermute | solution.py:615
  289.2 27.2 %collective-permute-start.22 = (bf16[512,1024]{1,0:T(8,128)(2,1)S(1)}, bf16[512,1024]{1,0:T(8,128)(2,1)S(1)}, u32[]{:S(2)}, u32[]{:S(2)}) collective-permute-start(bf16[512,1024]{1,0:T(8,128)(2,1)S(1)} %get-tuple-element.622.refs_6_), channel_id=1, source_target_pairs={{0,2},{1,3},{2,4},{3,5},{4,6},{5,7},{6,0},{7,1},{8,10},{9,11},{10,... | collective-permute-start | bytes 3145736 | tf_op jit(solution)/shard_map/ppermute | solution.py:620
  313.7 13.5 %collective-permute-start.23 = (bf16[128,6528]{1,0:T(8,128)(2,1)S(1)}, bf16[128,6528]{1,0:T(8,128)(2,1)S(1)}, u32[]{:S(2)}, u32[]{:S(2)}) collective-permute-start(bf16[128,6528]{1,0:T(8,128)(2,1)S(1)} %products.11.refs_0_), channel_id=1, source_target_pairs={{0,1},{1,0},{2,3},{3,2},{4,5},{5,4},{6,7},{7,6},{8,9},{9,8},{10,11... | collective-permute-start | bytes 5013512 | tf_op jit(solution)/shard_map/ppermute | solution.py:615
  320.3 27.9 %collective-permute-start.25 = (bf16[512,1024]{1,0:T(8,128)(2,1)S(1)}, bf16[512,1024]{1,0:T(8,128)(2,1)S(1)}, u32[]{:S(2)}, u32[]{:S(2)}) collective-permute-start(bf16[512,1024]{1,0:T(8,128)(2,1)S(1)} %products.12.refs_0_), channel_id=1, source_target_pairs={{0,2},{1,3},{2,4},{3,5},{4,6},{5,7},{6,0},{7,1},{8,10},{9,11},{10,... | collective-permute-start | bytes 3145736 | tf_op jit(solution)/shard_map/ppermute | solution.py:620
  327.2 33.8 %collective-permute-start.24 = (bf16[1024,1024]{1,0:T(8,128)(2,1)}, bf16[1024,1024]{1,0:T(8,128)(2,1)}, u32[]{:S(2)}, u32[]{:S(2)}) collective-permute-start(bf16[1024,1024]{1,0:T(8,128)(2,1)} %products.13.refs_0_), channel_id=1, source_target_pairs={{0,1},{1,0},{2,3},{3,2},{4,5},{5,4},{6,7},{7,6},{8,9},{9,8},{10,11... | collective-permute-start | bytes 6291464 | tf_op jit(solution)/shard_map/ppermute | solution.py:615
  335.0 47.7 %collective-permute-start.27 = (bf16[128,6528]{1,0:T(8,128)(2,1)}, bf16[128,6528]{1,0:T(8,128)(2,1)}, u32[]{:S(2)}, u32[]{:S(2)}) collective-permute-start(bf16[128,6528]{1,0:T(8,128)(2,1)} %products.14.refs_0_), channel_id=1, source_target_pairs={{0,2},{1,3},{2,4},{3,5},{4,6},{5,7},{6,0},{7,1},{8,10},{9,11},{10,... | collective-permute-start | bytes 5013512 | tf_op jit(solution)/shard_map/ppermute | solution.py:620
  360.9 8.7 %collective-permute-start.26 = (bf16[384,6528]{1,0:T(8,128)(2,1)}, bf16[384,6528]{1,0:T(8,128)(2,1)}, u32[]{:S(2)}, u32[]{:S(2)}) collective-permute-start(bf16[384,6528]{1,0:T(8,128)(2,1)} %products.16), channel_id=1, source_target_pairs={{0,1},{1,0},{2,3},{3,2},{4,5},{5,4},{6,7},{7,6},{8,9},{9,8},{10,11... | collective-permute-start | bytes 15040520 | tf_op jit(solution)/shard_map/ppermute | solution.py:615
  384.5 63.8 %copy-start.8 = (bf16[1024,1024]{1,0:T(8,128)(2,1)S(1)}, bf16[1024,1024]{1,0:T(8,128)(2,1)}, u32[]{:S(2)}) copy-start(bf16[1024,1024]{1,0:T(8,128)(2,1)} %copy-done.7) | copy-start | bytes 6291460
  384.5 41.3 %collective-permute-start.28 = (bf16[128,6528]{1,0:T(8,128)(2,1)S(1)}, bf16[128,6528]{1,0:T(8,128)(2,1)S(1)}, u32[]{:S(2)}, u32[]{:S(2)}) collective-permute-start(bf16[128,6528]{1,0:T(8,128)(2,1)S(1)} %add.160), channel_id=1, source_target_pairs={{0,2},{1,3},{2,4},{3,5},{4,6},{5,7},{6,0},{7,1},{8,10},{9,11},{10,... | collective-permute-start | bytes 5013512 | tf_op jit(solution)/shard_map/ppermute | solution.py:620
  384.6 63.7 %collective-permute-start.30 = (bf16[512,1024]{1,0:T(8,128)(2,1)S(1)}, bf16[512,1024]{1,0:T(8,128)(2,1)S(1)}, u32[]{:S(2)}, u32[]{:S(2)}) collective-permute-start(bf16[512,1024]{1,0:T(8,128)(2,1)S(1)} %add.159.refs_0_), channel_id=1, source_target_pairs={{0,2},{1,3},{2,4},{3,5},{4,6},{5,7},{6,0},{7,1},{8,10},{9,11},{10,... | collective-permute-start | bytes 3145736 | tf_op jit(solution)/shard_map/ppermute | solution.py:620
  426.2 56.5 %collective-permute-start.29 = (bf16[128,6528]{1,0:T(8,128)(2,1)S(1)}, bf16[128,6528]{1,0:T(8,128)(2,1)S(1)}, u32[]{:S(2)}, u32[]{:S(2)}) collective-permute-start(bf16[128,6528]{1,0:T(8,128)(2,1)S(1)} %add.161), channel_id=1, source_target_pairs={{0,2},{1,3},{2,4},{3,5},{4,6},{5,7},{6,0},{7,1},{8,10},{9,11},{10,... | collective-permute-start | bytes 5013512 | tf_op jit(solution)/shard_map/ppermute | solution.py:620
  (8 other events, 27.6 us)

commit v5 on v4

--- a/solution.py
+++ b/solution.py
@@ -16,7 +16,7 @@
 BWD_TILE = 2048
 SKEW = 2
 FWD_HEADS = 8
-BWD_HEADS = 2
+BWD_HEADS = 4
 NORM_BLOCK = 128
 NORM_UNROLL = 2
 SOFTMAX_BLOCK = 128
@@ -585,7 +585,7 @@
         ]
         + [pltpu.VMEM(shape, BF16) for shape in (weight_shapes(matrices) if last_call else ())]
         + [pltpu.SemaphoreType.DMA((8,))] * last_call,
-        compiler_params=pltpu.CompilerParams(vmem_limit_bytes=(42 if last_call else 20) * MIB),
+        compiler_params=pltpu.CompilerParams(vmem_limit_bytes=(46 if last_call else 24) * MIB),
         cost_estimate=pl.CostEstimate(
             flops=1024 if last_call else flops, bytes_accessed=1024 if last_call else 8 * MIB, transcendentals=0
         ),

time: 495 us -> 492 us (level)
  no operation moved by 1% of the time
where the time goes in v5:
time: 492 us; the launch traced here: 483 us
  Pallas kernels  266 us (54%)
  waiting for transfers between devices  187 us (38%)
  starting transfers between devices  22.5 us (5%)
    ppermute x6, waiting for transfers between devices, next_chip(): lax.ppermute(block, 'dp', [(i, (i + 2) % devices) for i in range(devices)])  112 us
    pallas_call x14, Pallas kernels, forward_chunk(): pl.pallas_call(functools.partial(forward_kernel, geometry, loading, place...  105 us
    pallas_call x10, Pallas kernels, backward_chunk(): pl.pallas_call(functools.partial(backward_kernel, geometry, last_call, le...  87.7 us
    ppermute x20, waiting for transfers between devices, hop(): return lax.ppermute(block, 'section', route) if route else None  70.5 us
    pallas_call x9, Pallas kernels, products(): pl.pallas_call(functools.partial(product_kernel, len(lefts), tuple((at fo...  65.8 us
    ppermute x20, starting transfers between devices, hop(): return lax.ppermute(block, 'section', route) if route else None  21.1 us
  transfers between devices with their start and end apart: 31, of which 10 were waited for; matrix products, arithmetic and copies ran while one was open for 0% of the time, Pallas kernels for 47%

profile of v5, /device:TPU:0, one launch (start us, length us, event | category | flops | bytes accessed | tf_op | source)
XLA Modules:
  0.0 483.5 jit_solution(15330623768132058655)
XLA Ops:
  4.8 14.8 %forward_chunk.14 = (bf16[128,1024]{1,0:T(8,128)(2,1)S(1)}, bf16[1024,1024]{1,0:T(8,128)(2,1)}, bf16[1024,1024]{1,0:T(8,128)(2,1)}, bf16[1024,1024]{1,0:T(8,128)...) custom-call(s32[112]{0:T(128)S(1)} %concatenate.3.meta, ...), custom_call_target="tpu_custom_call", output_to_operand_aliasing={{1}: (11, {}), {2}: (12, {}), {3}: (13, {}), {4}: (14, {}),... | custom-call | flops 2885681152 | bytes 8388608 | tf_op jit(solution)/shard_map/forward_chunk/pallas_call | solution.py:304
  20.9 8.1 %forward_chunk.15 = (bf16[128,1024]{1,0:T(8,128)(2,1)S(1)}, bf16[1024,1024]{1,0:T(8,128)(2,1)}, bf16[1024,1024]{1,0:T(8,128)(2,1)}, bf16[1024,1024]{1,0:T(8,128)...) custom-call(s32[112]{0:T(128)S(1)} %concatenate.3.meta, ...), custom_call_target="tpu_custom_call", output_to_operand_aliasing={{1}: (10, {}), {2}: (11, {}), {3}: (12, {}), {4}: (13, {}),... | custom-call | flops 2885681152 | bytes 8388608 | tf_op jit(solution)/shard_map/forward_chunk/pallas_call | solution.py:304
  30.3 8.9 %forward_chunk.16 = (bf16[128,1024]{1,0:T(8,128)(2,1)S(1)}, bf16[1024,1024]{1,0:T(8,128)(2,1)}, bf16[1024,1024]{1,0:T(8,128)(2,1)}, bf16[1024,1024]{1,0:T(8,128)...) custom-call(s32[112]{0:T(128)S(1)} %concatenate.3.meta, ...), custom_call_target="tpu_custom_call", output_to_operand_aliasing={{1}: (10, {}), {2}: (11, {}), {3}: (12, {}), {4}: (13, {}),... | custom-call | flops 2885681152 | bytes 8388608 | tf_op jit(solution)/shard_map/forward_chunk/pallas_call | solution.py:304
  40.6 8.7 %forward_chunk.17 = (bf16[128,1024]{1,0:T(8,128)(2,1)S(1)}, bf16[1024,1024]{1,0:T(8,128)(2,1)}, bf16[1024,1024]{1,0:T(8,128)(2,1)}, bf16[1024,1024]{1,0:T(8,128)...) custom-call(s32[112]{0:T(128)S(1)} %concatenate.3.meta, ...), custom_call_target="tpu_custom_call", output_to_operand_aliasing={{1}: (10, {}), {2}: (11, {}), {3}: (12, {}), {4}: (13, {}),... | custom-call | flops 2885681152 | bytes 8388608 | tf_op jit(solution)/shard_map/forward_chunk/pallas_call | solution.py:304
  50.6 9.8 %forward_chunk.18 = (bf16[128,1024]{1,0:T(8,128)(2,1)S(1)}, bf16[1024,1024]{1,0:T(8,128)(2,1)}, bf16[1024,1024]{1,0:T(8,128)(2,1)}, bf16[1024,1024]{1,0:T(8,128)...) custom-call(s32[112]{0:T(128)S(1)} %concatenate.3.meta, ...), custom_call_target="tpu_custom_call", output_to_operand_aliasing={{1}: (10, {}), {2}: (11, {}), {3}: (12, {}), {4}: (13, {}),... | custom-call | flops 2885681152 | bytes 8388608 | tf_op jit(solution)/shard_map/forward_chunk/pallas_call | solution.py:304
  61.7 8.2 %forward_chunk.19 = (bf16[128,1024]{1,0:T(8,128)(2,1)S(1)}, bf16[1024,1024]{1,0:T(8,128)(2,1)}, bf16[1024,1024]{1,0:T(8,128)(2,1)}, bf16[1024,1024]{1,0:T(8,128)...) custom-call(s32[112]{0:T(128)S(1)} %concatenate.3.meta, ...), custom_call_target="tpu_custom_call", output_to_operand_aliasing={{1}: (10, {}), {2}: (11, {}), {3}: (12, {}), {4}: (13, {}),... | custom-call | flops 2885681152 | bytes 8388608 | tf_op jit(solution)/shard_map/forward_chunk/pallas_call | solution.py:304
  71.3 9.9 %forward_chunk.20 = (bf16[128,1024]{1,0:T(8,128)(2,1)S(1)}, bf16[1024,1024]{1,0:T(8,128)(2,1)}, bf16[1024,1024]{1,0:T(8,128)(2,1)}, bf16[1024,1024]{1,0:T(8,128)...) custom-call(s32[112]{0:T(128)S(1)} %concatenate.3.meta, ...), custom_call_target="tpu_custom_call", output_to_operand_aliasing={{1}: (10, {}), {2}: (11, {}), {3}: (12, {}), {4}: (13, {}),... | custom-call | flops 2885681152 | bytes 8388608 | tf_op jit(solution)/shard_map/forward_chunk/pallas_call | solution.py:304
  82.6 8.7 %forward_chunk.21 = (bf16[128,1024]{1,0:T(8,128)(2,1)S(1)}, bf16[1024,1024]{1,0:T(8,128)(2,1)}, bf16[1024,1024]{1,0:T(8,128)(2,1)}, bf16[1024,1024]{1,0:T(8,128)...) custom-call(s32[112]{0:T(128)S(1)} %concatenate.3.meta, ...), custom_call_target="tpu_custom_call", output_to_operand_aliasing={{1}: (10, {}), {2}: (11, {}), {3}: (12, {}), {4}: (13, {}),... | custom-call | flops 2885681152 | bytes 8388608 | tf_op jit(solution)/shard_map/forward_chunk/pallas_call | solution.py:304
  92.6 7.5 %forward_chunk.22 = (bf16[128,1024]{1,0:T(8,128)(2,1)S(1)}, bf16[1024,1024]{1,0:T(8,128)(2,1)}, bf16[1024,1024]{1,0:T(8,128)(2,1)}, bf16[1024,1024]{1,0:T(8,128)...) custom-call(s32[112]{0:T(128)S(1)} %concatenate.3.meta, ...), custom_call_target="tpu_custom_call", output_to_operand_aliasing={{1}: (10, {}), {2}: (11, {}), {3}: (12, {}), {4}: (13, {}),... | custom-call | flops 2885681152 | bytes 8388608 | tf_op jit(solution)/shard_map/forward_chunk/pallas_call | solution.py:304
  102.2 9.7 %forward_chunk.24 = (bf16[128,1024]{1,0:T(8,128)(2,1)S(1)}, bf16[1024,1024]{1,0:T(8,128)(2,1)}, bf16[1024,1024]{1,0:T(8,128)(2,1)}, bf16[1024,1024]{1,0:T(8,128)...) custom-call(s32[112]{0:T(128)S(1)} %concatenate.3.meta, ...), custom_call_target="tpu_custom_call", output_to_operand_aliasing={{1}: (10, {}), {2}: (11, {}), {3}: (12, {}), {4}: (13, {}),... | custom-call | flops 2885681152 | bytes 8388608 | tf_op jit(solution)/shard_map/forward_chunk/pallas_call | solution.py:304
  115.5 8.0 %forward_chunk.27 = (bf16[128,1024]{1,0:T(8,128)(2,1)}, bf16[1024,1024]{1,0:T(8,128)(2,1)}, bf16[1024,1024]{1,0:T(8,128)(2,1)}, bf16[1024,1024]{1,0:T(8,128)(2,1...) custom-call(s32[112]{0:T(128)S(1)} %concatenate.3.meta, ...), custom_call_target="tpu_custom_call", output_to_operand_aliasing={{1}: (10, {}), {2}: (11, {}), {3}: (12, {}), {4}: (13, {}),... | custom-call | flops 2885681152 | bytes 8388608 | tf_op jit(solution)/shard_map/forward_chunk/pallas_call | solution.py:304
  125.0 9.2 %backward_chunk.11 = (bf16[256,1024]{1,0:T(8,128)(2,1)S(1)}, bf16[1024,1024]{1,0:T(8,128)(2,1)}, bf16[1024,4096]{1,0:T(8,128)(2,1)}, bf16[1024,1024]{1,0:T(8,128...) custom-call(s32[112]{0:T(128)S(1)} %concatenate.3.meta, ...), custom_call_target="tpu_custom_call", output_to_operand_aliasing={{1}: (18, {}), {2}: (19, {}), {3}: (20, {}), {4}: (21, {}),... | custom-call | flops 6308233216 | bytes 8388608 | tf_op jit(solution)/shard_map/backward_chunk/pallas_call | solution.py:552
  136.4 9.5 %backward_chunk.13 = (bf16[256,1024]{1,0:T(8,128)(2,1)S(1)}, bf16[1024,1024]{1,0:T(8,128)(2,1)}, bf16[1024,4096]{1,0:T(8,128)(2,1)}, bf16[1024,1024]{1,0:T(8,128...) custom-call(s32[112]{0:T(128)S(1)} %concatenate.3.meta, ...), custom_call_target="tpu_custom_call", output_to_operand_aliasing={{1}: (18, {}), {2}: (19, {}), {3}: (20, {}), {4}: (21, {}),... | custom-call | flops 6308233216 | bytes 8388608 | tf_op jit(solution)/shard_map/backward_chunk/pallas_call | solution.py:552
  148.7 8.6 %backward_chunk.15 = (bf16[256,1024]{1,0:T(8,128)(2,1)S(1)}, bf16[1024,1024]{1,0:T(8,128)(2,1)}, bf16[1024,4096]{1,0:T(8,128)(2,1)}, bf16[1024,1024]{1,0:T(8,128...) custom-call(s32[112]{0:T(128)S(1)} %concatenate.3.meta, ...), custom_call_target="tpu_custom_call", output_to_operand_aliasing={{1}: (18, {}), {2}: (19, {}), {3}: (20, {}), {4}: (21, {}),... | custom-call | flops 6308233216 | bytes 8388608 | tf_op jit(solution)/shard_map/backward_chunk/pallas_call | solution.py:552
  158.6 70.0 %collective-permute-done.17.incoming = bf16[256,1024]{1,0:T(8,128)(2,1)S(1)} collective-permute-done((bf16[256,1024]{1,0:T(8,128)(2,1)S(1)}, bf16[256,1024]{1,0:T(8,128)(2,1)S(1)}, u32[]{:S(2)}, u32[]{:S(2)}) %collective-permute-start.17) | collective-permute-done | bytes 524320 | tf_op jit(solution)/shard_map/ppermute | solution.py:821
  228.7 13.8 %backward_chunk.16 = (bf16[256,1024]{1,0:T(8,128)(2,1)S(1)}, bf16[1024,1024]{1,0:T(8,128)(2,1)}, bf16[1024,4096]{1,0:T(8,128)(2,1)}, bf16[1024,1024]{1,0:T(8,128...) custom-call(s32[112]{0:T(128)S(1)} %concatenate.3.meta, ...), custom_call_target="tpu_custom_call", output_to_operand_aliasing={{1}: (18, {}), {2}: (19, {}), {3}: (20, {}), {4}: (21, {}),... | custom-call | flops 6308233216 | bytes 8388608 | tf_op jit(solution)/shard_map/backward_chunk/pallas_call | solution.py:552
  243.8 13.1 %backward_chunk.17 = (bf16[256,1024]{1,0:T(8,128)(2,1)S(1)}, bf16[1024,1024]{1,0:T(8,128)(2,1)}, bf16[1024,4096]{1,0:T(8,128)(2,1)}, bf16[1024,1024]{1,0:T(8,128...) custom-call(s32[112]{0:T(128)S(1)} %concatenate.3.meta, ...), custom_call_target="tpu_custom_call", output_to_operand_aliasing={{1}: (18, {}), {2}: (19, {}), {3}: (20, {}), {4}: (21, {}),... | custom-call | flops 6308233216 | bytes 8388608 | tf_op jit(solution)/shard_map/backward_chunk/pallas_call | solution.py:552
  258.6 14.6 %backward_chunk.18 = (bf16[256,1024]{1,0:T(8,128)(2,1)}, bf16[1024,1024]{1,0:T(8,128)(2,1)}, bf16[1024,4096]{1,0:T(8,128)(2,1)}, bf16[1024,1024]{1,0:T(8,128)(2,...) custom-call(s32[112]{0:T(128)S(1)} %concatenate.3.meta, ...), custom_call_target="tpu_custom_call", output_to_operand_aliasing={{1}: (18, {}), {2}: (19, {}), {3}: (20, {}), {4}: (21, {}),... | custom-call | flops 6308233216 | bytes 8388608 | tf_op jit(solution)/shard_map/backward_chunk/pallas_call | solution.py:552
  274.7 3.8 products.9
  281.2 5.5 %products.10 = (bf16[512,1024]{1,0:T(8,128)(2,1)S(1)}, bf16[512,1024]{1,0:T(8,128)(2,1)S(1)}) custom-call(s32[112]{0:T(128)S(1)} %concatenate.3.meta, bf16[1024,4096]{1,0:T(8,128)(2,1)} %get-tuple-element.612.refs_0_.refs_1_, bf16[1024,1024]{1,0:T(8,128)(2,1)} %keep_last.1.refs_1_.refs_2_, bf16[512,1024]{1,0:T(8,128)(2,1)S(1)} %collective-permute-done.20.refs_2_), custom_call_target="tpu_custom_call" | custom-call | flops 5000000000 | bytes 1024 | tf_op jit(solution)/shard_map/products/pallas_call | solution.py:706
  286.9 16.6 %backward_chunk.19 = (bf16[256,1024]{1,0:T(8,128)(2,1)}, bf16[1024,4096]{1,0:T(8,128)(2,1)}, bf16[1024,1024]{1,0:T(8,128)(2,1)}, bf16[1024,1280]{1,0:T(8,128)(2,...) custom-call(s32[112]{0:T(128)S(1)} %concatenate.3.meta, ...), custom_call_target="tpu_custom_call", output_to_operand_aliasing={{1}: (21, {}), {2}: (22, {}), {3}: (23, {}), {4}: (24, {}),... | custom-call | flops 1024 | bytes 1024 | tf_op jit(solution)/shard_map/backward_chunk/pallas_call | solution.py:552
  304.4 6.5 %products.11.refs_0_ = bf16[128,6528]{1,0:T(8,128)(2,1)S(1)} custom-call(s32[112]{0:T(128)S(1)} %concatenate.3.meta, bf16[1024,1024]{1,0:T(8,128)(2,1)} %get-tuple-element.631.refs_0_.refs_1_.refs_2_, bf16[1024,1024]{1,0:T(8,128)(2,1)} %get-tuple-element.632.refs_1_.refs_2_.refs_3_, bf16[1024,1024]{1,0:T(8,128)(2,1)} %get-tuple-element.633.refs_2_.refs_3_.refs_4_, ...), custom_call_target="tpu_custom_call" | custom-call | flops 5000000000 | bytes 1024 | tf_op jit(solution)/shard_map/products/pallas_call | solution.py:706
  314.1 3.9 products.12.refs_0_
  318.0 6.8 %products.13.refs_0_ = bf16[1024,1024]{1,0:T(8,128)(2,1)} custom-call(s32[112]{0:T(128)S(1)} %concatenate.3.meta, bf16[512,1024]{1,0:T(8,128)(2,1)S(1)} %products.12.refs_0_, bf16[1024,4096]{1,0:T(8,128)(2,1)} %get-tuple-element.612.refs_0_.refs_1_, bf16[1024,1024]{1,0:T(8,128)(2,1)} %keep_last.1.refs_1_.refs_2_), custom_call_target="tpu_custom_call" | custom-call | flops 5000000000 | bytes 1024 | tf_op jit(solution)/shard_map/products/pallas_call | solution.py:706
  324.9 7.7 %products.14.refs_0_ = bf16[128,6528]{1,0:T(8,128)(2,1)} custom-call(s32[112]{0:T(128)S(1)} %concatenate.3.meta, bf16[1024,1024]{1,0:T(8,128)(2,1)} %products.13.refs_0_, bf16[1024,1024]{1,0:T(8,128)(2,1)} %get-tuple-element.631.refs_0_.refs_1_.refs_2_, bf16[1024,1024]{1,0:T(8,128)(2,1)} %get-tuple-element.632.refs_1_.refs_2_.refs_3_, ...), custom_call_target="tpu_custom_call" | custom-call | flops 99999997952 | bytes 1024 | tf_op jit(solution)/shard_map/products/pallas_call | solution.py:706
  333.0 12.9 %collective-permute-done.25.come.refs_1_ = bf16[512,1024]{1,0:T(8,128)(2,1)S(1)} collective-permute-done((bf16[512,1024]{1,0:T(8,128)(2,1)S(1)}, bf16[512,1024]{1,0:T(8,128)(2,1)S(1)}, u32[]{:S(2)}, u32[]{:S(2)}) %collective-permute-start.25) | collective-permute-done | bytes 1048608 | tf_op jit(solution)/shard_map/ppermute | solution.py:620
  345.9 12.6 %products.16 = bf16[384,6528]{1,0:T(8,128)(2,1)} custom-call(s32[112]{0:T(128)S(1)} %concatenate.3.meta, bf16[128,6528]{1,0:T(8,128)(2,1)} %products.14.refs_0_, bf16[512,1024]{1,0:T(8,128)(2,1)S(1)} %collective-permute-done.25.come.refs_1_, bf16[1024,1024]{1,0:T(8,128)(2,1)} %get-tuple-element.631.refs_0_.refs_1_.refs_2_, ...), custom_call_target="tpu_custom_call" | custom-call | flops 99999997952 | bytes 1024 | tf_op jit(solution)/shard_map/products/pallas_call | solution.py:706
  358.6 6.5 %products.15.kept = bf16[1024,1024]{1,0:T(8,128)(2,1)S(1)} custom-call(s32[112]{0:T(128)S(1)} %concatenate.3.meta, bf16[128,6528]{1,0:T(8,128)(2,1)} %products.14.refs_0_, bf16[1024,4096]{1,0:T(8,128)(2,1)} %get-tuple-element.612.refs_0_.refs_1_, bf16[1024,1024]{1,0:T(8,128)(2,1)} %keep_last.1.refs_1_.refs_2_, bf16[1024,1024]{1,0:T(8,128)(2,1)} %collective-permute-done.24.refs_3_), custom_call_target="tpu_custom_call" | custom-call | flops 99999997952 | bytes 1024 | tf_op jit(solution)/shard_map/products/pallas_call | solution.py:706
  367.3 12.6 %products.17.kept = bf16[384,6528]{1,0:T(8,128)(2,1)S(1)} custom-call(s32[112]{0:T(128)S(1)} %concatenate.3.meta, bf16[512,1024]{1,0:T(8,128)(2,1)S(1)} %add.159.refs_0_, bf16[1024,1024]{1,0:T(8,128)(2,1)} %get-tuple-element.631.refs_0_.refs_1_.refs_2_, bf16[1024,1024]{1,0:T(8,128)(2,1)} %get-tuple-element.632.refs_1_.refs_2_.refs_3_, ...), custom_call_target="tpu_custom_call" | custom-call | flops 99999997952 | bytes 1024 | tf_op jit(solution)/shard_map/products/pallas_call | solution.py:706
  382.3 41.1 %collective-permute-done.28.come = bf16[128,6528]{1,0:T(8,128)(2,1)S(1)} collective-permute-done((bf16[128,6528]{1,0:T(8,128)(2,1)S(1)}, bf16[128,6528]{1,0:T(8,128)(2,1)S(1)}, u32[]{:S(2)}, u32[]{:S(2)}) %collective-permute-start.28) | collective-permute-done | bytes 1671200 | tf_op jit(solution)/shard_map/ppermute | solution.py:620
  423.9 22.0 %collective-permute-done.30.come = bf16[512,1024]{1,0:T(8,128)(2,1)S(1)} collective-permute-done((bf16[512,1024]{1,0:T(8,128)(2,1)S(1)}, bf16[512,1024]{1,0:T(8,128)(2,1)S(1)}, u32[]{:S(2)}, u32[]{:S(2)}) %collective-permute-start.30) | collective-permute-done | bytes 1048608 | tf_op jit(solution)/shard_map/ppermute | solution.py:620
  447.5 32.9 %collective-permute-done.29.come = bf16[128,6528]{1,0:T(8,128)(2,1)S(1)} collective-permute-done((bf16[128,6528]{1,0:T(8,128)(2,1)S(1)}, bf16[128,6528]{1,0:T(8,128)(2,1)S(1)}, u32[]{:S(2)}, u32[]{:S(2)}) %collective-permute-start.29) | collective-permute-done | bytes 1671200 | tf_op jit(solution)/shard_map/ppermute | solution.py:620
  (92 shorter events, 48.5 us)
Async XLA Ops:
  19.6 10.7 %collective-permute-start.1 = (bf16[128,1024]{1,0:T(8,128)(2,1)S(1)}, bf16[128,1024]{1,0:T(8,128)(2,1)S(1)}, u32[]{:S(2)}, u32[]{:S(2)}) collective-permute-start(bf16[128,1024]{1,0:T(8,128)(2,1)S(1)} %get-tuple-element.361), channel_id=1, source_target_pairs={{0,8},{1,9},{2,10},{3,11},{4,12},{5,13},{6,14},{7,15}} | collective-permute-start | bytes 786440 | tf_op jit(solution)/shard_map/ppermute | solution.py:821
  29.0 11.6 %collective-permute-start = (bf16[128,1024]{1,0:T(8,128)(2,1)S(1)}, bf16[128,1024]{1,0:T(8,128)(2,1)S(1)}, u32[]{:S(2)}, u32[]{:S(2)}) collective-permute-start(bf16[128,1024]{1,0:T(8,128)(2,1)S(1)} %get-tuple-element.360), channel_id=1, source_target_pairs={{0,8},{1,9},{2,10},{3,11},{4,12},{5,13},{6,14},{7,15}} | collective-permute-start | bytes 786440 | tf_op jit(solution)/shard_map/ppermute | solution.py:821
  39.3 11.3 %collective-permute-start.3 = (bf16[128,1024]{1,0:T(8,128)(2,1)S(1)}, bf16[128,1024]{1,0:T(8,128)(2,1)S(1)}, u32[]{:S(2)}, u32[]{:S(2)}) collective-permute-start(bf16[128,1024]{1,0:T(8,128)(2,1)S(1)} %get-tuple-element.391), channel_id=1, source_target_pairs={{0,8},{8,16},{1,9},{9,17},{2,10},{10,18},{3,11},{11,19},{4,12},{12... | collective-permute-start | bytes 786440 | tf_op jit(solution)/shard_map/ppermute | solution.py:821
  49.3 12.4 %collective-permute-start.2 = (bf16[128,1024]{1,0:T(8,128)(2,1)S(1)}, bf16[128,1024]{1,0:T(8,128)(2,1)S(1)}, u32[]{:S(2)}, u32[]{:S(2)}) collective-permute-start(bf16[128,1024]{1,0:T(8,128)(2,1)S(1)} %get-tuple-element.390), channel_id=1, source_target_pairs={{0,8},{8,16},{1,9},{9,17},{2,10},{10,18},{3,11},{11,19},{4,12},{12... | collective-permute-start | bytes 786440 | tf_op jit(solution)/shard_map/ppermute | solution.py:821
  60.4 10.9 %collective-permute-start.5 = (bf16[128,1024]{1,0:T(8,128)(2,1)S(1)}, bf16[128,1024]{1,0:T(8,128)(2,1)S(1)}, u32[]{:S(2)}, u32[]{:S(2)}) collective-permute-start(bf16[128,1024]{1,0:T(8,128)(2,1)S(1)} %get-tuple-element.421), channel_id=1, source_target_pairs={{0,8},{8,16},{16,24},{1,9},{9,17},{17,25},{2,10},{10,18},{18,26},{... | collective-permute-start | bytes 786440 | tf_op jit(solution)/shard_map/ppermute | solution.py:821
  70.0 12.6 %collective-permute-start.4 = (bf16[128,1024]{1,0:T(8,128)(2,1)S(1)}, bf16[128,1024]{1,0:T(8,128)(2,1)S(1)}, u32[]{:S(2)}, u32[]{:S(2)}) collective-permute-start(bf16[128,1024]{1,0:T(8,128)(2,1)S(1)} %get-tuple-element.420), channel_id=1, source_target_pairs={{0,8},{8,16},{16,24},{1,9},{9,17},{17,25},{2,10},{10,18},{18,26},{... | collective-permute-start | bytes 786440 | tf_op jit(solution)/shard_map/ppermute | solution.py:821
  81.2 11.3 %collective-permute-start.7 = (bf16[128,1024]{1,0:T(8,128)(2,1)S(1)}, bf16[128,1024]{1,0:T(8,128)(2,1)S(1)}, u32[]{:S(2)}, u32[]{:S(2)}) collective-permute-start(bf16[128,1024]{1,0:T(8,128)(2,1)S(1)} %get-tuple-element.451), channel_id=1, source_target_pairs={{0,8},{8,16},{16,24},{1,9},{9,17},{17,25},{2,10},{10,18},{18,26},{... | collective-permute-start | bytes 786440 | tf_op jit(solution)/shard_map/ppermute | solution.py:821
  91.2 9.5 %collective-permute-start.6 = (bf16[128,1024]{1,0:T(8,128)(2,1)S(1)}, bf16[128,1024]{1,0:T(8,128)(2,1)S(1)}, u32[]{:S(2)}, u32[]{:S(2)}) collective-permute-start(bf16[128,1024]{1,0:T(8,128)(2,1)S(1)} %get-tuple-element.450), channel_id=1, source_target_pairs={{0,8},{8,16},{16,24},{1,9},{9,17},{17,25},{2,10},{10,18},{18,26},{... | collective-permute-start | bytes 786440 | tf_op jit(solution)/shard_map/ppermute | solution.py:821
  100.0 2.1 collective-permute-start.9
  101.5 11.1 %collective-permute-start.8 = (bf16[128,1024]{1,0:T(8,128)(2,1)S(1)}, bf16[128,1024]{1,0:T(8,128)(2,1)S(1)}, u32[]{:S(2)}, u32[]{:S(2)}) collective-permute-start(bf16[128,1024]{1,0:T(8,128)(2,1)S(1)} %get-tuple-element.480), channel_id=1, source_target_pairs={{8,16},{16,24},{9,17},{17,25},{10,18},{18,26},{11,19},{19,27},{12,... | collective-permute-start | bytes 786440 | tf_op jit(solution)/shard_map/ppermute | solution.py:821
  111.8 2.1 collective-permute-start.11
  113.3 2.2 collective-permute-start.10
  115.5 8.1 %copy-start.4 = (bf16[1,1024]{1,0:T(2,128)(2,1)S(1)}, bf16[1,1024]{1,0:T(2,128)(2,1)}, u32[]{:S(2)}) copy-start(bf16[1,1024]{1,0:T(2,128)(2,1)} %gain_attn.47) | copy-start | bytes 6148
  124.3 10.6 %collective-permute-start.13 = (bf16[256,1024]{1,0:T(8,128)(2,1)S(1)}, bf16[256,1024]{1,0:T(8,128)(2,1)S(1)}, u32[]{:S(2)}, u32[]{:S(2)}) collective-permute-start(bf16[256,1024]{1,0:T(8,128)(2,1)S(1)} %get-tuple-element.564), channel_id=1, source_target_pairs={{24,16},{25,17},{26,18},{27,19},{28,20},{29,21},{30,22},{31,23}} | collective-permute-start | bytes 1572872 | tf_op jit(solution)/shard_map/ppermute | solution.py:821
  134.2 2.2 collective-permute-start.12
  135.7 10.9 %collective-permute-start.15 = (bf16[256,1024]{1,0:T(8,128)(2,1)S(1)}, bf16[256,1024]{1,0:T(8,128)(2,1)S(1)}, u32[]{:S(2)}, u32[]{:S(2)}) collective-permute-start(bf16[256,1024]{1,0:T(8,128)(2,1)S(1)} %get-tuple-element.580), channel_id=1, source_target_pairs={{16,8},{24,16},{17,9},{25,17},{18,10},{26,18},{19,11},{27,19},{20,... | collective-permute-start | bytes 1572872 | tf_op jit(solution)/shard_map/ppermute | solution.py:821
  145.9 2.8 collective-permute-start.14
  147.4 81.3 %collective-permute-start.17 = (bf16[256,1024]{1,0:T(8,128)(2,1)S(1)}, bf16[256,1024]{1,0:T(8,128)(2,1)S(1)}, u32[]{:S(2)}, u32[]{:S(2)}) collective-permute-start(bf16[256,1024]{1,0:T(8,128)(2,1)S(1)} %get-tuple-element.596), channel_id=1, source_target_pairs={{8,0},{16,8},{9,1},{17,9},{10,2},{18,10},{11,3},{19,11},{12,4},{20... | collective-permute-start | bytes 1572872 | tf_op jit(solution)/shard_map/ppermute | solution.py:821
  157.3 86.5 %collective-permute-start.16 = (bf16[256,1024]{1,0:T(8,128)(2,1)S(1)}, bf16[256,1024]{1,0:T(8,128)(2,1)S(1)}, u32[]{:S(2)}, u32[]{:S(2)}) collective-permute-start(bf16[256,1024]{1,0:T(8,128)(2,1)S(1)} %get-tuple-element.595), channel_id=1, source_target_pairs={{8,0},{16,8},{9,1},{17,9},{10,2},{18,10},{11,3},{19,11},{12,4},{20... | collective-permute-start | bytes 1572872 | tf_op jit(solution)/shard_map/ppermute | solution.py:821
  242.5 16.1 %collective-permute-start.19 = (bf16[256,1024]{1,0:T(8,128)(2,1)S(1)}, bf16[256,1024]{1,0:T(8,128)(2,1)S(1)}, u32[]{:S(2)}, u32[]{:S(2)}) collective-permute-start(bf16[256,1024]{1,0:T(8,128)(2,1)S(1)} %get-tuple-element.613), channel_id=1, source_target_pairs={{8,0},{9,1},{10,2},{11,3},{12,4},{13,5},{14,6},{15,7}} | collective-permute-start | bytes 1572872 | tf_op jit(solution)/shard_map/ppermute | solution.py:821
  256.9 16.4 %collective-permute-start.18 = (bf16[256,1024]{1,0:T(8,128)(2,1)S(1)}, bf16[256,1024]{1,0:T(8,128)(2,1)S(1)}, u32[]{:S(2)}, u32[]{:S(2)}) collective-permute-start(bf16[256,1024]{1,0:T(8,128)(2,1)S(1)} %get-tuple-element.611), channel_id=1, source_target_pairs={{8,0},{9,1},{10,2},{11,3},{12,4},{13,5},{14,6},{15,7}} | collective-permute-start | bytes 1572872 | tf_op jit(solution)/shard_map/ppermute | solution.py:821
  278.4 2.7 collective-permute-start.20
  286.6 24.7 %collective-permute-start.21 = (bf16[512,1024]{1,0:T(8,128)(2,1)S(1)}, bf16[512,1024]{1,0:T(8,128)(2,1)S(1)}, u32[]{:S(2)}, u32[]{:S(2)}) collective-permute-start(bf16[512,1024]{1,0:T(8,128)(2,1)S(1)} %get-tuple-element.623.refs_7_), channel_id=1, source_target_pairs={{0,1},{1,0},{2,3},{3,2},{4,5},{5,4},{6,7},{7,6},{8,9},{9,8},{10,11... | collective-permute-start | bytes 3145736 | tf_op jit(solution)/shard_map/ppermute | solution.py:615
  286.9 27.2 %collective-permute-start.22 = (bf16[512,1024]{1,0:T(8,128)(2,1)S(1)}, bf16[512,1024]{1,0:T(8,128)(2,1)S(1)}, u32[]{:S(2)}, u32[]{:S(2)}) collective-permute-start(bf16[512,1024]{1,0:T(8,128)(2,1)S(1)} %get-tuple-element.622.refs_6_), channel_id=1, source_target_pairs={{0,2},{1,3},{2,4},{3,5},{4,6},{5,7},{6,0},{7,1},{8,10},{9,11},{10,... | collective-permute-start | bytes 3145736 | tf_op jit(solution)/shard_map/ppermute | solution.py:620
  311.0 14.0 %collective-permute-start.23 = (bf16[128,6528]{1,0:T(8,128)(2,1)S(1)}, bf16[128,6528]{1,0:T(8,128)(2,1)S(1)}, u32[]{:S(2)}, u32[]{:S(2)}) collective-permute-start(bf16[128,6528]{1,0:T(8,128)(2,1)S(1)} %products.11.refs_0_), channel_id=1, source_target_pairs={{0,1},{1,0},{2,3},{3,2},{4,5},{5,4},{6,7},{7,6},{8,9},{9,8},{10,11... | collective-permute-start | bytes 5013512 | tf_op jit(solution)/shard_map/ppermute | solution.py:615
  318.0 27.9 %collective-permute-start.25 = (bf16[512,1024]{1,0:T(8,128)(2,1)S(1)}, bf16[512,1024]{1,0:T(8,128)(2,1)S(1)}, u32[]{:S(2)}, u32[]{:S(2)}) collective-permute-start(bf16[512,1024]{1,0:T(8,128)(2,1)S(1)} %products.12.refs_0_), channel_id=1, source_target_pairs={{0,2},{1,3},{2,4},{3,5},{4,6},{5,7},{6,0},{7,1},{8,10},{9,11},{10,... | collective-permute-start | bytes 3145736 | tf_op jit(solution)/shard_map/ppermute | solution.py:620
  324.8 33.8 %collective-permute-start.24 = (bf16[1024,1024]{1,0:T(8,128)(2,1)}, bf16[1024,1024]{1,0:T(8,128)(2,1)}, u32[]{:S(2)}, u32[]{:S(2)}) collective-permute-start(bf16[1024,1024]{1,0:T(8,128)(2,1)} %products.13.refs_0_), channel_id=1, source_target_pairs={{0,1},{1,0},{2,3},{3,2},{4,5},{5,4},{6,7},{7,6},{8,9},{9,8},{10,11... | collective-permute-start | bytes 6291464 | tf_op jit(solution)/shard_map/ppermute | solution.py:615
  332.7 47.7 %collective-permute-start.27 = (bf16[128,6528]{1,0:T(8,128)(2,1)}, bf16[128,6528]{1,0:T(8,128)(2,1)}, u32[]{:S(2)}, u32[]{:S(2)}) collective-permute-start(bf16[128,6528]{1,0:T(8,128)(2,1)} %products.14.refs_0_), channel_id=1, source_target_pairs={{0,2},{1,3},{2,4},{3,5},{4,6},{5,7},{6,0},{7,1},{8,10},{9,11},{10,... | collective-permute-start | bytes 5013512 | tf_op jit(solution)/shard_map/ppermute | solution.py:620
  358.5 8.7 %collective-permute-start.26 = (bf16[384,6528]{1,0:T(8,128)(2,1)}, bf16[384,6528]{1,0:T(8,128)(2,1)}, u32[]{:S(2)}, u32[]{:S(2)}) collective-permute-start(bf16[384,6528]{1,0:T(8,128)(2,1)} %products.16), channel_id=1, source_target_pairs={{0,1},{1,0},{2,3},{3,2},{4,5},{5,4},{6,7},{7,6},{8,9},{9,8},{10,11... | collective-permute-start | bytes 15040520 | tf_op jit(solution)/shard_map/ppermute | solution.py:615
  382.2 41.3 %collective-permute-start.28 = (bf16[128,6528]{1,0:T(8,128)(2,1)S(1)}, bf16[128,6528]{1,0:T(8,128)(2,1)S(1)}, u32[]{:S(2)}, u32[]{:S(2)}) collective-permute-start(bf16[128,6528]{1,0:T(8,128)(2,1)S(1)} %add.160), channel_id=1, source_target_pairs={{0,2},{1,3},{2,4},{3,5},{4,6},{5,7},{6,0},{7,1},{8,10},{9,11},{10,... | collective-permute-start | bytes 5013512 | tf_op jit(solution)/shard_map/ppermute | solution.py:620
  382.3 63.7 %collective-permute-start.30 = (bf16[512,1024]{1,0:T(8,128)(2,1)S(1)}, bf16[512,1024]{1,0:T(8,128)(2,1)S(1)}, u32[]{:S(2)}, u32[]{:S(2)}) collective-permute-start(bf16[512,1024]{1,0:T(8,128)(2,1)S(1)} %add.159.refs_0_), channel_id=1, source_target_pairs={{0,2},{1,3},{2,4},{3,5},{4,6},{5,7},{6,0},{7,1},{8,10},{9,11},{10,... | collective-permute-start | bytes 3145736 | tf_op jit(solution)/shard_map/ppermute | solution.py:620
  423.8 56.5 %collective-permute-start.29 = (bf16[128,6528]{1,0:T(8,128)(2,1)S(1)}, bf16[128,6528]{1,0:T(8,128)(2,1)S(1)}, u32[]{:S(2)}, u32[]{:S(2)}) collective-permute-start(bf16[128,6528]{1,0:T(8,128)(2,1)S(1)} %add.161), channel_id=1, source_target_pairs={{0,2},{1,3},{2,4},{3,5},{4,6},{5,7},{6,0},{7,1},{8,10},{9,11},{10,... | collective-permute-start | bytes 5013512 | tf_op jit(solution)/shard_map/ppermute | solution.py:620
  (6 other events, 19.5 us)
